TPU v7x, 128 devices: a whole 4x4x4 slice. The times are simulated.
128 devices in a mesh: section: 8 (over y, core), perim: 16 (over z, x).
Axes of the slice: x: 4, y: 4, z: 4, core: 2. Of those that a mesh axis runs over, the one named last changes fastest.
Arguments:
- radiosity: float32 [8, 16, 128, 256], P(None, 'section', 'perim'), may hold values from -6 to 6
- emission: float32 [8, 16, 128, 256], P(None, 'section', 'perim'), may hold values from -6 to 6
- reflect: float32 [8, 16, 128, 256], P(None, 'section', 'perim'), may hold values from 0.3 to 0.9
- basis: bfloat16 [16, 128, 64, 256], P('section', 'perim'), may hold values from -0.375 to 0.375
- up_leaf: bfloat16 [16, 128, 64, 64], P('section', 'perim'), may hold values from -0.5 to 0.5
- upward_pair_transfer: bfloat16 [8, 128, 64, 64], P('section', 'perim'), may hold values from -0.25 to 0.25
- near_block: bfloat16 [16, 128, 6, 256, 256], P('section', 'perim'), may hold values from -0.15625 to 0.15625
- couple_leaf: bfloat16 [16, 128, 64, 1024], P('section', 'perim'), may hold values from -0.1875 to 0.1875
- couple_pair: bfloat16 [8, 128, 64, 1024], P('section', 'perim'), may hold values from -0.1875 to 0.1875
- couple_top: bfloat16 [8, 16, 64, 512], P('section', 'perim'), may hold values from -0.25 to 0.25
- near_list: int32 [16, 128, 6], P('section', 'perim'), may hold values from 0 to 2047, as said below
- far_leaf: int32 [16, 128, 16], P('section', 'perim'), may hold values from 0 to 2047, as said below
- far_pair: int32 [8, 128, 16], P('section', 'perim'), may hold values from 0 to 1023, as said below
- far_top: int32 [8, 16, 8], P('section', 'perim'), may hold values from 0 to 127, as said below
Outputs:
- radiosity_next: float32 [8, 16, 128, 256], P(None, 'section', 'perim')
Inputs may be any that keep to these rules, and one draw needn't show every extreme that they name: `near_list`: entry n > 0 names a leaf whose row differs by at most one (clipped to the tower) and whose column differs by at most one around the perimeter, which closes; entry 0 is the leaf itself. `far_leaf`: A partner leaf lies in a leaf row of the same device row (row // 2) as the leaf or of the one above or below, and two or more columns away around the perimeter. `far_pair`: A partner pair cluster lies in the same pair row or the one above or below, two or more columns away around the perimeter. `far_top`: A partner top cluster lies two or more pair rows away in height.
All inputs are finite; a program needn't handle non-finite values.
Results may differ from a plain program's by a relative error of at most 0.0023.
Values may be sent and summed in bfloat16 or wider, within the bound.
No kernel may reach another device: no remote copies, remote signals or barrier semaphores. Data moves between devices by JAX's collectives and lax.ppermute only.
A program may use at most 64 MiB of HBM per device.

v0:
```python
import jax
import jax.numpy as jnp
from jax import lax
from jax.sharding import PartitionSpec as P


def padded(cells, sides, width, closed):
    for axis, dim in sides:
        count = lax.axis_size(axis)
        ends = count if closed else count - 1
        head = lax.slice_in_dim(cells, 0, width, axis=dim)
        tail = lax.slice_in_dim(cells, cells.shape[dim] - width, cells.shape[dim], axis=dim)
        cells = jnp.concatenate(
            [
                lax.ppermute(tail, axis, [(i, (i + 1) % count) for i in range(ends)]),
                cells,
                lax.ppermute(head, axis, [((i + 1) % count, i) for i in range(ends)]),
            ],
            axis=dim,
        )
    return cells


def body(
    radiosity,
    emission,
    reflect,
    basis,
    up_leaf,
    upward_pair_transfer,
    near_block,
    couple_leaf,
    couple_pair,
    couple_top,
    near_list,
    far_leaf,
    far_pair,
    far_top,
):
    per_count = lax.axis_size("perim")
    band_size = radiosity.shape[0]
    row_count = radiosity.shape[1]
    column_count = radiosity.shape[2]
    rank_size = basis.shape[2]
    width_all = column_count * per_count
    coeff_rows = row_count * column_count + column_count
    shaded = radiosity.astype(jnp.bfloat16)
    broadened_result = padded(shaded, (("perim", 2),), 1, True)
    broadened_result = padded(broadened_result, (("section", 1),), 1, False)
    own_rows = (
        lax.axis_index("section") * row_count
        + jnp.arange(row_count, dtype=jnp.int32)[:, None, None]
    )
    own_cols = (
        lax.axis_index("perim") * column_count
        + jnp.arange(column_count, dtype=jnp.int32)[None, :, None]
    )
    rise = near_list // width_all - own_rows
    turn = (near_list % width_all - own_cols + 1) % width_all - 1
    offset_code = (rise + 1) * 3 + turn + 1
    picker = (offset_code[..., None] == jnp.arange(9, dtype=jnp.int32)).astype(jnp.bfloat16)
    windows = jnp.stack(
        [
            broadened_result[
                :,
                1 + height_step : 1 + height_step + row_count,
                1 + around_step : 1 + around_step + column_count,
                :,
            ]
            for height_step in (-1, 0, 1)
            for around_step in (-1, 0, 1)
        ]
    )
    collected_near_rows = jnp.einsum(
        "xlno,obxlj->xlnbj", picker, windows, preferred_element_type=jnp.float32
    ).astype(jnp.bfloat16)
    nearby_portion = jnp.einsum(
        "xlnij,xlnbj->bxli", near_block, collected_near_rows, preferred_element_type=jnp.float32
    )
    leaf_coef = jnp.einsum(
        "xlrj,bxlj->xlrb", basis, shaded, preferred_element_type=jnp.float32
    ).astype(jnp.bfloat16)
    pair_coefficient = jnp.einsum(
        "xlsr,xlsb->lrb", up_leaf, leaf_coef, preferred_element_type=jnp.float32
    ).astype(jnp.bfloat16)
    top_coef = jnp.einsum(
        "hzy,hzx->yx", upward_pair_transfer[0], pair_coefficient, preferred_element_type=jnp.float32
    ).astype(jnp.bfloat16)
    coeffs = jnp.concatenate(
        [
            leaf_coef.reshape(row_count * column_count, rank_size * band_size),
            pair_coefficient.reshape(column_count, rank_size * band_size),
        ],
        axis=0,
    )
    leaf_rows = far_leaf // width_all
    leaf_cols = far_leaf % width_all
    pair_cols = far_pair % width_all
    source_sec = jnp.concatenate(
        [(leaf_rows // row_count).reshape(-1), (far_pair // width_all).reshape(-1)]
    )
    source_col = jnp.concatenate(
        [(leaf_cols // column_count).reshape(-1), (pair_cols // column_count).reshape(-1)]
    )
    source_local = jnp.concatenate(
        [
            (leaf_rows % row_count * column_count + leaf_cols % column_count).reshape(-1),
            (row_count * column_count + pair_cols % column_count).reshape(-1),
        ]
    )
    rise_sec = source_sec - lax.axis_index("section") + 1
    beside_all = lax.all_gather(coeffs, "perim", axis=0, tiled=True)
    tiers = padded(beside_all[None], (("section", 0),), 1, False)
    tier_rows = beside_all.shape[0]
    slots = rise_sec * tier_rows + source_col * coeff_rows + source_local
    chooser = (slots[:, None] == jnp.arange(3 * tier_rows, dtype=jnp.int32)[None, :]).astype(
        jnp.bfloat16
    )
    picked = jnp.dot(
        chooser, tiers.reshape(3 * tier_rows, tiers.shape[2]), preferred_element_type=jnp.float32
    )
    picked = picked.astype(jnp.bfloat16)
    split_at = row_count * column_count * far_leaf.shape[2]
    leaf_pick = picked[:split_at].reshape(row_count, column_count, -1, band_size)
    pair_pick = picked[split_at:].reshape(column_count, -1, band_size)
    leaf_radiosity_field = jnp.einsum(
        "xlrc,xlcb->xlrb", couple_leaf, leaf_pick, preferred_element_type=jnp.float32
    )
    pair_radiosity_field = jnp.einsum(
        "lrc,lcb->lrb", couple_pair[0], pair_pick, preferred_element_type=jnp.float32
    )
    everyone = lax.all_gather(
        top_coef.reshape(1, rank_size * band_size), ("section", "perim"), axis=0, tiled=True
    )
    top_chooser = (
        far_top[0, 0][:, None] == jnp.arange(everyone.shape[0], dtype=jnp.int32)[None, :]
    ).astype(jnp.bfloat16)
    top_pick = (
        jnp.dot(top_chooser, everyone, preferred_element_type=jnp.float32)
        .astype(jnp.bfloat16)
        .reshape(-1, band_size)
    )
    top_field = jnp.dot(couple_top[0, 0], top_pick, preferred_element_type=jnp.float32)
    pair_total = pair_radiosity_field + jnp.einsum(
        "hic,co->hio",
        upward_pair_transfer[0],
        top_field.astype(jnp.bfloat16),
        preferred_element_type=jnp.float32,
    )
    leaf_total = leaf_radiosity_field + jnp.einsum(
        "xlsr,lrb->xlsb",
        up_leaf,
        pair_total.astype(jnp.bfloat16),
        preferred_element_type=jnp.float32,
    )
    far_part = jnp.einsum(
        "xlrj,xlrb->bxlj",
        basis,
        leaf_total.astype(jnp.bfloat16),
        preferred_element_type=jnp.float32,
    )
    return emission + reflect * (nearby_portion + far_part)


def solution(mesh):
    return jax.shard_map(
        body,
        mesh=mesh,
        in_specs=(
            P(None, "section", "perim", None),
            P(None, "section", "perim", None),
            P(None, "section", "perim", None),
            P("section", "perim", None, None),
            P("section", "perim", None, None),
            P("section", "perim", None, None),
            P("section", "perim", None, None, None),
            P("section", "perim", None, None),
            P("section", "perim", None, None),
            P("section", "perim", None, None),
            P("section", "perim", None),
            P("section", "perim", None),
            P("section", "perim", None),
            P("section", "perim", None),
        ),
        out_specs=P(None, "section", "perim", None),
        check_vma=False,
    )
```

profile of v0, /device:TPU:1, one launch (start us, length us, event | category | flops | bytes accessed | tf_op | source)
XLA Modules:
  0.0 147.5 jit_solution(17012552225369399940)
XLA Ops:
  0.1 1.1 convert_element_type.40
  1.1 1.3 convolution_convert_fusion.1
  2.6 1.2 fusion.11
  4.4 20.9 %all_gather.6 = bf16[384,512]{1,0:T(8,128)(2,1)S(1)} all-gather(bf16[24,512]{1,0:T(8,128)(2,1)S(1)} %pad_maximum_fusion.5), channel_id=1, replica_groups=mesh['section'=8,'perim'=16] {'perim'}, dimensions={0}, use_global_device_ids=true | all-gather | bytes 417792 | tf_op jit(solution)/shard_map/all_gather | solution.py:112
  25.3 7.8 %collective-permute-start.5 = (bf16[1,384,512]{2,1,0:T(8,128)(2,1)S(1)}, bf16[1,384,512]{2,1,0:T(8,128)(2,1)}, u32[]{:S(2)}, u32[]{:S(2)}) collective-permute-start(bf16[1,384,512]{2,1,0:T(8,128)(2,1)S(1)} %bitcast.108), channel_id=1, source_target_pairs={{16,0},{32,16},{48,32},{64,48},{80,64},{96,80},{112,96},{17,1},{33... | collective-permute-start | bytes 1179656 | tf_op jit(solution)/shard_map/ppermute | solution.py:17
  33.1 3.1 %collective-permute-start.4 = (bf16[1,384,512]{2,1,0:T(8,128)(2,1)S(1)}, bf16[1,384,512]{2,1,0:T(8,128)(2,1)}, u32[]{:S(2)}, u32[]{:S(2)}) collective-permute-start(bf16[1,384,512]{2,1,0:T(8,128)(2,1)S(1)} %bitcast.109), channel_id=1, source_target_pairs={{0,16},{16,32},{32,48},{48,64},{64,80},{80,96},{96,112},{1,17},{17... | collective-permute-start | bytes 1179656 | tf_op jit(solution)/shard_map/ppermute | solution.py:15
  36.2 1.0 collective-permute-start
  37.2 3.9 %collective-permute-start.1 = (bf16[8,2,1,256]{3,2,1,0:T(2,128)(2,1)S(1)}, bf16[8,2,1,256]{3,2,1,0:T(2,128)(2,1)S(1)}, u32[]{:S(2)}, u32[]{:S(2)}) collective-permute-start(bf16[8,2,1,256]{3,2,1,0:T(2,128)(2,1)S(1)} %get-tuple-element.18), channel_id=1, source_target_pairs={{1,0},{2,1},{3,2},{4,3},{5,4},{6,5},{7,6},{8,7},{9,8},{10,9},{11,1... | collective-permute-start | bytes 24584 | tf_op jit(solution)/shard_map/ppermute | solution.py:17
  42.1 57.4 %all-gather = bf16[128,1,512]{2,1,0:T(2,128)(2,1)S(1)} all-gather(bf16[1,1,512]{2,1,0:T(2,128)(2,1)S(1)} %reshape.100), channel_id=1, replica_groups=mesh['section'=8,'perim'=16] {'section','perim'}, dimensions={0}, use_global_device_ids=true | all-gather | bytes 132096 | tf_op jit(solution)/shard_map/all_gather | solution.py:132
  99.9 0.8 copy.244
  100.6 0.8 reshape.99
  101.6 2.9 %collective-permute-start.3 = (bf16[8,1,10,256]{3,2,1,0:T(8,128)(2,1)S(1)}, bf16[8,1,10,256]{3,2,1,0:T(8,128)(2,1)S(1)}, u32[]{:S(2)}, u32[]{:S(2)}) collective-permute-start(bf16[8,1,10,256]{3,2,1,0:T(8,128)(2,1)S(1)} %get-tuple-element.11), channel_id=1, source_target_pairs={{16,0},{32,16},{48,32},{64,48},{80,64},{96,80},{112,96},{17,1},{33... | collective-permute-start | bytes 122888 | tf_op jit(solution)/shard_map/ppermute | solution.py:17
  104.5 2.6 %collective-permute-start.2 = (bf16[8,1,10,256]{3,2,1,0:T(8,128)(2,1)S(1)}, bf16[8,1,10,256]{3,2,1,0:T(8,128)(2,1)S(1)}, u32[]{:S(2)}, u32[]{:S(2)}) collective-permute-start(bf16[8,1,10,256]{3,2,1,0:T(8,128)(2,1)S(1)} %get-tuple-element.12), channel_id=1, source_target_pairs={{0,16},{16,32},{32,48},{48,64},{64,80},{80,96},{96,112},{1,17},{17... | collective-permute-start | bytes 122888 | tf_op jit(solution)/shard_map/ppermute | solution.py:15
  107.2 0.8 copy.245
  108.0 0.8 copy.243
  108.9 0.8 copy.248
  109.7 0.7 copy.247
  110.5 0.8 copy.246
  111.2 0.8 copy.240
  112.0 0.8 copy.241
  112.7 0.7 copy.242
  113.5 4.6 %stack.39 = bf16[9,8,2,8,256]{4,0,1,3,2:T(8,128)(2,1)S(1)} concatenate(bf16[1,8,2,8,256]{4,0,1,3,2:T(2,128)(2,1)} %copy.240, bf16[1,8,2,8,256]{4,0,1,3,2:T(2,128)(2,1)} %copy.241, bf16[1,8,2,8,256]{4,0,1,3,2:T(2,128)(2,1)} %copy.242, bf16[1,8,2,8,256]{4,0,1,3,2:T(2,128)(2,1)} %copy.243, bf16[1,8,2,8,256]{4,0,1,3,2:T(2,128)(2,1)} %copy.244, bf16[1,8,2,8,256]{4,0,1,3,2:T(2,128)(2,1)} %copy.245, ...), dimensions={0} | concatenate | bytes 1179648 | tf_op jit(solution)/shard_map/stack | solution.py:62
  118.4 8.6 %convolution_bitcast_fusion = f32[2,8,8,256]{3,2,1,0:T(8,128)} fusion(bf16[2,8,6,256,256]{4,3,2,1,0:T(8,128)(2,1)} %param.20, bf16[2,8,6,8,256]{4,2,3,1,0:T(8,128)(2,1)S(1)} %convolution_convert_fusion), kind=kOutput, calls=%fused_computation.9 | convolution fusion | flops 100663296 | bytes 13107200 | tf_op jit(solution)/shard_map/xlnij,xlnbj->bxli/dot_general | solution.py:77
  127.0 1.2 pad_maximum_fusion
  128.3 0.7 fusion.1
  129.0 3.4 %reshape.97 = bf16[8,1024,8]{2,1,0:T(8,128)(2,1)} reshape(bf16[128,512]{1,0:T(8,128)(2,1)S(1)} %slice.75) | data formatting | bytes 262144 | tf_op jit(solution)/shard_map/reshape | solution.py:125
  132.5 5.9 %reshape.96 = bf16[2,8,1024,8]{3,2,1,0:T(8,128)(2,1)} reshape(bf16[256,512]{1,0:T(8,128)(2,1)S(1)} %slice.74) | data formatting | bytes 524288 | tf_op jit(solution)/shard_map/reshape | solution.py:124
  138.4 2.3 %convolution_bitcast_fusion.4 = f32[8,64,8]{1,2,0:T(8,128)S(1)} fusion(bf16[8,1024,8]{2,1,0:T(8,128)(2,1)} %reshape.97, bf16[1,8,64,1024]{3,2,1,0:T(8,128)(2,1)S(1)} %copy-done.2), kind=kOutput, calls=%fused_computation.17 | convolution fusion | flops 8388608 | bytes 1196032 | tf_op jit(solution)/shard_map/lrc,lcb->lrb/dot_general | solution.py:129
  140.7 3.5 %convolution_bitcast_fusion.2 = f32[2,8,64,8]{2,3,1,0:T(8,128)S(1)} fusion(bf16[2,8,1024,8]{3,2,1,0:T(8,128)(2,1)} %reshape.96, bf16[2,8,64,1024]{3,2,1,0:T(8,128)(2,1)S(1)} %copy-done), kind=kOutput, calls=%fused_computation.12 | convolution fusion | flops 16777216 | bytes 2392064 | tf_op jit(solution)/shard_map/xlrc,xlcb->xlrb/dot_general | solution.py:126
  144.2 1.2 fusion.10
  145.4 1.4 fusion.4
  146.8 0.7 copy.258
  (66 shorter events, 3.0 us)
Async XLA Ops:
  0.0 140.6 %copy-start = (bf16[2,8,64,1024]{3,2,1,0:T(8,128)(2,1)S(1)}, bf16[2,8,64,1024]{3,2,1,0:T(8,128)(2,1)}, u32[]{:S(2)}) copy-start(bf16[2,8,64,1024]{3,2,1,0:T(8,128)(2,1)} %param.21) | copy-start | bytes 6291460
  0.0 41.1 %copy-start.8 = (f32[8,2,8,256]{3,2,1,0:T(8,128)S(1)}, f32[8,2,8,256]{3,2,1,0:T(8,128)}, u32[]{:S(2)}) copy-start(f32[8,2,8,256]{3,2,1,0:T(8,128)} %param.14) | copy-start | bytes 393220
  0.0 41.1 %copy-start.12 = (s32[1,8,16]{2,1,0:T(8,128)S(1)}, s32[1,8,16]{2,1,0:T(8,128)}, u32[]{:S(2)}) copy-start(s32[1,8,16]{2,1,0:T(8,128)} %param.26) | copy-start | bytes 1540
  0.0 41.4 %copy-start.10 = (s32[2,8,16]{2,1,0:T(8,128)S(1)}, s32[2,8,16]{2,1,0:T(8,128)}, u32[]{:S(2)}) copy-start(s32[2,8,16]{2,1,0:T(8,128)} %param.25) | copy-start | bytes 3076
  0.0 41.6 %copy-start.5 = (bf16[1,8,64,64]{3,2,1,0:T(8,128)(2,1)S(1)}, bf16[1,8,64,64]{3,2,1,0:T(8,128)(2,1)}, u32[]{:S(2)}) copy-start(bf16[1,8,64,64]{3,2,1,0:T(8,128)(2,1)} %param.19) | copy-start | bytes 196612
  0.0 99.4 %copy-start.13 = (s32[1,1,8]{2,1,0:T(1,128)S(1)}, s32[1,1,8]{2,1,0:T(1,128)}, u32[]{:S(2)}) copy-start(s32[1,1,8]{2,1,0:T(1,128)} %param.27) | copy-start | bytes 100
  0.0 99.6 %copy-start.11 = (s32[2,8,6]{1,0,2:T(2,128)S(1)}, s32[2,8,6]{1,0,2:T(2,128)}, u32[]{:S(2)}) copy-start(s32[2,8,6]{1,0,2:T(2,128)} %param.24) | copy-start | bytes 1156
  25.3 101.7 %collective-permute-start.5 = (bf16[1,384,512]{2,1,0:T(8,128)(2,1)S(1)}, bf16[1,384,512]{2,1,0:T(8,128)(2,1)}, u32[]{:S(2)}, u32[]{:S(2)}) collective-permute-start(bf16[1,384,512]{2,1,0:T(8,128)(2,1)S(1)} %bitcast.108), channel_id=1, source_target_pairs={{16,0},{32,16},{48,32},{64,48},{80,64},{96,80},{112,96},{17,1},{33... | collective-permute-start | bytes 1179656 | tf_op jit(solution)/shard_map/ppermute | solution.py:17
  33.1 94.0 %collective-permute-start.4 = (bf16[1,384,512]{2,1,0:T(8,128)(2,1)S(1)}, bf16[1,384,512]{2,1,0:T(8,128)(2,1)}, u32[]{:S(2)}, u32[]{:S(2)}) collective-permute-start(bf16[1,384,512]{2,1,0:T(8,128)(2,1)S(1)} %bitcast.109), channel_id=1, source_target_pairs={{0,16},{16,32},{32,48},{48,64},{64,80},{80,96},{96,112},{1,17},{17... | collective-permute-start | bytes 1179656 | tf_op jit(solution)/shard_map/ppermute | solution.py:15
  36.2 65.3 %collective-permute-start = (bf16[8,2,1,256]{3,2,1,0:T(2,128)(2,1)S(1)}, bf16[8,2,1,256]{3,2,1,0:T(2,128)(2,1)S(1)}, u32[]{:S(2)}, u32[]{:S(2)}) collective-permute-start(bf16[8,2,1,256]{3,2,1,0:T(2,128)(2,1)S(1)} %get-tuple-element.17), channel_id=1, source_target_pairs={{0,1},{1,2},{2,3},{3,4},{4,5},{5,6},{6,7},{7,8},{8,9},{9,10},{10,1... | collective-permute-start | bytes 24584 | tf_op jit(solution)/shard_map/ppermute | solution.py:15
  37.2 64.3 %collective-permute-start.1 = (bf16[8,2,1,256]{3,2,1,0:T(2,128)(2,1)S(1)}, bf16[8,2,1,256]{3,2,1,0:T(2,128)(2,1)S(1)}, u32[]{:S(2)}, u32[]{:S(2)}) collective-permute-start(bf16[8,2,1,256]{3,2,1,0:T(2,128)(2,1)S(1)} %get-tuple-element.18), channel_id=1, source_target_pairs={{1,0},{2,1},{3,2},{4,3},{5,4},{6,5},{7,6},{8,7},{9,8},{10,9},{11,1... | collective-permute-start | bytes 24584 | tf_op jit(solution)/shard_map/ppermute | solution.py:17
  101.6 7.2 %collective-permute-start.3 = (bf16[8,1,10,256]{3,2,1,0:T(8,128)(2,1)S(1)}, bf16[8,1,10,256]{3,2,1,0:T(8,128)(2,1)S(1)}, u32[]{:S(2)}, u32[]{:S(2)}) collective-permute-start(bf16[8,1,10,256]{3,2,1,0:T(8,128)(2,1)S(1)} %get-tuple-element.11), channel_id=1, source_target_pairs={{16,0},{32,16},{48,32},{64,48},{80,64},{96,80},{112,96},{17,1},{33... | collective-permute-start | bytes 122888 | tf_op jit(solution)/shard_map/ppermute | solution.py:17
  104.5 4.2 %collective-permute-start.2 = (bf16[8,1,10,256]{3,2,1,0:T(8,128)(2,1)S(1)}, bf16[8,1,10,256]{3,2,1,0:T(8,128)(2,1)S(1)}, u32[]{:S(2)}, u32[]{:S(2)}) collective-permute-start(bf16[8,1,10,256]{3,2,1,0:T(8,128)(2,1)S(1)} %get-tuple-element.12), channel_id=1, source_target_pairs={{0,16},{16,32},{32,48},{48,64},{64,80},{80,96},{96,112},{1,17},{17... | collective-permute-start | bytes 122888 | tf_op jit(solution)/shard_map/ppermute | solution.py:15
  132.5 5.9 %copy-start.2 = (bf16[1,8,64,1024]{3,2,1,0:T(8,128)(2,1)S(1)}, bf16[1,8,64,1024]{3,2,1,0:T(8,128)(2,1)}, u32[]{:S(2)}) copy-start(bf16[1,8,64,1024]{3,2,1,0:T(8,128)(2,1)} %param.22) | copy-start | bytes 3145732
  140.6 3.6 %copy-start.6 = (bf16[1,8,64,64]{3,2,1,0:T(8,128)(2,1)S(1)}, bf16[1,8,64,64]{3,2,1,0:T(8,128)(2,1)}, u32[]{:S(2)}) copy-start(bf16[1,8,64,64]{3,2,1,0:T(8,128)(2,1)} %param.19) | copy-start | bytes 196612
  140.6 3.6 %copy-start.7 = (bf16[512,8]{1,0:T(8,128)(2,1)S(1)}, bf16[512,8]{1,0:T(8,128)(2,1)}, u32[]{:S(2)}) copy-start(bf16[512,8]{1,0:T(8,128)(2,1)} %reshape.99) | copy-start | bytes 24580
  140.6 4.7 %copy-start.1 = (bf16[2,8,64,256]{3,2,1,0:T(8,128)(2,1)S(1)}, bf16[2,8,64,256]{3,2,1,0:T(8,128)(2,1)}, u32[]{:S(2)}) copy-start(bf16[2,8,64,256]{3,2,1,0:T(8,128)(2,1)} %param.17) | copy-start | bytes 1572868
  140.7 4.7 %copy-start.3 = (bf16[2,8,64,64]{3,2,1,0:T(8,128)(2,1)S(1)}, bf16[2,8,64,64]{3,2,1,0:T(8,128)(2,1)}, u32[]{:S(2)}) copy-start(bf16[2,8,64,64]{3,2,1,0:T(8,128)(2,1)} %param.18) | copy-start | bytes 393220
  140.7 4.7 %copy-start.4 = (f32[2,8,8,256]{3,2,1,0:T(8,128)S(1)}, f32[2,8,8,256]{3,2,1,0:T(8,128)}, u32[]{:S(2)}) copy-start(f32[2,8,8,256]{3,2,1,0:T(8,128)} %convolution_bitcast_fusion) | copy-start | bytes 393220
  140.7 4.7 %copy-start.9 = (f32[8,2,8,256]{3,2,1,0:T(8,128)S(1)}, f32[8,2,8,256]{3,2,1,0:T(8,128)}, u32[]{:S(2)}) copy-start(f32[8,2,8,256]{3,2,1,0:T(8,128)} %param.15) | copy-start | bytes 393220
where the time goes:
time: 148 us
  blocking collectives  78.3 us (53%)
  local copies, waits for them, and re-layouts  24.1 us (16%)
  starting transfers between devices  21.3 us (14%)
  matrix products  20.8 us (14%)
  other arithmetic  2.75 us (2%)
    all_gather x1, blocking collectives, body(): lax.all_gather(top_coef.reshape(1, rank_size * band_size), ('section', 'p...  57.4 us
    all_gather x1, blocking collectives, body(): beside_all = lax.all_gather(coeffs, 'perim', axis=0, tiled=True)  20.9 us
    ppermute x3, starting transfers between devices, padded(): lax.ppermute(head, axis, [((i + 1) % count, i) for i in range(ends)])  14.6 us
    another operation x11, local copies, waits for them, and re-layouts, body(): jnp.stack([broadened_result[:, 1 + height_step:1 + height_step + row_coun...  11.5 us
    dot_general x1, matrix products, body(): jnp.einsum('xlnij,xlnbj->bxli', near_block, collected_near_rows, preferre...  8.58 us
    ppermute x3, starting transfers between devices, padded(): lax.ppermute(tail, axis, [(i, (i + 1) % count) for i in range(ends)])  6.71 us
    reshape x1, local copies, waits for them, and re-layouts, body(): picked[:split_at].reshape(row_count, column_count, -1, band_size)  5.87 us
    dot_general x1, matrix products, body(): jnp.einsum('xlrc,xlcb->xlrb', couple_leaf, leaf_pick, preferred_element_t...  3.5 us
  transfers between devices with their start and end apart: 6, of which 0 were waited for; matrix products, arithmetic and copies ran while one was open for 15% of the time, Pallas kernels for 0%

commit v1 on v0

v1 whole, which is shorter than its diff:
```python
import jax
import jax.numpy as jnp
from jax import lax
from jax.experimental import pallas as pl
from jax.experimental.pallas import tpu as pltpu
from jax.sharding import PartitionSpec as P

F32 = jnp.float32
BF16 = jnp.bfloat16
NT = (((1,), (1,)), ((), ()))
NN = (((1,), (0,)), ((), ()))
LANES = 128
RANK = 64
WIDE = 1152
VMEM = pl.BlockSpec(memory_space=pltpu.VMEM)
SMEM = pl.BlockSpec(memory_space=pltpu.SMEM)


def dot(left, right, dims):
    return lax.dot_general(left, right, dims, preferred_element_type=F32)


def row_of(shape, count):
    return lax.broadcasted_iota(jnp.int32, shape, 0) % count


def own_blocks(products, count):
    shape = (products.shape[0], LANES)
    mine = row_of(shape, count) - lax.broadcasted_iota(jnp.int32, shape, 1) // RANK
    total = jnp.zeros(shape, F32)
    for tile in range(count // 2):
        total += jnp.where(mine == 2 * tile, products[:, tile * LANES : (tile + 1) * LANES], 0.0)
    return total + pltpu.roll(total, RANK, 1)


def side_by_side(twice, count):
    low = lax.broadcasted_iota(jnp.int32, (count, LANES), 1) < RANK
    return jnp.concatenate(
        [
            jnp.where(low, twice[b * count : (b + 1) * count], twice[(b + 1) * count : (b + 2) * count])
            for b in range(0, twice.shape[0] // count, 2)
        ],
        axis=1,
    )


def coefficients_kernel(
    place, radiosity, basis, up_leaf, up_pair, sent, cells, to_mate, to_other
):
    section, column = place[0], place[1]
    bands, rows, cols, leaf = radiosity.shape
    leaves = rows * cols
    for g in range(rows):
        turned = jnp.swapaxes(radiosity[:, g], 0, 1)
        cells[g * cols : (g + 1) * cols] = turned.astype(BF16)
    odd = section % 2
    for g in range(rows):
        row = cells[g * cols : (g + 1) * cols]

        @pl.when(odd == g)
        def _():
            to_other[...] = row

        @pl.when(odd != g)
        def _():
            to_mate[...] = row

    shaded = radiosity[...].reshape(bands * leaves, leaf).astype(BF16)
    leaf_twice = own_blocks(dot(shaded, basis[...], NT), leaves)
    leaf_coef = leaf_twice[:, :RANK].astype(BF16)
    parts = jnp.zeros((bands * leaves, RANK), F32)
    which = row_of(parts.shape, leaves)
    for at in range(leaves):
        parts += jnp.where(which == at, dot(leaf_coef, up_leaf[at], NN), 0.0)
    pair = jnp.sum(parts.reshape(bands, rows, cols, RANK), axis=1).reshape(bands * cols, RANK)
    pair_coef = pair.astype(BF16)
    parts = jnp.zeros((bands * cols, RANK), F32)
    which = row_of(parts.shape, cols)
    for at in range(cols):
        parts += jnp.where(which == at, dot(pair_coef, up_pair[at], NN), 0.0)
    top = jnp.sum(parts.reshape(bands, cols, RANK), axis=1)
    top_twice = jnp.concatenate([top, top], axis=1)
    pair_twice = jnp.concatenate([pair, pair], axis=1)

    def edge(col):
        return jnp.concatenate(
            [radiosity[:, g, col, :] for g in range(rows)], axis=1
        )

    leaf_part = side_by_side(leaf_twice, leaves)
    pair_part = side_by_side(pair_twice, cols)
    top_part = jnp.concatenate([top_twice, jnp.zeros_like(top_twice)], axis=0)

    def block(col):
        return jnp.concatenate(
            [leaf_part, jnp.concatenate([pair_part, edge(col)], axis=0), top_part], axis=1
        ).astype(BF16)

    first = block(0)
    for to in range(sent.shape[0]):
        sent[to] = first
    sent[(column + 1) % sent.shape[0]] = block(cols - 1)


def near_kernel(
    place, listed, cells, from_mate, from_other, ring, ring_mate, ring_other, blocks, out, window
):
    section, column = place[0], place[1]
    step = pl.program_id(0)
    cols = from_mate.shape[0]
    leaf = cells.shape[-1]
    around = ring.shape[0]
    broad = cols + 2

    @pl.when(step == 0)
    def _():
        odd = section % 2
        left = (column + around - 1) % around
        right = (column + 1) % around

        def edges(source, g, at):
            start = at * broad
            lanes = slice(512 + g * leaf, 512 + (g + 1) * leaf)
            window[start] = source[left, 8:16, lanes].astype(F32)
            window[start + broad - 1] = source[right, 8:16, lanes].astype(F32)

        for g in range(2):
            start = (g + 1) * broad + 1
            window[start : start + cols] = cells[g * cols : (g + 1) * cols].astype(F32)
            edges(ring, g, g + 1)

        @pl.when(odd == 0)
        def _():
            window[1 : 1 + cols] = from_other[...].astype(F32)
            window[3 * broad + 1 : 3 * broad + 1 + cols] = from_mate[...].astype(F32)
            edges(ring_other, 1, 0)
            edges(ring_mate, 0, 3)

        @pl.when(odd == 1)
        def _():
            window[1 : 1 + cols] = from_mate[...].astype(F32)
            window[3 * broad + 1 : 3 * broad + 1 + cols] = from_other[...].astype(F32)
            edges(ring_mate, 1, 0)
            edges(ring_other, 0, 3)

    count = blocks.shape[1]
    width_all = around * cols
    total = jnp.zeros(out.shape[1:], F32)
    for n in range(count):
        name = listed[step * count + n]
        up = name // width_all - 2 * section + 1
        turn = (name % width_all + width_all + 1 - cols * column) % width_all
        seen = window[up * broad + turn].astype(BF16)
        total += dot(seen, blocks[0, n], NT)
    out[0] = total


def chosen(tables, lanes, tier, inner, count):
    size = tables[0].shape[0] * tables[0].shape[1]
    picks = inner.shape[1]
    result = jnp.zeros((count * picks, 512), F32)
    at = lax.broadcasted_iota(jnp.int32, (count, size), 1)
    for number, table in enumerate(tables):
        slots = jnp.where(tier == number, inner, -1)
        choose = jnp.concatenate(
            [(at == slots[:, k : k + 1]).astype(F32) for k in range(picks)], axis=0
        ).astype(BF16)
        result += dot(choose, table[:, :, lanes].reshape(size, 512), NN)
    low = lax.broadcasted_iota(jnp.int32, (count, LANES), 1) < RANK
    bands = []
    for n in range(4):
        even, odd = [], []
        for k in range(0, picks, 2):
            one = result[k * count : (k + 1) * count, n * LANES : (n + 1) * LANES]
            two = result[(k + 1) * count : (k + 2) * count, n * LANES : (n + 1) * LANES]
            even.append(jnp.where(low, one, pltpu.roll(two, RANK, 1)))
            odd.append(jnp.where(low, pltpu.roll(one, RANK, 1), two))
        bands += [jnp.concatenate(even, axis=1), jnp.concatenate(odd, axis=1)]
    return jnp.concatenate(bands, axis=0).astype(BF16)


def far_kernel(
    place,
    far_top,
    far_leaf,
    far_pair,
    ring,
    ring_mate,
    ring_other,
    tops,
    couple_leaf,
    couple_pair,
    couple_top,
    basis,
    up_leaf,
    up_pair,
    near,
    emission,
    reflect,
    out,
):
    section = place[0]
    mate = section + 1 - 2 * (section % 2)
    bands, rows, cols, leaf = out.shape
    leaves = rows * cols
    around = ring.shape[0]
    width_all = around * cols
    tables = (ring, ring_mate, ring_other)

    def tier_of(source):
        return jnp.where(source == section, 0, jnp.where(source == mate, 1, 2))

    names = far_leaf[...]
    turn = names % width_all
    height = names // width_all
    leaf_pick = chosen(
        tables,
        slice(0, 512),
        tier_of(height // rows),
        turn // cols * leaves + height % rows * cols + turn % cols,
        leaves,
    )
    leaf_field = own_blocks(dot(leaf_pick, couple_leaf[...], NT), leaves)[:, :RANK]
    names = far_pair[...]
    turn = names % width_all
    pair_pick = chosen(
        tables,
        slice(512, 1024),
        tier_of(names // width_all),
        turn // cols * leaves + turn % cols,
        cols,
    )
    pair_field = own_blocks(dot(pair_pick, couple_pair[...], NT), cols)[:, :RANK]
    top_pick = jnp.concatenate(
        [tops[far_top[k]][:, :RANK].astype(F32) for k in range(far_top.shape[0])], axis=1
    ).astype(BF16)
    top_field = dot(top_pick, couple_top[...], NT)
    spread = jnp.broadcast_to(top_field[:, None, :], (bands, cols, RANK))
    spread = spread.reshape(bands * cols, RANK).astype(BF16)
    pair_total = pair_field + own_blocks(dot(spread, up_pair[...], NT), cols)[:, :RANK]
    spread = jnp.broadcast_to(
        pair_total.reshape(bands, 1, cols, RANK), (bands, rows, cols, RANK)
    )
    spread = spread.reshape(bands * leaves, RANK).astype(BF16)
    leaf_total = leaf_field + own_blocks(dot(spread, up_leaf[...], NT), leaves)[:, :RANK]
    leaf_total = leaf_total.astype(BF16)
    far_part = jnp.zeros((bands * leaves, leaf), F32)
    which = row_of(far_part.shape, leaves)
    for at in range(leaves):
        far_part += jnp.where(which == at, dot(leaf_total, basis[at], NN), 0.0)
    far_part = far_part.reshape(bands, rows, cols, leaf)
    for g in range(rows):
        near_part = jnp.swapaxes(near[g * cols : (g + 1) * cols], 0, 1)
        out[:, g] = emission[:, g] + reflect[:, g] * (near_part + far_part[:, g])


def body(
    radiosity,
    emission,
    reflect,
    basis,
    up_leaf,
    upward_pair_transfer,
    near_block,
    couple_leaf,
    couple_pair,
    couple_top,
    near_list,
    far_leaf,
    far_pair,
    far_top,
):
    around = lax.axis_size("perim")
    tall = lax.axis_size("section")
    bands, rows, cols, leaf = radiosity.shape
    leaves = rows * cols
    place = jnp.stack([lax.axis_index("section"), lax.axis_index("perim")]).astype(jnp.int32)
    mates = [(s, s ^ 1) for s in range(tall)]
    others = [(s, s + 1 if s % 2 else s - 1) for s in range(1, tall - 1)]
    params = pltpu.CompilerParams(vmem_limit_bytes=40 * 1024 * 1024)
    sent, cells, to_mate, to_other = pl.pallas_call(
        coefficients_kernel,
        out_shape=[
            jax.ShapeDtypeStruct((around, 16, WIDE), BF16),
            jax.ShapeDtypeStruct((leaves, bands, leaf), BF16),
            jax.ShapeDtypeStruct((cols, bands, leaf), BF16),
            jax.ShapeDtypeStruct((cols, bands, leaf), BF16),
        ],
        in_specs=[SMEM, VMEM, VMEM, VMEM, VMEM],
        out_specs=[VMEM] * 4,
        compiler_params=params,
        name="coefficients",
    )(
        place,
        radiosity,
        basis.reshape(leaves * RANK, leaf),
        up_leaf.reshape(leaves, RANK, RANK),
        upward_pair_transfer[0],
    )
    from_mate = lax.ppermute(to_mate, "section", mates)
    from_other = lax.ppermute(to_other, "section", others)
    ring = lax.all_to_all(sent, "perim", 0, 0)
    ring_mate = lax.ppermute(ring, "section", mates)
    ring_other = lax.ppermute(ring, "section", others)
    tops = ring[:, :bands, 1024:]
    tops = lax.all_to_all(jnp.broadcast_to(tops[None], (tall,) + tops.shape), "section", 0, 0)
    near = pl.pallas_call(
        near_kernel,
        grid=(leaves,),
        out_shape=jax.ShapeDtypeStruct((leaves, bands, leaf), F32),
        in_specs=[SMEM, SMEM] + [VMEM] * 6
        + [pl.BlockSpec((1,) + near_block.shape[2:], lambda i: (i, 0, 0, 0))],
        out_specs=pl.BlockSpec((1, bands, leaf), lambda i: (i, 0, 0)),
        scratch_shapes=[pltpu.VMEM(((rows + 2) * (cols + 2), bands, leaf), F32)],
        compiler_params=params,
        name="near",
    )(
        place,
        near_list.reshape(-1),
        cells,
        from_mate,
        from_other,
        ring,
        ring_mate,
        ring_other,
        near_block.reshape((leaves,) + near_block.shape[2:]),
    )
    return pl.pallas_call(
        far_kernel,
        out_shape=jax.ShapeDtypeStruct(radiosity.shape, F32),
        in_specs=[SMEM, SMEM] + [VMEM] * 15,
        out_specs=VMEM,
        compiler_params=params,
        name="far",
    )(
        place,
        far_top.reshape(-1),
        far_leaf.reshape(leaves, -1),
        far_pair.reshape(cols, -1),
        ring,
        ring_mate,
        ring_other,
        tops.reshape(tall * around, bands, LANES),
        couple_leaf.reshape(leaves * RANK, -1),
        couple_pair.reshape(cols * RANK, -1),
        couple_top[0, 0],
        basis.reshape(leaves, RANK, leaf),
        up_leaf.reshape(leaves * RANK, RANK),
        upward_pair_transfer.reshape(cols * RANK, RANK),
        near,
        emission,
        reflect,
    )


def solution(mesh):
    cells = P(None, "section", "perim", None)
    four = P("section", "perim", None, None)
    lists = P("section", "perim", None)
    return jax.shard_map(
        body,
        mesh=mesh,
        in_specs=(cells,) * 3
        + (four,) * 3
        + (P("section", "perim", None, None, None),)
        + (four,) * 3
        + (lists,) * 4,
        out_specs=cells,
        check_vma=False,
    )
```

time: 148 us -> 68.7 us (0.46)
  blocking collectives: 78.3 us -> 19.5 us
  matrix products: 20.8 us -> 0 us
  Pallas kernels: 0 us -> 18.1 us
  starting transfers between devices: 21.3 us -> 13.5 us
  local copies, waits for them, and re-layouts: 24.1 us -> 16.6 us
  other arithmetic: 2.75 us -> 0.07 us
    all_gather x2 -> x0, blocking collectives: 78.3 us -> none  [the longest x1 57.4 us: body(): lax.all_gather(top_coef.reshape(1, rank_size * band_size), ('section', 'p...]
    dot_general x11 -> x0, matrix products: 20.8 us -> none  [the longest x1 8.58 us: body(): jnp.einsum('xlnij,xlnbj->bxli', near_block, collected_near_rows, preferre...]
    all_to_all x0 -> x1, blocking collectives: none -> 19.5 us  [body(): ring = lax.all_to_all(sent, 'perim', 0, 0)]
    pallas_call x0 -> x3, Pallas kernels: none -> 18.1 us  [the longest x1 12.4 us: body(): pl.pallas_call(near_kernel, grid=(leaves,), out_shape=jax.ShapeDtypeStruc...]
    unnamed x29 -> x45, local copies, waits for them, and re-layouts: 0.19 us -> 14.5 us
    ppermute x6 -> x4, starting transfers between devices: 21.3 us -> 8.8 us  [the longest x1 5.03 us: body(): ring_other = lax.ppermute(ring, 'section', others)]
    another operation x11 -> x0, local copies, waits for them, and re-layouts: 11.5 us -> none  [body(): jnp.stack([broadened_result[:, 1 + height_step:1 + height_step + row_coun...]
    reshape x5 -> x1, local copies, waits for them, and re-layouts: 10.7 us -> 1.36 us  [body(): near_list.reshape(-1)]
  transfers between devices with their start and end apart: 6 -> 5, of which waited for: 0 -> 0; matrix products, arithmetic and copies ran while one was open for 15% -> 5% of each run, Pallas kernels for 0% -> 18%
where the time goes in v1:
time: 68.7 us; the launch traced here: 67.9 us
  blocking collectives  19.5 us (28%)
  Pallas kernels  18.1 us (26%)
  local copies, waits for them, and re-layouts  16.6 us (24%)
  starting transfers between devices  13.5 us (20%)
    all_to_all x1, blocking collectives, body(): ring = lax.all_to_all(sent, 'perim', 0, 0)  19.5 us
    unnamed x45, local copies, waits for them, and re-layouts  14.5 us
    pallas_call x1, Pallas kernels, body(): pl.pallas_call(near_kernel, grid=(leaves,), out_shape=jax.ShapeDtypeStruc...  12.4 us
    ppermute x1, starting transfers between devices, body(): ring_other = lax.ppermute(ring, 'section', others)  5.03 us
    all_to_all x1, starting transfers between devices, body(): lax.all_to_all(jnp.broadcast_to(tops[None], (tall,) + tops.shape), 'secti...  4.66 us
    pallas_call x1, Pallas kernels, body(): pl.pallas_call(far_kernel, out_shape=jax.ShapeDtypeStruct(radiosity.shape...  4.22 us
    ppermute x1, starting transfers between devices, body(): from_other = lax.ppermute(to_other, 'section', others)  3.66 us
    pallas_call x1, Pallas kernels, body(): pl.pallas_call(coefficients_kernel, out_shape=[jax.ShapeDtypeStruct((arou...  1.46 us
  transfers between devices with their start and end apart: 5, of which 0 were waited for; matrix products, arithmetic and copies ran while one was open for 5% of the time, Pallas kernels for 18%

profile of v1, /device:TPU:1, one launch (start us, length us, event | category | flops | bytes accessed | tf_op | source)
XLA Modules:
  0.0 67.9 jit_solution(7357491527818144086)
XLA Ops:
  0.0 0.1 pad_add_fusion.place
  0.1 1.0 %copy-done = bf16[2,8,64,256]{3,2,1,0:T(8,128)(2,1)S(1)} copy-done((bf16[2,8,64,256]{3,2,1,0:T(8,128)(2,1)S(1)}, bf16[2,8,64,256]{3,2,1,0:T(8,128)(2,1)}, u32[]{:S(2)}) %copy-start) | copy-done | bytes 524312
  1.1 0.9 %copy-done.4 = bf16[2,8,64,64]{3,2,1,0:T(8,128)(2,1)S(1)} copy-done((bf16[2,8,64,64]{3,2,1,0:T(8,128)(2,1)S(1)}, bf16[2,8,64,64]{3,2,1,0:T(8,128)(2,1)}, u32[]{:S(2)}) %copy-start.4) | copy-done | bytes 131096
  2.1 0.9 %copy-done.6 = bf16[1,8,64,64]{3,2,1,0:T(8,128)(2,1)S(1)} copy-done((bf16[1,8,64,64]{3,2,1,0:T(8,128)(2,1)S(1)}, bf16[1,8,64,64]{3,2,1,0:T(8,128)(2,1)}, u32[]{:S(2)}) %copy-start.6) | copy-done | bytes 65560
  3.0 0.9 %copy-done.12 = f32[8,2,8,256]{3,2,1,0:T(8,128)S(1)} copy-done((f32[8,2,8,256]{3,2,1,0:T(8,128)S(1)}, f32[8,2,8,256]{3,2,1,0:T(8,128)}, u32[]{:S(2)}) %copy-start.12) | copy-done | bytes 131096
  3.9 1.5 %coefficients.1 = (bf16[16,16,1152]{2,1,0:T(8,128)(2,1)S(1)}, bf16[16,8,256]{2,1,0:T(8,128)(2,1)S(1)}, bf16[8,8,256]{2,1,0:T(8,128)(2,1)S(1)}, bf16[8,8,256]{2,1,0:T(8,128)(2,1)S(1)}) custom-call(s32[2]{0:T(128)S(1)} %pad_add_fusion.place, f32[8,2,8,256]{3,2,1,0:T(8,128)S(1)} %copy-done.12, bf16[1024,256]{1,0:T(8,128)(2,1)S(1)} %bitcast.16, ...), custom_call_target="tpu_custom_call" | custom-call | tf_op jit(solution)/shard_map/coefficients/pallas_call | solution.py:281
  5.4 0.6 copy-done.20
  6.0 0.6 copy-done.21
  6.6 19.5 %all_to_all.10.ring = bf16[16,16,1152]{2,1,0:T(8,128)(2,1)S(1)} all-to-all(bf16[16,16,1152]{2,1,0:T(8,128)(2,1)S(1)} %get-tuple-element.9), channel_id=1, replica_groups=mesh['section'=8,'perim'=16] {'perim'}, dimensions={0} | all-to-all | bytes 1179648 | tf_op jit(solution)/shard_map/all_to_all | solution.py:302
  26.1 5.0 %collective-permute-start.1 = (bf16[16,16,1152]{2,1,0:T(8,128)(2,1)S(1)}, bf16[16,16,1152]{2,1,0:T(8,128)(2,1)S(1)}, u32[]{:S(2)}, u32[]{:S(2)}) collective-permute-start(bf16[16,16,1152]{2,1,0:T(8,128)(2,1)S(1)} %all_to_all.10.ring), channel_id=1, source_target_pairs={{16,32},{32,16},{48,64},{64,48},{80,96},{96,80},{17,33},{33,17},{4... | collective-permute-start | bytes 1769480 | tf_op jit(solution)/shard_map/ppermute | solution.py:304
  31.1 0.1 collective-permute-start
  31.2 0.7 %broadcast_in_dim.2 = bf16[8,16,8,128]{3,2,1,0:T(8,128)(2,1)} broadcast(bf16[16,8,128]{2,1,0:T(8,128)(2,1)S(1)} %slice.4), dimensions={1,2,3} | broadcast | bytes 294912 | tf_op jit(solution)/shard_map/broadcast_in_dim | solution.py:306
  31.9 4.7 %all-to-all-start.1 = ((bf16[8,16,8,128]{3,2,1,0:T(8,128)(2,1)}), bf16[8,16,8,128]{3,2,1,0:T(8,128)(2,1)}, u32[]{:S(2)}, u32[]{:S(2)}) async-start(bf16[8,16,8,128]{3,2,1,0:T(8,128)(2,1)} %broadcast_in_dim.2), calls=%async_computation.1 | async-start | bytes 524288 | tf_op jit(solution)/shard_map/all_to_all | solution.py:306
  36.6 0.0 collective-permute-start.2
  36.6 3.7 %collective-permute-start.3 = (bf16[8,8,256]{2,1,0:T(8,128)(2,1)}, bf16[8,8,256]{2,1,0:T(8,128)(2,1)}, u32[]{:S(2)}, u32[]{:S(2)}) collective-permute-start(bf16[8,8,256]{2,1,0:T(8,128)(2,1)} %copy-done.20), channel_id=1, source_target_pairs={{16,32},{32,16},{48,64},{64,48},{80,96},{96,80},{17,33},{33,17},{4... | collective-permute-start | bytes 98312 | tf_op jit(solution)/shard_map/ppermute | solution.py:301
  40.3 1.4 %copy.16 = s32[2,8,6]{2,1,0:T(8,128)} copy(s32[2,8,6]{1,0,2:T(2,128)} %param.24) | data formatting | bytes 768 | tf_op args[10]
  41.7 1.4 %reshape.51.listed = s32[96]{0:T(128)} reshape(s32[2,8,6]{2,1,0:T(8,128)} %copy.16) | data formatting | bytes 768 | tf_op jit(solution)/shard_map/reshape | solution.py:319
  43.0 0.0 collective-permute-done.2.from_mate
  43.0 0.0 collective-permute-done.3.from_other
  43.0 0.0 copy-start.15
  43.0 0.8 %copy-done.15 = bf16[16,8,256]{2,1,0:T(8,128)(2,1)S(1)} copy-done((bf16[16,8,256]{2,1,0:T(8,128)(2,1)S(1)}, bf16[16,8,256]{2,1,0:T(8,128)(2,1)}, u32[]{:S(2)}) %copy-start.15) | copy-done | bytes 65560
  43.9 0.7 copy-done.18
  44.5 12.4 %near.1 = f32[16,8,256]{2,1,0:T(8,128)S(1)} custom-call(s32[2]{0:T(128)S(1)} %pad_add_fusion.place, s32[96]{0:T(128)S(1)} %copy-done.18, bf16[16,8,256]{2,1,0:T(8,128)(2,1)S(1)} %copy-done.15, bf16[8,8,256]{2,1,0:T(8,128)(2,1)} %collective-permute-done.2.from_mate, bf16[8,8,256]{2,1,0:T(8,128)(2,1)} %collective-permute-done.3.from_other, ...), custom_call_target="tpu_custom_call" | custom-call | tf_op jit(solution)/shard_map/near/pallas_call | solution.py:307
  57.0 0.7 copy-done.8
  57.7 0.0 copy-start.2
  57.7 1.6 %copy-done.2 = bf16[2,8,64,1024]{3,2,1,0:T(8,128)(2,1)S(1)} copy-done((bf16[2,8,64,1024]{3,2,1,0:T(8,128)(2,1)S(1)}, bf16[2,8,64,1024]{3,2,1,0:T(8,128)(2,1)}, u32[]{:S(2)}) %copy-start.2) | copy-done | bytes 2097176
  59.3 0.9 %copy-done.5 = bf16[2,8,64,64]{3,2,1,0:T(8,128)(2,1)S(1)} copy-done((bf16[2,8,64,64]{3,2,1,0:T(8,128)(2,1)S(1)}, bf16[2,8,64,64]{3,2,1,0:T(8,128)(2,1)}, u32[]{:S(2)}) %copy-start.5) | copy-done | bytes 131096
  60.3 0.9 %copy-done.9 = f32[16,8,256]{2,1,0:T(8,128)S(1)} copy-done((f32[16,8,256]{2,1,0:T(8,128)S(1)}, f32[16,8,256]{2,1,0:T(8,128)}, u32[]{:S(2)}) %copy-start.9) | copy-done | bytes 131096
  61.2 0.9 %copy-done.10 = f32[8,2,8,256]{3,2,1,0:T(8,128)S(1)} copy-done((f32[8,2,8,256]{3,2,1,0:T(8,128)S(1)}, f32[8,2,8,256]{3,2,1,0:T(8,128)}, u32[]{:S(2)}) %copy-start.10) | copy-done | bytes 131096
  62.1 0.9 %copy-done.11 = f32[8,2,8,256]{3,2,1,0:T(8,128)S(1)} copy-done((f32[8,2,8,256]{3,2,1,0:T(8,128)S(1)}, f32[8,2,8,256]{3,2,1,0:T(8,128)}, u32[]{:S(2)}) %copy-start.11) | copy-done | bytes 131096
  63.0 0.7 copy-done.19
  63.6 4.2 %far.1 = f32[8,2,8,256]{3,2,1,0:T(8,128)} custom-call(s32[2]{0:T(128)S(1)} %pad_add_fusion.place, s32[8]{0:T(128)S(1)} %bitcast.27, s32[16,16]{1,0:T(8,128)S(1)} %bitcast.25, s32[8,16]{1,0:T(8,128)S(1)} %bitcast.26, bf16[16,16,1152]{2,1,0:T(8,128)(2,1)S(1)} %all_to_all.10.ring, bf16[16,16,1152]{2,1,0:T(8,128)(2,1)S(1)} %collective-permute-done.ring_mate, ...), custom_call_target="tpu_custom_call" | custom-call | tf_op jit(solution)/shard_map/far/pallas_call | solution.py:328
  (31 shorter events, 0.1 us)
Async XLA Ops:
  0.0 57.7 %copy-start.17 = (s32[1,8,16]{2,1,0:T(8,128)S(1)}, s32[1,8,16]{2,1,0:T(8,128)}, u32[]{:S(2)}) copy-start(s32[1,8,16]{2,1,0:T(8,128)} %param.26) | copy-start | bytes 1540
  0.0 57.7 %copy-start.16 = (s32[2,8,16]{2,1,0:T(8,128)S(1)}, s32[2,8,16]{2,1,0:T(8,128)}, u32[]{:S(2)}) copy-start(s32[2,8,16]{2,1,0:T(8,128)} %param.25) | copy-start | bytes 3076
  0.1 1.0 %copy-start = (bf16[2,8,64,256]{3,2,1,0:T(8,128)(2,1)S(1)}, bf16[2,8,64,256]{3,2,1,0:T(8,128)(2,1)}, u32[]{:S(2)}) copy-start(bf16[2,8,64,256]{3,2,1,0:T(8,128)(2,1)} %param.17) | copy-start | bytes 1572868
  1.1 0.9 %copy-start.4 = (bf16[2,8,64,64]{3,2,1,0:T(8,128)(2,1)S(1)}, bf16[2,8,64,64]{3,2,1,0:T(8,128)(2,1)}, u32[]{:S(2)}) copy-start(bf16[2,8,64,64]{3,2,1,0:T(8,128)(2,1)} %param.18) | copy-start | bytes 393220
  2.1 0.9 %copy-start.6 = (bf16[1,8,64,64]{3,2,1,0:T(8,128)(2,1)S(1)}, bf16[1,8,64,64]{3,2,1,0:T(8,128)(2,1)}, u32[]{:S(2)}) copy-start(bf16[1,8,64,64]{3,2,1,0:T(8,128)(2,1)} %param.19) | copy-start | bytes 196612
  3.0 0.9 %copy-start.12 = (f32[8,2,8,256]{3,2,1,0:T(8,128)S(1)}, f32[8,2,8,256]{3,2,1,0:T(8,128)}, u32[]{:S(2)}) copy-start(f32[8,2,8,256]{3,2,1,0:T(8,128)} %radiosity.1) | copy-start | bytes 393220
  3.9 53.8 %copy-start.1 = (bf16[2,8,64,256]{3,2,1,0:T(8,128)(2,1)S(1)}, bf16[2,8,64,256]{3,2,1,0:T(8,128)(2,1)}, u32[]{:S(2)}) copy-start(bf16[2,8,64,256]{3,2,1,0:T(8,128)(2,1)} %param.17) | copy-start | bytes 1572868
  3.9 53.8 %copy-start.3 = (bf16[1,8,64,1024]{3,2,1,0:T(8,128)(2,1)S(1)}, bf16[1,8,64,1024]{3,2,1,0:T(8,128)(2,1)}, u32[]{:S(2)}) copy-start(bf16[1,8,64,1024]{3,2,1,0:T(8,128)(2,1)} %param.22) | copy-start | bytes 3145732
  3.9 53.8 %copy-start.7 = (bf16[1,8,64,64]{3,2,1,0:T(8,128)(2,1)S(1)}, bf16[1,8,64,64]{3,2,1,0:T(8,128)(2,1)}, u32[]{:S(2)}) copy-start(bf16[1,8,64,64]{3,2,1,0:T(8,128)(2,1)} %param.19) | copy-start | bytes 196612
  3.9 53.8 %copy-start.13 = (bf16[1,1,64,512]{3,2,1,0:T(8,128)(2,1)S(1)}, bf16[1,1,64,512]{3,2,1,0:T(8,128)(2,1)}, u32[]{:S(2)}) copy-start(bf16[1,1,64,512]{3,2,1,0:T(8,128)(2,1)} %param.23) | copy-start | bytes 196612
  5.4 0.6 copy-start.20
  6.0 0.6 copy-start.21
  6.6 19.5 %copy-start.14 = (bf16[16,8,256]{2,1,0:T(8,128)(2,1)}, bf16[16,8,256]{2,1,0:T(8,128)(2,1)S(1)}, u32[]{:S(2)}) copy-start(bf16[16,8,256]{2,1,0:T(8,128)(2,1)S(1)} %get-tuple-element.10.cells) | copy-start | bytes 196612
  26.1 17.0 %collective-permute-start.1 = (bf16[16,16,1152]{2,1,0:T(8,128)(2,1)S(1)}, bf16[16,16,1152]{2,1,0:T(8,128)(2,1)S(1)}, u32[]{:S(2)}, u32[]{:S(2)}) collective-permute-start(bf16[16,16,1152]{2,1,0:T(8,128)(2,1)S(1)} %all_to_all.10.ring), channel_id=1, source_target_pairs={{16,32},{32,16},{48,64},{64,48},{80,96},{96,80},{17,33},{33,17},{4... | collective-permute-start | bytes 1769480 | tf_op jit(solution)/shard_map/ppermute | solution.py:304
  31.1 11.9 %collective-permute-start = (bf16[16,16,1152]{2,1,0:T(8,128)(2,1)S(1)}, bf16[16,16,1152]{2,1,0:T(8,128)(2,1)S(1)}, u32[]{:S(2)}, u32[]{:S(2)}) collective-permute-start(bf16[16,16,1152]{2,1,0:T(8,128)(2,1)S(1)} %all_to_all.10.ring), channel_id=1, source_target_pairs={{0,16},{16,0},{32,48},{48,32},{64,80},{80,64},{96,112},{112,96},{1... | collective-permute-start | bytes 1769480 | tf_op jit(solution)/shard_map/ppermute | solution.py:303
  31.9 25.7 %all-to-all-start.1 = ((bf16[8,16,8,128]{3,2,1,0:T(8,128)(2,1)}), bf16[8,16,8,128]{3,2,1,0:T(8,128)(2,1)}, u32[]{:S(2)}, u32[]{:S(2)}) async-start(bf16[8,16,8,128]{3,2,1,0:T(8,128)(2,1)} %broadcast_in_dim.2), calls=%async_computation.1 | async-start | bytes 524288 | tf_op jit(solution)/shard_map/all_to_all | solution.py:306
  36.6 6.4 %collective-permute-start.2 = (bf16[8,8,256]{2,1,0:T(8,128)(2,1)}, bf16[8,8,256]{2,1,0:T(8,128)(2,1)}, u32[]{:S(2)}, u32[]{:S(2)}) collective-permute-start(bf16[8,8,256]{2,1,0:T(8,128)(2,1)} %copy-done.21), channel_id=1, source_target_pairs={{0,16},{16,0},{32,48},{48,32},{64,80},{80,64},{96,112},{112,96},{1... | collective-permute-start | bytes 98312 | tf_op jit(solution)/shard_map/ppermute | solution.py:300
  36.6 6.4 %collective-permute-start.3 = (bf16[8,8,256]{2,1,0:T(8,128)(2,1)}, bf16[8,8,256]{2,1,0:T(8,128)(2,1)}, u32[]{:S(2)}, u32[]{:S(2)}) collective-permute-start(bf16[8,8,256]{2,1,0:T(8,128)(2,1)} %copy-done.20), channel_id=1, source_target_pairs={{16,32},{32,16},{48,64},{64,48},{80,96},{96,80},{17,33},{33,17},{4... | collective-permute-start | bytes 98312 | tf_op jit(solution)/shard_map/ppermute | solution.py:301
  43.0 0.8 %copy-start.15 = (bf16[16,8,256]{2,1,0:T(8,128)(2,1)S(1)}, bf16[16,8,256]{2,1,0:T(8,128)(2,1)}, u32[]{:S(2)}) copy-start(bf16[16,8,256]{2,1,0:T(8,128)(2,1)} %copy-done.14) | copy-start | bytes 196612
  43.9 0.7 copy-start.18
  57.0 0.7 copy-start.8
  57.7 1.6 %copy-start.2 = (bf16[2,8,64,1024]{3,2,1,0:T(8,128)(2,1)S(1)}, bf16[2,8,64,1024]{3,2,1,0:T(8,128)(2,1)}, u32[]{:S(2)}) copy-start(bf16[2,8,64,1024]{3,2,1,0:T(8,128)(2,1)} %param.21) | copy-start | bytes 6291460
  59.3 0.9 %copy-start.5 = (bf16[2,8,64,64]{3,2,1,0:T(8,128)(2,1)S(1)}, bf16[2,8,64,64]{3,2,1,0:T(8,128)(2,1)}, u32[]{:S(2)}) copy-start(bf16[2,8,64,64]{3,2,1,0:T(8,128)(2,1)} %param.18) | copy-start | bytes 393220
  60.3 0.9 %copy-start.9 = (f32[16,8,256]{2,1,0:T(8,128)S(1)}, f32[16,8,256]{2,1,0:T(8,128)}, u32[]{:S(2)}) copy-start(f32[16,8,256]{2,1,0:T(8,128)} %copy-done.8) | copy-start | bytes 393220
  61.2 0.9 %copy-start.10 = (f32[8,2,8,256]{3,2,1,0:T(8,128)S(1)}, f32[8,2,8,256]{3,2,1,0:T(8,128)}, u32[]{:S(2)}) copy-start(f32[8,2,8,256]{3,2,1,0:T(8,128)} %emission.1) | copy-start | bytes 393220
  62.1 0.9 %copy-start.11 = (f32[8,2,8,256]{3,2,1,0:T(8,128)S(1)}, f32[8,2,8,256]{3,2,1,0:T(8,128)}, u32[]{:S(2)}) copy-start(f32[8,2,8,256]{3,2,1,0:T(8,128)} %reflect.1) | copy-start | bytes 393220
  63.0 0.7 copy-start.19

commit v2 on v1

v2 whole, which is shorter than its diff:
```python
import jax
import jax.numpy as jnp
from jax import lax
from jax.experimental import pallas as pl
from jax.experimental.pallas import tpu as pltpu
from jax.sharding import PartitionSpec as P

F32 = jnp.float32
BF16 = jnp.bfloat16
NT = (((1,), (1,)), ((), ()))
NN = (((1,), (0,)), ((), ()))
LANES = 128
RANK = 64
WIDE = 1152
VMEM = pl.BlockSpec(memory_space=pltpu.VMEM)
SMEM = pl.BlockSpec(memory_space=pltpu.SMEM)
HBM = pl.BlockSpec(memory_space=pltpu.HBM)


def dot(left, right, dims):
    return lax.dot_general(left, right, dims, preferred_element_type=F32)


def far(x):
    return pltpu.with_memory_space_constraint(x, pltpu.HBM)


def limit(mib):
    return pltpu.CompilerParams(vmem_limit_bytes=mib * 1024 * 1024)


def row_of(shape, count):
    return lax.broadcasted_iota(jnp.int32, shape, 0) % count


def own_blocks(products, count):
    shape = (products.shape[0], LANES)
    mine = row_of(shape, count) - lax.broadcasted_iota(jnp.int32, shape, 1) // RANK
    total = jnp.zeros(shape, F32)
    for tile in range(count // 2):
        total += jnp.where(mine == 2 * tile, products[:, tile * LANES : (tile + 1) * LANES], 0.0)
    return total + pltpu.roll(total, RANK, 1)


def side_by_side(twice, count):
    low = lax.broadcasted_iota(jnp.int32, (count, LANES), 1) < RANK
    return jnp.concatenate(
        [
            jnp.where(low, twice[b * count : (b + 1) * count], twice[(b + 1) * count : (b + 2) * count])
            for b in range(0, twice.shape[0] // count, 2)
        ],
        axis=1,
    )


def started(copies, sems, at=0):
    made = []
    for number, (source, target) in enumerate(copies):
        made.append(pltpu.make_async_copy(source, target, sems.at[at + number]))
        made[-1].start()
    return made


def coefficients_kernel(
    place,
    far_radiosity,
    far_basis,
    far_up_leaf,
    far_up_pair,
    sent,
    cells,
    radiosity,
    basis,
    up_leaf,
    up_pair,
    sems,
):
    copies = started(
        [
            (far_radiosity, radiosity),
            (far_basis, basis),
            (far_up_leaf, up_leaf),
            (far_up_pair, up_pair),
        ],
        sems,
    )
    copies[0].wait()
    column = place[1]
    bands, rows, cols, leaf = radiosity.shape
    leaves = rows * cols
    for g in range(rows):
        turned = jnp.swapaxes(radiosity[:, g], 0, 1)
        cells[g * cols : (g + 1) * cols] = turned.astype(BF16)
    shaded = radiosity[...].reshape(bands * leaves, leaf).astype(BF16)
    copies[1].wait()
    leaf_twice = own_blocks(dot(shaded, basis[...], NT), leaves)
    leaf_coef = leaf_twice[:, :RANK].astype(BF16)
    copies[2].wait()
    parts = jnp.zeros((bands * leaves, RANK), F32)
    which = row_of(parts.shape, leaves)
    for at in range(leaves):
        parts += jnp.where(which == at, dot(leaf_coef, up_leaf[at], NN), 0.0)
    pair = jnp.sum(parts.reshape(bands, rows, cols, RANK), axis=1).reshape(bands * cols, RANK)
    pair_coef = pair.astype(BF16)
    copies[3].wait()
    parts = jnp.zeros((bands * cols, RANK), F32)
    which = row_of(parts.shape, cols)
    for at in range(cols):
        parts += jnp.where(which == at, dot(pair_coef, up_pair[at], NN), 0.0)
    top = jnp.sum(parts.reshape(bands, cols, RANK), axis=1)
    top_twice = jnp.concatenate([top, top], axis=1)
    pair_twice = jnp.concatenate([pair, pair], axis=1)

    def edge(col):
        return jnp.concatenate(
            [radiosity[:, g, col, :] for g in range(rows)], axis=1
        )

    leaf_part = side_by_side(leaf_twice, leaves)
    pair_part = side_by_side(pair_twice, cols)
    top_part = jnp.concatenate([top_twice, jnp.zeros_like(top_twice)], axis=0)

    def block(col):
        return jnp.concatenate(
            [leaf_part, jnp.concatenate([pair_part, edge(col)], axis=0), top_part], axis=1
        ).astype(BF16)

    first = block(0)
    for to in range(sent.shape[0]):
        sent[to] = first
    sent[(column + 1) % sent.shape[0]] = block(cols - 1)


def packing_kernel(place, ring, cells, packed, tops):
    column = place[1]
    around, leaves = ring.shape[:2]
    cols = leaves // 2
    for at in range(around):
        packed[at * leaves : (at + 1) * leaves] = ring[at, :, :512]
        tops[:, at] = jnp.broadcast_to(ring[at, :, 1024:][None, :8], (tops.shape[0], 8, LANES))
    for at in range(0, around, 2):
        start = around * leaves + at * cols
        both = [ring[at + k, :, 512:1024].astype(F32)[:cols] for k in range(2)]
        packed[start : start + 2 * cols] = jnp.concatenate(both, axis=0).astype(BF16)
    start = around * (leaves + cols)
    for at in range(0, leaves, 4):
        four = [cells[at + k].astype(F32) for k in range(4)]
        two = [jnp.concatenate(four[:2], axis=1), jnp.concatenate(four[2:], axis=1)]
        packed[start + at * 4 : start + at * 4 + 16] = jnp.concatenate(two, axis=0).astype(BF16)
    start += leaves * 4
    sides = [(column + around - 1) % around, (column + 1) % around]
    both = [ring[at, :, 512:1024].astype(F32)[8:] for at in sides]
    packed[start : start + 16] = jnp.concatenate(both, axis=0).astype(BF16)


def chosen(tables, start, size, tier, inner, count):
    picks = inner.shape[1]
    result = jnp.zeros((count * picks, 512), F32)
    at = lax.broadcasted_iota(jnp.int32, (count, size), 1)
    for number, table in enumerate(tables):
        slots = jnp.where(tier == number, inner, -1)
        choose = jnp.concatenate(
            [(at == slots[:, k : k + 1]).astype(F32) for k in range(picks)], axis=0
        ).astype(BF16)
        result += dot(choose, table[start : start + size], NN)
    low = lax.broadcasted_iota(jnp.int32, (count, LANES), 1) < RANK
    bands = []
    for n in range(4):
        even, odd = [], []
        for k in range(0, picks, 2):
            one = result[k * count : (k + 1) * count, n * LANES : (n + 1) * LANES]
            two = result[(k + 1) * count : (k + 2) * count, n * LANES : (n + 1) * LANES]
            even.append(jnp.where(low, one, pltpu.roll(two, RANK, 1)))
            odd.append(jnp.where(low, pltpu.roll(one, RANK, 1), two))
        bands += [jnp.concatenate(even, axis=1), jnp.concatenate(odd, axis=1)]
    return jnp.concatenate(bands, axis=0).astype(BF16)


def field_kernel(
    place,
    own,
    from_mate,
    from_other,
    tops,
    far_listed,
    far_names_leaf,
    far_names_pair,
    far_names_top,
    far_blocks,
    far_couple_leaf,
    far_couple_pair,
    far_couple_top,
    far_basis,
    far_up_leaf,
    far_up_pair,
    far_emission,
    far_reflect,
    out,
    window,
    listed,
    names_leaf,
    names_pair,
    names_top,
    blocks,
    couple_leaf,
    couple_pair,
    couple_top,
    basis,
    up_leaf,
    up_pair,
    emission,
    reflect,
    gathered,
    sems,
):
    leaves, count = blocks.shape[:2]
    lists = started(
        [
            (far_names_leaf, names_leaf),
            (far_names_pair, names_pair),
            (far_names_top, names_top),
            (far_listed, listed),
        ],
        sems,
    )
    block_copies = started(
        [(far_blocks.at[at], blocks.at[at]) for at in range(leaves)], sems, len(lists)
    )
    couple_copies = started(
        [(far_couple_leaf, couple_leaf), (far_couple_pair, couple_pair)], sems, len(lists) + leaves
    )
    later = started(
        [
            (far_couple_top, couple_top),
            (far_basis, basis),
            (far_up_leaf, up_leaf),
            (far_up_pair, up_pair),
            (far_emission, emission),
            (far_reflect, reflect),
        ],
        sems,
        len(lists) + leaves + 2,
    )
    section, column = place[0], place[1]
    bands, rows, cols, leaf = out.shape
    around = (own.shape[0] - 16 - leaves * 4) // (leaves + cols)
    broad = cols + 2
    width_all = around * cols
    odd = section % 2
    cells_at = around * (leaves + cols)
    sides_at = cells_at + leaves * 4

    def seen_row(source, g, at):
        for p in range(0, cols, 4):
            start = cells_at + (g * cols + p) * 4
            four = source[start : start + 16].astype(F32)
            for k in range(4):
                lanes = slice(k % 2 * leaf, (k % 2 + 1) * leaf)
                window[at * broad + 1 + p + k] = four[k // 2 * 8 : (k // 2 + 1) * 8, lanes]
        two = source[sides_at : sides_at + 16].astype(F32)[:, g * leaf : (g + 1) * leaf]
        window[at * broad] = two[:8]
        window[(at + 1) * broad - 1] = two[8:]

    for g in range(rows):
        seen_row(own, g, g + 1)

    @pl.when(odd == 0)
    def _():
        seen_row(from_other, rows - 1, 0)
        seen_row(from_mate, 0, rows + 1)

    @pl.when(odd == 1)
    def _():
        seen_row(from_mate, rows - 1, 0)
        seen_row(from_other, 0, rows + 1)

    for copy in lists:
        copy.wait()
    mate = section + 1 - 2 * odd
    tables = (own, from_mate, from_other)

    def tier_of(source):
        return jnp.where(source == section, 0, jnp.where(source == mate, 1, 2))

    names = names_leaf[...]
    turn = names % width_all
    height = names // width_all
    leaf_pick = chosen(
        tables,
        0,
        around * leaves,
        tier_of(height // rows),
        turn // cols * leaves + height % rows * cols + turn % cols,
        leaves,
    )
    names = names_pair[...]
    turn = names % width_all
    pair_pick = chosen(
        tables,
        around * leaves,
        around * cols,
        tier_of(names // width_all),
        turn,
        cols,
    )
    picks = names_top.shape[1]
    square = (picks, picks)
    names = jnp.broadcast_to(names_top[...], square)
    diagonal = lax.broadcasted_iota(jnp.int32, square, 0) == lax.broadcasted_iota(jnp.int32, square, 1)
    names = jnp.sum(jnp.where(diagonal, names, 0), axis=1, keepdims=True)
    at = lax.broadcasted_iota(jnp.int32, (picks, tops.shape[0]), 1)
    choose_top = jnp.concatenate(
        [(at == names * bands + b).astype(F32) for b in range(bands)], axis=0
    ).astype(BF16)

    for at in range(leaves):
        seen = []
        for n in range(count):
            name = listed[n, at // cols, at % cols]
            up = name // width_all - rows * section + 1
            turn = (name % width_all + width_all + 1 - cols * column) % width_all
            seen.append(window[up * broad + turn].astype(BF16))
        block_copies[at].wait()
        total = jnp.zeros((bands, leaf), F32)
        turned = jnp.zeros((leaf, bands), F32)
        for n in range(count):
            if n % 2 == 0:
                total += dot(seen[n], blocks[at, n], NT)
            else:
                turned += dot(blocks[at, n], seen[n], NT)
        gathered[at] = total + turned.T
    couple_copies[0].wait()
    leaf_field = own_blocks(dot(leaf_pick, couple_leaf[...], NT), leaves)[:, :RANK]
    couple_copies[1].wait()
    pair_field = own_blocks(dot(pair_pick, couple_pair[...], NT), cols)[:, :RANK]
    for copy in later:
        copy.wait()
    top_pick = dot(choose_top, tops[...], NN)
    top_pick = jnp.concatenate([top_pick] * (picks // 2), axis=1)
    kept = row_of(top_pick.shape, picks) == lax.broadcasted_iota(jnp.int32, top_pick.shape, 1) // RANK
    top_pick = jnp.where(kept, top_pick, 0.0).astype(BF16)
    top_field = dot(top_pick, couple_top[...], NT)
    top_field = jnp.sum(top_field.reshape(bands, picks, RANK), axis=1)
    spread = jnp.broadcast_to(top_field[:, None, :], (bands, cols, RANK))
    spread = spread.reshape(bands * cols, RANK).astype(BF16)
    pair_total = pair_field + own_blocks(dot(spread, up_pair[...], NT), cols)[:, :RANK]
    spread = jnp.broadcast_to(
        pair_total.reshape(bands, 1, cols, RANK), (bands, rows, cols, RANK)
    )
    spread = spread.reshape(bands * leaves, RANK).astype(BF16)
    leaf_total = leaf_field + own_blocks(dot(spread, up_leaf[...], NT), leaves)[:, :RANK]
    leaf_total = leaf_total.astype(BF16)
    far_part = jnp.zeros((bands * leaves, leaf), F32)
    which = row_of(far_part.shape, leaves)
    for at in range(leaves):
        far_part += jnp.where(which == at, dot(leaf_total, basis[at], NN), 0.0)
    far_part = far_part.reshape(out.shape)
    for g in range(rows):
        near_part = jnp.swapaxes(gathered[g * cols : (g + 1) * cols], 0, 1)
        out[:, g] = emission[:, g] + reflect[:, g] * (near_part + far_part[:, g])


def body(
    radiosity,
    emission,
    reflect,
    basis,
    up_leaf,
    upward_pair_transfer,
    near_block,
    couple_leaf,
    couple_pair,
    couple_top,
    near_list,
    far_leaf,
    far_pair,
    far_top,
):
    around = lax.axis_size("perim")
    tall = lax.axis_size("section")
    bands, rows, cols, leaf = radiosity.shape
    leaves = rows * cols
    place = jnp.stack([lax.axis_index("section"), lax.axis_index("perim")]).astype(jnp.int32)
    mates = [(s, s ^ 1) for s in range(tall)]
    others = [(s, s + 1 if s % 2 else s - 1) for s in range(1, tall - 1)]
    sems = pltpu.SemaphoreType.DMA
    basis_wide = far(basis.reshape(leaves * RANK, leaf))
    basis = far(basis.reshape(leaves, RANK, leaf))
    up_leaf_wide = far(up_leaf.reshape(leaves * RANK, RANK))
    up_leaf = far(up_leaf.reshape(leaves, RANK, RANK))
    up_pair_wide = far(upward_pair_transfer.reshape(cols * RANK, RANK))
    up_pair = far(upward_pair_transfer[0])
    sent, cells = pl.pallas_call(
        coefficients_kernel,
        out_shape=[
            jax.ShapeDtypeStruct((around, 16, WIDE), BF16),
            jax.ShapeDtypeStruct((leaves, bands, leaf), BF16),
        ],
        in_specs=[SMEM] + [HBM] * 4,
        out_specs=[VMEM] * 2,
        scratch_shapes=[
            pltpu.VMEM(radiosity.shape, F32),
            pltpu.VMEM(basis_wide.shape, BF16),
            pltpu.VMEM(up_leaf.shape, BF16),
            pltpu.VMEM(up_pair.shape, BF16),
            sems((4,)),
        ],
        compiler_params=limit(12),
        name="coefficients",
    )(place, far(radiosity), basis_wide, up_leaf, up_pair)
    ring = lax.all_to_all(sent, "perim", 0, 0)
    packed, tops = pl.pallas_call(
        packing_kernel,
        out_shape=[
            jax.ShapeDtypeStruct((around * (leaves + cols) + leaves * 4 + 16, 512), BF16),
            jax.ShapeDtypeStruct((tall, around, bands, LANES), BF16),
        ],
        in_specs=[SMEM, VMEM, VMEM],
        out_specs=[VMEM] * 2,
        compiler_params=limit(8),
        name="packing",
    )(place, ring, cells)
    from_mate = lax.ppermute(packed, "section", mates)
    from_other = lax.ppermute(packed, "section", others)
    tops = lax.all_to_all(tops, "section", 0, 0)
    blocks = near_block.reshape((leaves,) + near_block.shape[2:])
    couple_leaf = couple_leaf.reshape(leaves * RANK, -1)
    couple_pair = couple_pair.reshape(cols * RANK, -1)
    couple_top = couple_top[0, 0]
    listed = near_list.transpose(2, 0, 1)
    names_leaf = far_leaf.reshape(leaves, -1)
    names_pair = far_pair.reshape(cols, -1)
    names_top = far_top.reshape(1, -1)
    passed = [couple_top, basis, up_leaf_wide, up_pair_wide, emission, reflect]
    held = [names_leaf, names_pair, names_top, blocks, couple_leaf, couple_pair] + passed
    return pl.pallas_call(
        field_kernel,
        out_shape=jax.ShapeDtypeStruct(radiosity.shape, F32),
        in_specs=[SMEM] + [VMEM] * 4 + [HBM] * 13,
        out_specs=VMEM,
        scratch_shapes=[
            pltpu.VMEM(((rows + 2) * (cols + 2), bands, leaf), F32),
            pltpu.SMEM(listed.shape, jnp.int32),
        ]
        + [pltpu.VMEM(x.shape, x.dtype) for x in held]
        + [pltpu.VMEM((leaves, bands, leaf), F32), sems((leaves + 12,))],
        compiler_params=limit(32),
        name="fields",
    )(
        place,
        packed,
        from_mate,
        from_other,
        tops.reshape(tall * around * bands, LANES),
        far(listed),
        *map(far, held),
    )


def solution(mesh):
    cells = P(None, "section", "perim", None)
    four = P("section", "perim", None, None)
    lists = P("section", "perim", None)
    return jax.shard_map(
        body,
        mesh=mesh,
        in_specs=(cells,) * 3
        + (four,) * 3
        + (P("section", "perim", None, None, None),)
        + (four,) * 3
        + (lists,) * 4,
        out_specs=cells,
        check_vma=False,
    )
```

time: 68.7 us -> 50.9 us (0.74)
  local copies, waits for them, and re-layouts: 16.6 us -> 0 us
  blocking collectives: 19.5 us -> 30.5 us
  starting transfers between devices: 13.5 us -> 5.13 us
  Pallas kernels: 18.1 us -> 14.9 us
    unnamed x45 -> x0, local copies, waits for them, and re-layouts: 14.5 us -> none
    all_to_all x0 -> x1, blocking collectives: none -> 11 us  [body(): tops = lax.all_to_all(tops, 'section', 0, 0)]
    all_to_all x1 -> x0, starting transfers between devices: 4.66 us -> none  [body(): lax.all_to_all(jnp.broadcast_to(tops[None], (tall,) + tops.shape), 'secti...]
    pallas_call x2, Pallas kernels: 16.7 us -> 12.3 us  [the longest x1 11.7 us: body(): pl.pallas_call(field_kernel, out_shape=jax.ShapeDtypeStruct(radiosity.sha...]
    ppermute x4 -> x2, starting transfers between devices: 8.8 us -> 5.13 us  [the longest x1 5.05 us: body(): from_other = lax.ppermute(packed, 'section', others)]
    reshape x1 -> x0, local copies, waits for them, and re-layouts: 1.36 us -> none  [body(): near_list.reshape(-1)]
    pallas_call x1, Pallas kernels: 1.46 us -> 2.62 us  [body(): pl.pallas_call(coefficients_kernel, out_shape=[jax.ShapeDtypeStruct((arou...]
    broadcast_in_dim x1 -> x0, local copies, waits for them, and re-layouts: 0.73 us -> none  [body(): jnp.broadcast_to(tops[None], (tall,) + tops.shape)]
  transfers between devices with their start and end apart: 5 -> 2, of which waited for: 0 -> 0; matrix products, arithmetic and copies ran while one was open for 5% -> 0% of each run, Pallas kernels for 18% -> 0%
where the time goes in v2:
time: 50.9 us; the launch traced here: 50.6 us
  blocking collectives  30.5 us (60%)
  Pallas kernels  14.9 us (29%)
  starting transfers between devices  5.13 us (10%)
    all_to_all x1, blocking collectives, body(): ring = lax.all_to_all(sent, 'perim', 0, 0)  19.5 us
    pallas_call x1, Pallas kernels, body(): pl.pallas_call(field_kernel, out_shape=jax.ShapeDtypeStruct(radiosity.sha...  11.7 us
    all_to_all x1, blocking collectives, body(): tops = lax.all_to_all(tops, 'section', 0, 0)  11 us
    ppermute x1, starting transfers between devices, body(): from_other = lax.ppermute(packed, 'section', others)  5.05 us
    pallas_call x1, Pallas kernels, body(): pl.pallas_call(coefficients_kernel, out_shape=[jax.ShapeDtypeStruct((arou...  2.62 us
  transfers between devices with their start and end apart: 2, of which 0 were waited for; matrix products, arithmetic and copies ran while one was open for 0% of the time, Pallas kernels for 0%

profile of v2, /device:TPU:1, one launch (start us, length us, event | category | flops | bytes accessed | tf_op | source)
XLA Modules:
  0.0 50.6 jit_solution(4567685949358045024)
XLA Ops:
  0.0 0.1 pad_add_fusion.place
  0.1 2.6 %coefficients.1 = (bf16[16,16,1152]{2,1,0:T(8,128)(2,1)S(1)}, bf16[16,8,256]{2,1,0:T(8,128)(2,1)S(1)}) custom-call(s32[2]{0:T(128)S(1)} %pad_add_fusion.place, f32[8,2,8,256]{3,2,1,0:T(8,128)} %far_radiosity.1, bf16[1024,256]{1,0:T(8,128)(2,1)} %bitcast.20, bf16[16,64,64]{2,1,0:T(8,128)(2,1)} %bitcast.22, bf16[8,64,64]{2,1,0:T(8,128)(2,1)} %bitcast.25), custom_call_target="tpu_custom_call" | custom-call | tf_op jit(solution)/shard_map/coefficients/pallas_call | solution.py:393
  2.7 19.5 %all_to_all.10.ring = bf16[16,16,1152]{2,1,0:T(8,128)(2,1)S(1)} all-to-all(bf16[16,16,1152]{2,1,0:T(8,128)(2,1)S(1)} %get-tuple-element.9), channel_id=1, replica_groups=mesh['section'=8,'perim'=16] {'perim'}, dimensions={0} | all-to-all | bytes 1179648 | tf_op jit(solution)/shard_map/all_to_all | solution.py:411
  22.2 0.6 %packing.1 = (bf16[464,512]{1,0:T(8,128)(2,1)S(1)}, bf16[8,16,8,128]{3,2,1,0:T(8,128)(2,1)S(1)}) custom-call(s32[2]{0:T(128)S(1)} %pad_add_fusion.place, bf16[16,16,1152]{2,1,0:T(8,128)(2,1)S(1)} %all_to_all.10.ring, bf16[16,8,256]{2,1,0:T(8,128)(2,1)S(1)} %get-tuple-element.10.cells), custom_call_target="tpu_custom_call" | custom-call | tf_op jit(solution)/shard_map/packing/pallas_call | solution.py:412
  22.8 5.0 %collective-permute-start.1 = (bf16[464,512]{1,0:T(8,128)(2,1)S(1)}, bf16[464,512]{1,0:T(8,128)(2,1)S(1)}, u32[]{:S(2)}, u32[]{:S(2)}) collective-permute-start(bf16[464,512]{1,0:T(8,128)(2,1)S(1)} %get-tuple-element.11.own), channel_id=1, source_target_pairs={{16,32},{32,16},{48,64},{64,48},{80,96},{96,80},{17,33},{33,17},{4... | collective-permute-start | bytes 1425416 | tf_op jit(solution)/shard_map/ppermute | solution.py:424
  27.9 0.1 collective-permute-start
  28.0 11.0 %all_to_all.11 = bf16[8,16,8,128]{3,2,1,0:T(8,128)(2,1)S(1)} all-to-all(bf16[8,16,8,128]{3,2,1,0:T(8,128)(2,1)S(1)} %get-tuple-element.12), channel_id=1, replica_groups=mesh['section'=8,'perim'=16] {'section'}, dimensions={0} | all-to-all | bytes 524288 | tf_op jit(solution)/shard_map/all_to_all | solution.py:425
  39.0 0.0 collective-permute-done.1.from_other
  39.0 0.0 collective-permute-done.from_mate
  39.0 11.7 %fields.1 = f32[8,2,8,256]{3,2,1,0:T(8,128)} custom-call(s32[2]{0:T(128)S(1)} %pad_add_fusion.place, bf16[464,512]{1,0:T(8,128)(2,1)S(1)} %get-tuple-element.11.own, bf16[464,512]{1,0:T(8,128)(2,1)S(1)} %collective-permute-done.from_mate, bf16[464,512]{1,0:T(8,128)(2,1)S(1)} %collective-permute-done.1.from_other, bf16[1024,128]{1,0:T(8,128)(2,1)S(1)} %bitcast.17, ...), custom_call_target="tpu_custom_call" | custom-call | tf_op jit(solution)/shard_map/fields/pallas_call | solution.py:436
Async XLA Ops:
  22.8 16.2 %collective-permute-start.1 = (bf16[464,512]{1,0:T(8,128)(2,1)S(1)}, bf16[464,512]{1,0:T(8,128)(2,1)S(1)}, u32[]{:S(2)}, u32[]{:S(2)}) collective-permute-start(bf16[464,512]{1,0:T(8,128)(2,1)S(1)} %get-tuple-element.11.own), channel_id=1, source_target_pairs={{16,32},{32,16},{48,64},{64,48},{80,96},{96,80},{17,33},{33,17},{4... | collective-permute-start | bytes 1425416 | tf_op jit(solution)/shard_map/ppermute | solution.py:424
  27.9 11.1 %collective-permute-start = (bf16[464,512]{1,0:T(8,128)(2,1)S(1)}, bf16[464,512]{1,0:T(8,128)(2,1)S(1)}, u32[]{:S(2)}, u32[]{:S(2)}) collective-permute-start(bf16[464,512]{1,0:T(8,128)(2,1)S(1)} %get-tuple-element.11.own), channel_id=1, source_target_pairs={{0,16},{16,0},{32,48},{48,32},{64,80},{80,64},{96,112},{112,96},{1... | collective-permute-start | bytes 1425416 | tf_op jit(solution)/shard_map/ppermute | solution.py:423

commit v3 on v2

--- a/solution.py
+++ b/solution.py
@@ -15,6 +15,8 @@
 VMEM = pl.BlockSpec(memory_space=pltpu.VMEM)
 SMEM = pl.BlockSpec(memory_space=pltpu.SMEM)
 HBM = pl.BlockSpec(memory_space=pltpu.HBM)
+ANY = pl.BlockSpec(memory_space=pl.ANY)
+AT_ONCE = 8
 
 
 def dot(left, right, dims):
@@ -73,6 +75,7 @@
     basis,
     up_leaf,
     up_pair,
+    block,
     sems,
 ):
     copies = started(
@@ -120,24 +123,25 @@
     pair_part = side_by_side(pair_twice, cols)
     top_part = jnp.concatenate([top_twice, jnp.zeros_like(top_twice)], axis=0)
 
-    def block(col):
-        return jnp.concatenate(
+    for right, col in enumerate((0, cols - 1)):
+        block[right] = jnp.concatenate(
             [leaf_part, jnp.concatenate([pair_part, edge(col)], axis=0), top_part], axis=1
         ).astype(BF16)
-
-    first = block(0)
-    for to in range(sent.shape[0]):
-        sent[to] = first
-    sent[(column + 1) % sent.shape[0]] = block(cols - 1)
-
-
-def packing_kernel(place, ring, cells, packed, tops):
+    around = sent.shape[0]
+    to_right = (column + 1) % around
+    copies = started(
+        [(block.at[jnp.where(to_right == to, 1, 0)], sent.at[to]) for to in range(around)], sems, 4
+    )
+    for copy in copies:
+        copy.wait()
+
+
+def packing_kernel(place, ring, cells, local_part, packed):
     column = place[1]
     around, leaves = ring.shape[:2]
     cols = leaves // 2
     for at in range(around):
         packed[at * leaves : (at + 1) * leaves] = ring[at, :, :512]
-        tops[:, at] = jnp.broadcast_to(ring[at, :, 1024:][None, :8], (tops.shape[0], 8, LANES))
     for at in range(0, around, 2):
         start = around * leaves + at * cols
         both = [ring[at + k, :, 512:1024].astype(F32)[:cols] for k in range(2)]
@@ -153,16 +157,159 @@
     packed[start : start + 16] = jnp.concatenate(both, axis=0).astype(BF16)
 
 
-def chosen(tables, start, size, tier, inner, count):
-    picks = inner.shape[1]
+def tops_kernel(ring, tops, row_tops, sems):
+    row_tops[...] = ring[:, :8, 1024:]
+    for copy in started([(row_tops, tops.at[to]) for to in range(tops.shape[0])], sems):
+        copy.wait()
+
+
+def one_hot(tier, inner, size):
+    count, picks = inner.shape
+    slots = tier * size + inner
+    at = lax.broadcasted_iota(jnp.int32, (count, 3 * size), 1)
+    return jnp.concatenate(
+        [(at == slots[:, k : k + 1]).astype(F32) for k in range(picks)], axis=0
+    ).astype(BF16)
+
+
+def near_products(seen, blocks):
+    total = jnp.zeros(seen[0].shape, F32)
+    turned = jnp.zeros(seen[0].shape[::-1], F32)
+    for n, cell in enumerate(seen):
+        if n % 2 == 0:
+            total += dot(cell, blocks[n], NT)
+        else:
+            turned += dot(blocks[n], cell, NT)
+    return total + turned.T
+
+
+def split_name(name, width_all):
+    if width_all & (width_all - 1):
+        return name // width_all, name % width_all
+    return name >> (width_all.bit_length() - 1), name & (width_all - 1)
+
+
+def position(name, section, column, rows, cols, width_all):
+    row = split_name(name, width_all)[0]
+    turn = split_name(name + (width_all + 1 - cols * column), width_all)[1]
+    return row - (rows * section - 1), turn
+
+
+def local_kernel(
+    place,
+    cells,
+    far_listed,
+    far_names_leaf,
+    far_names_pair,
+    far_names_top,
+    far_blocks,
+    far_choose_leaf,
+    far_choose_pair,
+    far_choose_top,
+    far_local_part,
+    far_todo,
+    window,
+    listed,
+    todo,
+    names_leaf,
+    names_pair,
+    names_top,
+    blocks,
+    choose_leaf,
+    choose_pair,
+    choose_top,
+    local_part,
+    sems,
+):
+    leaves, count = blocks.shape[:2]
+    lists = started(
+        [
+            (far_names_leaf, names_leaf),
+            (far_names_pair, names_pair),
+            (far_names_top, names_top),
+            (far_listed, listed),
+        ],
+        sems,
+    )
+    block_copies = started(
+        [(far_blocks.at[at], blocks.at[at]) for at in range(leaves)], sems, len(lists)
+    )
+    for copy in lists:
+        copy.wait()
+    section = place[0]
+    cols = names_pair.shape[0]
+    rows = leaves // cols
+    width_all = choose_pair.shape[1] // 3
+    mate = section + 1 - 2 * (section % 2)
+
+    def tier_of(source):
+        return jnp.where(source == section, 0, jnp.where(source == mate, 1, 2))
+
+    names = names_leaf[...]
+    height, turn = split_name(names, width_all)
+    source, height = split_name(height, rows)
+    device, turn = split_name(turn, cols)
+    choose_leaf[...] = one_hot(
+        tier_of(source), device * leaves + height * cols + turn, width_all * rows
+    )
+    height, turn = split_name(names_pair[...], width_all)
+    choose_pair[...] = one_hot(tier_of(height), turn, width_all)
+    picks = names_top.shape[1]
+    bands = choose_top.shape[0] // picks
+    square = (picks, picks)
+    names = jnp.broadcast_to(names_top[...], square)
+    diagonal = lax.broadcasted_iota(jnp.int32, square, 0) == lax.broadcasted_iota(jnp.int32, square, 1)
+    names = jnp.sum(jnp.where(diagonal, names, 0), axis=1, keepdims=True)
+    at = lax.broadcasted_iota(jnp.int32, (picks, choose_top.shape[1]), 1)
+    choose_top[...] = jnp.concatenate(
+        [(at == names * bands + b).astype(F32) for b in range(bands)], axis=0
+    ).astype(BF16)
+    results = started(
+        [
+            (choose_leaf, far_choose_leaf),
+            (choose_pair, far_choose_pair),
+            (choose_top, far_choose_top),
+        ],
+        sems,
+        len(lists) + leaves,
+    )
+    broad = cols + 2
+    window[...] = jnp.zeros_like(window)
+    for g in range(rows):
+        start = (g + 1) * broad + 1
+        window[start : start + cols] = cells[g * cols : (g + 1) * cols].astype(F32)
+    found = jnp.int32(0)
+    for at in range(leaves):
+        seen = []
+        for n in range(count):
+            name = listed[n, at // cols, at % cols]
+            up, turn = position(name, section, place[1], rows, cols, width_all)
+            where = up * broad + turn
+            seen.append(window[where].astype(BF16))
+            if n > 0:
+                todo[0, found] = (where << 12) + (at << 4) + n
+                inside = (up >= 1) & (up <= rows) & (turn >= 1) & (turn <= cols)
+                found = found + jnp.where(inside, 0, 1)
+        if at % 2 == 0:
+            for copy in block_copies[at : at + 2]:
+                copy.wait()
+        local_part[at] = near_products(seen, blocks.at[at])
+    todo[0, todo.shape[1] - 1] = found
+    results += started(
+        [(local_part, far_local_part), (todo, far_todo)], sems, len(lists) + leaves + 3
+    )
+    for copy in results:
+        copy.wait()
+
+
+def chosen(choose, tables, start, count):
+    size = choose.shape[1] // 3
+    picks = choose.shape[0] // count
     result = jnp.zeros((count * picks, 512), F32)
-    at = lax.broadcasted_iota(jnp.int32, (count, size), 1)
     for number, table in enumerate(tables):
-        slots = jnp.where(tier == number, inner, -1)
-        choose = jnp.concatenate(
-            [(at == slots[:, k : k + 1]).astype(F32) for k in range(picks)], axis=0
-        ).astype(BF16)
-        result += dot(choose, table[start : start + size], NN)
+        result += dot(
+            choose[:, number * size : (number + 1) * size], table[start : start + size], NN
+        )
     low = lax.broadcasted_iota(jnp.int32, (count, LANES), 1) < RANK
     bands = []
     for n in range(4):
@@ -181,68 +328,49 @@
     own,
     from_mate,
     from_other,
-    tops,
-    far_listed,
-    far_names_leaf,
-    far_names_pair,
-    far_names_top,
-    far_blocks,
+    far_todo,
+    far_choose_leaf,
+    far_choose_pair,
+    far_choose_top,
+    far_gathered,
+    far_emission,
+    far_reflect,
     far_couple_leaf,
     far_couple_pair,
-    far_couple_top,
-    far_basis,
-    far_up_leaf,
-    far_up_pair,
-    far_emission,
-    far_reflect,
-    out,
+    far_blocks,
+    parts,
+    fields,
+    choose_top,
     window,
-    listed,
-    names_leaf,
-    names_pair,
-    names_top,
-    blocks,
+    todo,
+    choose_leaf,
+    choose_pair,
+    gathered,
+    emission,
+    reflect,
     couple_leaf,
     couple_pair,
-    couple_top,
-    basis,
-    up_leaf,
-    up_pair,
-    emission,
-    reflect,
-    gathered,
+    blocks,
     sems,
+    block_sems,
 ):
-    leaves, count = blocks.shape[:2]
-    lists = started(
+    copies = started(
         [
-            (far_names_leaf, names_leaf),
-            (far_names_pair, names_pair),
-            (far_names_top, names_top),
-            (far_listed, listed),
-        ],
-        sems,
-    )
-    block_copies = started(
-        [(far_blocks.at[at], blocks.at[at]) for at in range(leaves)], sems, len(lists)
-    )
-    couple_copies = started(
-        [(far_couple_leaf, couple_leaf), (far_couple_pair, couple_pair)], sems, len(lists) + leaves
-    )
-    later = started(
-        [
-            (far_couple_top, couple_top),
-            (far_basis, basis),
-            (far_up_leaf, up_leaf),
-            (far_up_pair, up_pair),
+            (far_todo, todo),
+            (far_choose_leaf, choose_leaf),
+            (far_choose_pair, choose_pair),
+            (far_couple_leaf, couple_leaf),
+            (far_couple_pair, couple_pair),
+            (far_gathered, gathered),
+            (far_choose_top, choose_top),
             (far_emission, emission),
             (far_reflect, reflect),
         ],
         sems,
-        len(lists) + leaves + 2,
-    )
+    )
+    leaves = gathered.shape[0]
     section, column = place[0], place[1]
-    bands, rows, cols, leaf = out.shape
+    bands, rows, cols, leaf = emission.shape
     around = (own.shape[0] - 16 - leaves * 4) // (leaves + cols)
     broad = cols + 2
     width_all = around * cols
@@ -274,68 +402,72 @@
         seen_row(from_mate, rows - 1, 0)
         seen_row(from_other, 0, rows + 1)
 
-    for copy in lists:
+    zero_cell = window.shape[0] - 1
+    window[zero_cell] = jnp.zeros(window.shape[1:], F32)
+    copies[0].wait()
+
+    found = todo[0, todo.shape[1] - 1]
+
+    def block_copy(at, n, slot):
+        return pltpu.make_async_copy(
+            far_blocks.at[at, n], blocks.at[slot], block_sems.at[slot]
+        )
+
+    def fetch(slot, _):
+        pair = todo[0, slot]
+        block_copy((pair >> 4) & 255, pair & 15, slot).start()
+        return 0
+
+    lax.fori_loop(0, found, fetch, 0)
+    tables = (own, from_mate, from_other)
+    copies[1].wait()
+    leaf_pick = chosen(choose_leaf, tables, 0, leaves)
+    copies[2].wait()
+    pair_pick = chosen(choose_pair, tables, around * leaves, cols)
+    split = bands * leaves
+    copies[3].wait()
+    fields[:split] = own_blocks(dot(leaf_pick, couple_leaf[...], NT), leaves)
+    copies[4].wait()
+    fields[split:] = own_blocks(dot(pair_pick, couple_pair[...], NT), cols)
+    for copy in copies[5:]:
         copy.wait()
-    mate = section + 1 - 2 * odd
-    tables = (own, from_mate, from_other)
-
-    def tier_of(source):
-        return jnp.where(source == section, 0, jnp.where(source == mate, 1, 2))
-
-    names = names_leaf[...]
-    turn = names % width_all
-    height = names // width_all
-    leaf_pick = chosen(
-        tables,
-        0,
-        around * leaves,
-        tier_of(height // rows),
-        turn // cols * leaves + height % rows * cols + turn % cols,
-        leaves,
-    )
-    names = names_pair[...]
-    turn = names % width_all
-    pair_pick = chosen(
-        tables,
-        around * leaves,
-        around * cols,
-        tier_of(names // width_all),
-        turn,
-        cols,
-    )
-    picks = names_top.shape[1]
-    square = (picks, picks)
-    names = jnp.broadcast_to(names_top[...], square)
-    diagonal = lax.broadcasted_iota(jnp.int32, square, 0) == lax.broadcasted_iota(jnp.int32, square, 1)
-    names = jnp.sum(jnp.where(diagonal, names, 0), axis=1, keepdims=True)
-    at = lax.broadcasted_iota(jnp.int32, (picks, tops.shape[0]), 1)
-    choose_top = jnp.concatenate(
-        [(at == names * bands + b).astype(F32) for b in range(bands)], axis=0
-    ).astype(BF16)
-
-    for at in range(leaves):
-        seen = []
-        for n in range(count):
-            name = listed[n, at // cols, at % cols]
-            up = name // width_all - rows * section + 1
-            turn = (name % width_all + width_all + 1 - cols * column) % width_all
-            seen.append(window[up * broad + turn].astype(BF16))
-        block_copies[at].wait()
-        total = jnp.zeros((bands, leaf), F32)
-        turned = jnp.zeros((leaf, bands), F32)
-        for n in range(count):
-            if n % 2 == 0:
-                total += dot(seen[n], blocks[at, n], NT)
+
+    def several(step, _):
+        first = step * AT_ONCE
+        for k in range(AT_ONCE):
+
+            @pl.when(first + k < found)
+            def _():
+                block_copy(0, 0, first + k).wait()
+
+        results = []
+        for k in range(AT_ONCE):
+            slot = jnp.minimum(first + k, found - 1)
+            where = jnp.where(first + k < found, todo[0, slot] >> 12, zero_cell)
+            cell = window[where].astype(BF16)
+            if k % 2 == 0:
+                results.append(dot(cell, blocks[slot], NT))
             else:
-                turned += dot(blocks[at, n], seen[n], NT)
-        gathered[at] = total + turned.T
-    couple_copies[0].wait()
-    leaf_field = own_blocks(dot(leaf_pick, couple_leaf[...], NT), leaves)[:, :RANK]
-    couple_copies[1].wait()
-    pair_field = own_blocks(dot(pair_pick, couple_pair[...], NT), cols)[:, :RANK]
-    for copy in later:
-        copy.wait()
-    top_pick = dot(choose_top, tops[...], NN)
+                results.append(dot(blocks[slot], cell, NT).T)
+        for k in range(AT_ONCE):
+            at = (todo[0, jnp.minimum(first + k, found - 1)] >> 4) & 255
+            gathered[at] += results[k]
+        return 0
+
+    lax.fori_loop(0, (found + AT_ONCE - 1) // AT_ONCE, several, 0)
+    for g in range(rows):
+        near_part = jnp.swapaxes(gathered[g * cols : (g + 1) * cols], 0, 1)
+        parts[0, :, g] = emission[:, g] + reflect[:, g] * near_part
+        parts[1, :, g] = reflect[:, g]
+
+
+def result_kernel(tops, parts, fields, choose_top, couple_top, basis, up_leaf, up_pair, out):
+    bands, rows, cols, leaf = out.shape
+    leaves = rows * cols
+    picks = couple_top.shape[1] // RANK
+    leaf_field = fields[: bands * leaves, :RANK]
+    pair_field = fields[bands * leaves :, :RANK]
+    top_pick = dot(choose_top[...], tops[...], NN)
     top_pick = jnp.concatenate([top_pick] * (picks // 2), axis=1)
     kept = row_of(top_pick.shape, picks) == lax.broadcasted_iota(jnp.int32, top_pick.shape, 1) // RANK
     top_pick = jnp.where(kept, top_pick, 0.0).astype(BF16)
@@ -354,10 +486,7 @@
     which = row_of(far_part.shape, leaves)
     for at in range(leaves):
         far_part += jnp.where(which == at, dot(leaf_total, basis[at], NN), 0.0)
-    far_part = far_part.reshape(out.shape)
-    for g in range(rows):
-        near_part = jnp.swapaxes(gathered[g * cols : (g + 1) * cols], 0, 1)
-        out[:, g] = emission[:, g] + reflect[:, g] * (near_part + far_part[:, g])
+    out[...] = parts[0] + parts[1] * far_part.reshape(out.shape)
 
 
 def body(
@@ -384,45 +513,32 @@
     mates = [(s, s ^ 1) for s in range(tall)]
     others = [(s, s + 1 if s % 2 else s - 1) for s in range(1, tall - 1)]
     sems = pltpu.SemaphoreType.DMA
-    basis_wide = far(basis.reshape(leaves * RANK, leaf))
-    basis = far(basis.reshape(leaves, RANK, leaf))
-    up_leaf_wide = far(up_leaf.reshape(leaves * RANK, RANK))
-    up_leaf = far(up_leaf.reshape(leaves, RANK, RANK))
-    up_pair_wide = far(upward_pair_transfer.reshape(cols * RANK, RANK))
-    up_pair = far(upward_pair_transfer[0])
+    basis_wide = basis.reshape(leaves * RANK, leaf)
+    basis = basis.reshape(leaves, RANK, leaf)
+    up_leaf_wide = up_leaf.reshape(leaves * RANK, RANK)
+    up_leaf = up_leaf.reshape(leaves, RANK, RANK)
+    up_pair_wide = upward_pair_transfer.reshape(cols * RANK, RANK)
+    up_pair = upward_pair_transfer[0]
     sent, cells = pl.pallas_call(
         coefficients_kernel,
         out_shape=[
-            jax.ShapeDtypeStruct((around, 16, WIDE), BF16),
+            pltpu.HBM((around, 16, WIDE), BF16),
             jax.ShapeDtypeStruct((leaves, bands, leaf), BF16),
         ],
         in_specs=[SMEM] + [HBM] * 4,
-        out_specs=[VMEM] * 2,
+        out_specs=[HBM, VMEM],
         scratch_shapes=[
             pltpu.VMEM(radiosity.shape, F32),
             pltpu.VMEM(basis_wide.shape, BF16),
             pltpu.VMEM(up_leaf.shape, BF16),
             pltpu.VMEM(up_pair.shape, BF16),
-            sems((4,)),
+            pltpu.VMEM((2, 16, WIDE), BF16),
+            sems((around + 4,)),
         ],
         compiler_params=limit(12),
         name="coefficients",
-    )(place, far(radiosity), basis_wide, up_leaf, up_pair)
+    )(place, *map(far, [radiosity, basis_wide, up_leaf, up_pair]))
     ring = lax.all_to_all(sent, "perim", 0, 0)
-    packed, tops = pl.pallas_call(
-        packing_kernel,
-        out_shape=[
-            jax.ShapeDtypeStruct((around * (leaves + cols) + leaves * 4 + 16, 512), BF16),
-            jax.ShapeDtypeStruct((tall, around, bands, LANES), BF16),
-        ],
-        in_specs=[SMEM, VMEM, VMEM],
-        out_specs=[VMEM] * 2,
-        compiler_params=limit(8),
-        name="packing",
-    )(place, ring, cells)
-    from_mate = lax.ppermute(packed, "section", mates)
-    from_other = lax.ppermute(packed, "section", others)
-    tops = lax.all_to_all(tops, "section", 0, 0)
     blocks = near_block.reshape((leaves,) + near_block.shape[2:])
     couple_leaf = couple_leaf.reshape(leaves * RANK, -1)
     couple_pair = couple_pair.reshape(cols * RANK, -1)
@@ -431,29 +547,92 @@
     names_leaf = far_leaf.reshape(leaves, -1)
     names_pair = far_pair.reshape(cols, -1)
     names_top = far_top.reshape(1, -1)
-    passed = [couple_top, basis, up_leaf_wide, up_pair_wide, emission, reflect]
-    held = [names_leaf, names_pair, names_top, blocks, couple_leaf, couple_pair] + passed
-    return pl.pallas_call(
+    names = [names_leaf, names_pair, names_top]
+    window = ((rows + 2) * (cols + 2), bands, leaf)
+    choices = [
+        pltpu.HBM((names_leaf.size, 3 * around * leaves), BF16),
+        pltpu.HBM((names_pair.size, 3 * around * cols), BF16),
+        pltpu.HBM((bands * names_top.size, tall * around * bands), BF16),
+        pltpu.HBM((leaves, bands, leaf), F32),
+        pltpu.HBM((1, LANES), jnp.int32),
+    ]
+    choose_leaf, choose_pair, choose_top, local_part, todo = pl.pallas_call(
+        local_kernel,
+        out_shape=choices,
+        in_specs=[SMEM, VMEM] + [HBM] * 5,
+        out_specs=[HBM] * 5,
+        scratch_shapes=[
+            pltpu.VMEM(window, F32),
+            pltpu.SMEM(listed.shape, jnp.int32),
+            pltpu.SMEM((1, LANES), jnp.int32),
+        ]
+        + [pltpu.VMEM(x.shape, x.dtype) for x in names + [blocks] + choices[:4]]
+        + [sems((leaves + 9,))],
+        compiler_params=limit(28),
+        name="local",
+    )(place, cells, *map(far, [listed] + names + [blocks]))
+    packed = pl.pallas_call(
+        packing_kernel,
+        out_shape=jax.ShapeDtypeStruct((around * (leaves + cols) + leaves * 4 + 16, 512), BF16),
+        in_specs=[SMEM, VMEM, VMEM, HBM],
+        out_specs=VMEM,
+        compiler_params=limit(8),
+        name="packing",
+    )(place, ring, cells, far(local_part))
+    tops = pl.pallas_call(
+        tops_kernel,
+        out_shape=pltpu.HBM((tall, around, bands, LANES), BF16),
+        in_specs=[VMEM],
+        out_specs=HBM,
+        scratch_shapes=[pltpu.VMEM((around, bands, LANES), BF16), sems((tall,))],
+        compiler_params=limit(8),
+        name="tops",
+    )(ring)
+    from_mate = lax.ppermute(packed, "section", mates)
+    from_other = lax.ppermute(packed, "section", others)
+    tops = lax.all_to_all(tops, "section", 0, 0)
+    most = leaves * (listed.shape[0] - 1)
+    held = [choose_leaf, choose_pair, local_part, emission, reflect, couple_leaf, couple_pair]
+    parts, fields, choose_top = pl.pallas_call(
         field_kernel,
-        out_shape=jax.ShapeDtypeStruct(radiosity.shape, F32),
-        in_specs=[SMEM] + [VMEM] * 4 + [HBM] * 13,
-        out_specs=VMEM,
+        out_shape=[
+            jax.ShapeDtypeStruct((2,) + radiosity.shape, F32),
+            jax.ShapeDtypeStruct((bands * (leaves + cols), LANES), F32),
+            jax.ShapeDtypeStruct(choose_top.shape, BF16),
+        ],
+        in_specs=[SMEM] + [VMEM] * 3 + [HBM] * 10,
+        out_specs=[VMEM] * 3,
         scratch_shapes=[
-            pltpu.VMEM(((rows + 2) * (cols + 2), bands, leaf), F32),
-            pltpu.SMEM(listed.shape, jnp.int32),
+            pltpu.VMEM((window[0] + 1,) + window[1:], F32),
+            pltpu.SMEM(todo.shape, jnp.int32),
         ]
         + [pltpu.VMEM(x.shape, x.dtype) for x in held]
-        + [pltpu.VMEM((leaves, bands, leaf), F32), sems((leaves + 12,))],
-        compiler_params=limit(32),
+        + [pltpu.VMEM((most, leaf, leaf), BF16), sems((9,)), sems((most,))],
+        compiler_params=limit(28),
         name="fields",
     )(
         place,
         packed,
         from_mate,
         from_other,
+        *map(far, [todo] + held[:2] + [choose_top] + held[2:] + [blocks]),
+    )
+    return pl.pallas_call(
+        result_kernel,
+        out_shape=jax.ShapeDtypeStruct(radiosity.shape, F32),
+        in_specs=[VMEM] * 8,
+        out_specs=VMEM,
+        compiler_params=limit(8),
+        name="result",
+    )(
         tops.reshape(tall * around * bands, LANES),
-        far(listed),
-        *map(far, held),
+        parts,
+        fields,
+        choose_top,
+        couple_top,
+        basis,
+        up_leaf_wide,
+        up_pair_wide,
     )
 
 

time: 50.9 us -> 44 us (0.86)
  blocking collectives: 30.5 us -> 0 us
  starting transfers between devices: 5.13 us -> 18.4 us
  Pallas kernels: 14.9 us -> 20.6 us
  waiting for transfers between devices: 0.01 us -> 4.34 us
    all_to_all x2 -> x0, blocking collectives: 30.5 us -> none  [the longest x1 19.5 us: body(): ring = lax.all_to_all(sent, 'perim', 0, 0)]
    all_to_all x0 -> x2, starting transfers between devices: none -> 13.1 us  [the longest x1 8.43 us: body(): ring = lax.all_to_all(sent, 'perim', 0, 0)]
    pallas_call x3 -> x6, Pallas kernels: 14.9 us -> 20.6 us  [the longest x1 7.41 us: body(): pl.pallas_call(local_kernel, out_shape=choices, in_specs=[SMEM, VMEM] + [...]
    all_to_all x0 -> x2, waiting for transfers between devices: none -> 3.59 us  [the longest x1 3.58 us: body(): ring = lax.all_to_all(sent, 'perim', 0, 0)]
    ppermute x1, waiting for transfers between devices: 0.01 us -> 0.75 us  [body(): from_other = lax.ppermute(packed, 'section', others)]
  transfers between devices with their start and end apart: 2 -> 4, of which waited for: 0 -> 2; matrix products, arithmetic and copies ran while one was open for 0% -> 0% of each run, Pallas kernels for 0% -> 34%
where the time goes in v3:
time: 44 us; the launch traced here: 43.6 us
  Pallas kernels  20.6 us (47%)
  starting transfers between devices  18.4 us (42%)
  waiting for transfers between devices  4.34 us (10%)
    all_to_all x1, starting transfers between devices, body(): ring = lax.all_to_all(sent, 'perim', 0, 0)  8.43 us
    pallas_call x1, Pallas kernels, body(): pl.pallas_call(local_kernel, out_shape=choices, in_specs=[SMEM, VMEM] + [...  7.41 us
    pallas_call x1, Pallas kernels, body(): pl.pallas_call(field_kernel, out_shape=[jax.ShapeDtypeStruct((2,) + radio...  6.47 us
    ppermute x1, starting transfers between devices, body(): from_other = lax.ppermute(packed, 'section', others)  5.23 us
    all_to_all x1, starting transfers between devices, body(): tops = lax.all_to_all(tops, 'section', 0, 0)  4.69 us
    all_to_all x1, waiting for transfers between devices, body(): ring = lax.all_to_all(sent, 'perim', 0, 0)  3.58 us
    pallas_call x1, Pallas kernels, body(): pl.pallas_call(coefficients_kernel, out_shape=[pltpu.HBM((around, 16, WID...  3.56 us
    pallas_call x1, Pallas kernels, body(): pl.pallas_call(result_kernel, out_shape=jax.ShapeDtypeStruct(radiosity.sh...  1.82 us
  transfers between devices with their start and end apart: 4, of which 2 were waited for; matrix products, arithmetic and copies ran while one was open for 0% of the time, Pallas kernels for 34%

profile of v3, /device:TPU:1, one launch (start us, length us, event | category | flops | bytes accessed | tf_op | source)
XLA Modules:
  0.0 43.6 jit_solution(14427612861040002218)
XLA Ops:
  0.0 0.1 pad_add_fusion.place
  0.1 3.6 %coefficients.1 = (bf16[16,16,1152]{2,1,0:T(8,128)(2,1)}, bf16[16,8,256]{2,1,0:T(8,128)(2,1)S(1)}) custom-call(s32[2]{0:T(128)S(1)} %pad_add_fusion.place, f32[8,2,8,256]{3,2,1,0:T(8,128)} %far_radiosity.1, bf16[1024,256]{1,0:T(8,128)(2,1)} %bitcast.17, bf16[16,64,64]{2,1,0:T(8,128)(2,1)} %bitcast.20, bf16[8,64,64]{2,1,0:T(8,128)(2,1)} %bitcast.22), custom_call_target="tpu_custom_call" | custom-call | tf_op jit(solution)/shard_map/coefficients/pallas_call | solution.py:522
  3.6 8.4 %all-to-all-start = ((bf16[16,16,1152]{2,1,0:T(8,128)(2,1)}), bf16[16,16,1152]{2,1,0:T(8,128)(2,1)S(1)}, u32[]{:S(2)}, u32[]{:S(2)}) async-start(bf16[16,16,1152]{2,1,0:T(8,128)(2,1)} %get-tuple-element.15), calls=%async_computation | async-start | bytes 1179648 | tf_op jit(solution)/shard_map/all_to_all | solution.py:541
  12.1 7.4 %local.1 = (bf16[256,768]{1,0:T(8,128)(2,1)}, bf16[128,384]{1,0:T(8,128)(2,1)}, bf16[64,1024]{1,0:T(8,128)(2,1)}, f32[16,8,256]{2,1,0:T(8,128)}, s32[1,128]{1,0:T(1,128)}) custom-call(s32[2]{0:T(128)S(1)} %pad_add_fusion.place, bf16[16,8,256]{2,1,0:T(8,128)(2,1)S(1)} %get-tuple-element.16.cells, s32[6,2,8]{2,1,0:T(2,128)} %bitcast.30, s32[16,16]{1,0:T(8,128)} %bitcast.29, ...), custom_call_target="tpu_custom_call" | custom-call | tf_op jit(solution)/shard_map/local/pallas_call | solution.py:559
  19.5 0.0 copy-start
  19.5 0.0 copy-start.1
  19.5 0.0 copy-start.2
  19.5 0.0 copy-start.3
  19.6 3.6 %all-to-all-done.ring = bf16[16,16,1152]{2,1,0:T(8,128)(2,1)S(1)} async-done(((bf16[16,16,1152]{2,1,0:T(8,128)(2,1)}), bf16[16,16,1152]{2,1,0:T(8,128)(2,1)S(1)}, u32[]{:S(2)}, u32[]{:S(2)}) %all-to-all-start) | async-done | bytes 589856 | tf_op jit(solution)/shard_map/all_to_all | solution.py:541
  23.1 0.6 %packing.1.own = bf16[464,512]{1,0:T(8,128)(2,1)S(1)} custom-call(s32[2]{0:T(128)S(1)} %pad_add_fusion.place, bf16[16,16,1152]{2,1,0:T(8,128)(2,1)S(1)} %all-to-all-done.ring, bf16[16,8,256]{2,1,0:T(8,128)(2,1)S(1)} %get-tuple-element.16.cells, f32[16,8,256]{2,1,0:T(8,128)} %get-tuple-element.17.local_part.far_gathered), custom_call_target="tpu_custom_call" | custom-call | tf_op jit(solution)/shard_map/packing/pallas_call | solution.py:574
  23.7 5.2 %collective-permute-start.1 = (bf16[464,512]{1,0:T(8,128)(2,1)S(1)}, bf16[464,512]{1,0:T(8,128)(2,1)S(1)}, u32[]{:S(2)}, u32[]{:S(2)}) collective-permute-start(bf16[464,512]{1,0:T(8,128)(2,1)S(1)} %packing.1.own), channel_id=1, source_target_pairs={{16,32},{32,16},{48,64},{64,48},{80,96},{96,80},{17,33},{33,17},{4... | collective-permute-start | bytes 1425416 | tf_op jit(solution)/shard_map/ppermute | solution.py:592
  29.0 0.1 collective-permute-start
  29.0 0.8 %tops.1 = bf16[8,16,8,128]{3,2,1,0:T(8,128)(2,1)} custom-call(bf16[16,16,1152]{2,1,0:T(8,128)(2,1)S(1)} %all-to-all-done.ring), custom_call_target="tpu_custom_call" | custom-call | tf_op jit(solution)/shard_map/tops/pallas_call | solution.py:582
  29.8 4.7 %all-to-all-start.1 = ((bf16[8,16,8,128]{3,2,1,0:T(8,128)(2,1)}), bf16[8,16,8,128]{3,2,1,0:T(8,128)(2,1)S(1)}, u32[]{:S(2)}, u32[]{:S(2)}) async-start(bf16[8,16,8,128]{3,2,1,0:T(8,128)(2,1)} %tops.1), calls=%async_computation.1 | async-start | bytes 524288 | tf_op jit(solution)/shard_map/all_to_all | solution.py:593
  34.5 0.8 %collective-permute-done.1.from_other = bf16[464,512]{1,0:T(8,128)(2,1)S(1)} collective-permute-done((bf16[464,512]{1,0:T(8,128)(2,1)S(1)}, bf16[464,512]{1,0:T(8,128)(2,1)S(1)}, u32[]{:S(2)}, u32[]{:S(2)}) %collective-permute-start.1) | collective-permute-done | bytes 475168 | tf_op jit(solution)/shard_map/ppermute | solution.py:592
  35.3 0.0 collective-permute-done.from_mate
  35.3 6.5 %fields.1 = (f32[2,8,2,8,256]{4,3,2,1,0:T(8,128)S(1)}, f32[192,128]{1,0:T(8,128)S(1)}, bf16[64,1024]{1,0:T(8,128)(2,1)S(1)}) custom-call(s32[2]{0:T(128)S(1)} %pad_add_fusion.place, bf16[464,512]{1,0:T(8,128)(2,1)S(1)} %packing.1.own, bf16[464,512]{1,0:T(8,128)(2,1)S(1)} %collective-permute-done.from_mate, ...), custom_call_target="tpu_custom_call" | custom-call | tf_op jit(solution)/shard_map/fields/pallas_call | solution.py:596
  41.8 0.0 all-to-all-done.1
  41.8 0.0 copy-done
  41.8 0.0 copy-done.1
  41.8 0.0 copy-done.2
  41.8 0.0 copy-done.3
  41.8 1.8 %result.1 = f32[8,2,8,256]{3,2,1,0:T(8,128)} custom-call(bf16[1024,128]{1,0:T(8,128)(2,1)S(1)} %bitcast.19, f32[2,8,2,8,256]{4,3,2,1,0:T(8,128)S(1)} %get-tuple-element.22.parts, f32[192,128]{1,0:T(8,128)S(1)} %get-tuple-element.23.fields, bf16[64,1024]{1,0:T(8,128)(2,1)S(1)} %get-tuple-element.24.choose_top, bf16[64,512]{1,0:T(8,128)(2,1)S(1)} %bitcast.24, ...), custom_call_target="tpu_custom_call" | custom-call | tf_op jit(solution)/shard_map/result/pallas_call | solution.py:620
Async XLA Ops:
  3.6 19.5 %all-to-all-start = ((bf16[16,16,1152]{2,1,0:T(8,128)(2,1)}), bf16[16,16,1152]{2,1,0:T(8,128)(2,1)S(1)}, u32[]{:S(2)}, u32[]{:S(2)}) async-start(bf16[16,16,1152]{2,1,0:T(8,128)(2,1)} %get-tuple-element.15), calls=%async_computation | async-start | bytes 1179648 | tf_op jit(solution)/shard_map/all_to_all | solution.py:541
  19.5 22.3 %copy-start = (bf16[2,8,64,256]{3,2,1,0:T(8,128)(2,1)S(1)}, bf16[2,8,64,256]{3,2,1,0:T(8,128)(2,1)}, u32[]{:S(2)}) copy-start(bf16[2,8,64,256]{3,2,1,0:T(8,128)(2,1)} %param.17) | copy-start | bytes 1572868
  19.5 22.3 %copy-start.1 = (bf16[2,8,64,64]{3,2,1,0:T(8,128)(2,1)S(1)}, bf16[2,8,64,64]{3,2,1,0:T(8,128)(2,1)}, u32[]{:S(2)}) copy-start(bf16[2,8,64,64]{3,2,1,0:T(8,128)(2,1)} %param.18) | copy-start | bytes 393220
  19.5 22.3 %copy-start.2 = (bf16[1,8,64,64]{3,2,1,0:T(8,128)(2,1)S(1)}, bf16[1,8,64,64]{3,2,1,0:T(8,128)(2,1)}, u32[]{:S(2)}) copy-start(bf16[1,8,64,64]{3,2,1,0:T(8,128)(2,1)} %param.19) | copy-start | bytes 196612
  19.5 22.3 %copy-start.3 = (bf16[1,1,64,512]{3,2,1,0:T(8,128)(2,1)S(1)}, bf16[1,1,64,512]{3,2,1,0:T(8,128)(2,1)}, u32[]{:S(2)}) copy-start(bf16[1,1,64,512]{3,2,1,0:T(8,128)(2,1)} %param.23) | copy-start | bytes 196612
  23.7 11.6 %collective-permute-start.1 = (bf16[464,512]{1,0:T(8,128)(2,1)S(1)}, bf16[464,512]{1,0:T(8,128)(2,1)S(1)}, u32[]{:S(2)}, u32[]{:S(2)}) collective-permute-start(bf16[464,512]{1,0:T(8,128)(2,1)S(1)} %packing.1.own), channel_id=1, source_target_pairs={{16,32},{32,16},{48,64},{64,48},{80,96},{96,80},{17,33},{33,17},{4... | collective-permute-start | bytes 1425416 | tf_op jit(solution)/shard_map/ppermute | solution.py:592
  29.0 6.3 %collective-permute-start = (bf16[464,512]{1,0:T(8,128)(2,1)S(1)}, bf16[464,512]{1,0:T(8,128)(2,1)S(1)}, u32[]{:S(2)}, u32[]{:S(2)}) collective-permute-start(bf16[464,512]{1,0:T(8,128)(2,1)S(1)} %packing.1.own), channel_id=1, source_target_pairs={{0,16},{16,0},{32,48},{48,32},{64,80},{80,64},{96,112},{112,96},{1... | collective-permute-start | bytes 1425416 | tf_op jit(solution)/shard_map/ppermute | solution.py:591
  29.8 11.9 %all-to-all-start.1 = ((bf16[8,16,8,128]{3,2,1,0:T(8,128)(2,1)}), bf16[8,16,8,128]{3,2,1,0:T(8,128)(2,1)S(1)}, u32[]{:S(2)}, u32[]{:S(2)}) async-start(bf16[8,16,8,128]{3,2,1,0:T(8,128)(2,1)} %tops.1), calls=%async_computation.1 | async-start | bytes 524288 | tf_op jit(solution)/shard_map/all_to_all | solution.py:593

commit v4 on v3

--- a/solution.py
+++ b/solution.py
@@ -13,10 +13,9 @@
 RANK = 64
 WIDE = 1152
 VMEM = pl.BlockSpec(memory_space=pltpu.VMEM)
-SMEM = pl.BlockSpec(memory_space=pltpu.SMEM)
 HBM = pl.BlockSpec(memory_space=pltpu.HBM)
 ANY = pl.BlockSpec(memory_space=pl.ANY)
-AT_ONCE = 8
+AT_ONCE = 16
 
 
 def dot(left, right, dims):
@@ -44,6 +43,12 @@
     return total + pltpu.roll(total, RANK, 1)
 
 
+def on_diagonal(twice, count):
+    mine = row_of(twice.shape, count) - lax.broadcasted_iota(jnp.int32, twice.shape, 1) // RANK
+    tiles = [jnp.where(mine == 2 * tile, twice, 0.0) for tile in range(count // 2)]
+    return jnp.concatenate(tiles, axis=1).astype(BF16)
+
+
 def side_by_side(twice, count):
     low = lax.broadcasted_iota(jnp.int32, (count, LANES), 1) < RANK
     return jnp.concatenate(
@@ -64,7 +69,6 @@
 
 
 def coefficients_kernel(
-    place,
     far_radiosity,
     far_basis,
     far_up_leaf,
@@ -88,31 +92,24 @@
         sems,
     )
     copies[0].wait()
-    column = place[1]
+    column = lax.axis_index("perim")
     bands, rows, cols, leaf = radiosity.shape
     leaves = rows * cols
-    for g in range(rows):
-        turned = jnp.swapaxes(radiosity[:, g], 0, 1)
-        cells[g * cols : (g + 1) * cols] = turned.astype(BF16)
     shaded = radiosity[...].reshape(bands * leaves, leaf).astype(BF16)
     copies[1].wait()
     leaf_twice = own_blocks(dot(shaded, basis[...], NT), leaves)
-    leaf_coef = leaf_twice[:, :RANK].astype(BF16)
+    of_pairs = leaf_twice.reshape(bands, rows, cols, LANES)
+    of_pairs = jnp.concatenate(
+        [on_diagonal(of_pairs[:, g].reshape(bands * cols, LANES), cols) for g in range(rows)],
+        axis=1,
+    )
     copies[2].wait()
-    parts = jnp.zeros((bands * leaves, RANK), F32)
-    which = row_of(parts.shape, leaves)
-    for at in range(leaves):
-        parts += jnp.where(which == at, dot(leaf_coef, up_leaf[at], NN), 0.0)
-    pair = jnp.sum(parts.reshape(bands, rows, cols, RANK), axis=1).reshape(bands * cols, RANK)
-    pair_coef = pair.astype(BF16)
+    pair = dot(of_pairs, up_leaf[...], NN)
+    pair_twice = jnp.concatenate([pair, pair], axis=1)
     copies[3].wait()
-    parts = jnp.zeros((bands * cols, RANK), F32)
-    which = row_of(parts.shape, cols)
-    for at in range(cols):
-        parts += jnp.where(which == at, dot(pair_coef, up_pair[at], NN), 0.0)
-    top = jnp.sum(parts.reshape(bands, cols, RANK), axis=1)
+    top = dot(on_diagonal(pair_twice, cols), up_pair[...], NN)
+    top = jnp.sum(top.reshape(bands, cols, RANK), axis=1)
     top_twice = jnp.concatenate([top, top], axis=1)
-    pair_twice = jnp.concatenate([pair, pair], axis=1)
 
     def edge(col):
         return jnp.concatenate(
@@ -132,12 +129,15 @@
     copies = started(
         [(block.at[jnp.where(to_right == to, 1, 0)], sent.at[to]) for to in range(around)], sems, 4
     )
+    for g in range(rows):
+        turned = jnp.swapaxes(radiosity[:, g], 0, 1)
+        cells[g * cols : (g + 1) * cols] = turned.astype(BF16)
     for copy in copies:
         copy.wait()
 
 
-def packing_kernel(place, ring, cells, local_part, packed):
-    column = place[1]
+def packing_kernel(ring, cells, local_part, packed):
+    column = lax.axis_index("perim")
     around, leaves = ring.shape[:2]
     cols = leaves // 2
     for at in range(around):
@@ -196,7 +196,6 @@
 
 
 def local_kernel(
-    place,
     cells,
     far_listed,
     far_names_leaf,
@@ -206,8 +205,8 @@
     far_choose_leaf,
     far_choose_pair,
     far_choose_top,
-    far_local_part,
     far_todo,
+    local_part,
     window,
     listed,
     todo,
@@ -218,7 +217,6 @@
     choose_leaf,
     choose_pair,
     choose_top,
-    local_part,
     sems,
 ):
     leaves, count = blocks.shape[:2]
@@ -236,7 +234,7 @@
     )
     for copy in lists:
         copy.wait()
-    section = place[0]
+    section, column = lax.axis_index("section"), lax.axis_index("perim")
     cols = names_pair.shape[0]
     rows = leaves // cols
     width_all = choose_pair.shape[1] // 3
@@ -283,7 +281,7 @@
         seen = []
         for n in range(count):
             name = listed[n, at // cols, at % cols]
-            up, turn = position(name, section, place[1], rows, cols, width_all)
+            up, turn = position(name, section, column, rows, cols, width_all)
             where = up * broad + turn
             seen.append(window[where].astype(BF16))
             if n > 0:
@@ -296,7 +294,7 @@
         local_part[at] = near_products(seen, blocks.at[at])
     todo[0, todo.shape[1] - 1] = found
     results += started(
-        [(local_part, far_local_part), (todo, far_todo)], sems, len(lists) + leaves + 3
+        [(todo, far_todo)], sems, len(lists) + leaves + 3
     )
     for copy in results:
         copy.wait()
@@ -324,15 +322,14 @@
 
 
 def field_kernel(
-    place,
     own,
     from_mate,
     from_other,
+    local_part,
     far_todo,
     far_choose_leaf,
     far_choose_pair,
     far_choose_top,
-    far_gathered,
     far_emission,
     far_reflect,
     far_couple_leaf,
@@ -361,7 +358,6 @@
             (far_choose_pair, choose_pair),
             (far_couple_leaf, couple_leaf),
             (far_couple_pair, couple_pair),
-            (far_gathered, gathered),
             (far_choose_top, choose_top),
             (far_emission, emission),
             (far_reflect, reflect),
@@ -369,7 +365,7 @@
         sems,
     )
     leaves = gathered.shape[0]
-    section, column = place[0], place[1]
+    section = lax.axis_index("section")
     bands, rows, cols, leaf = emission.shape
     around = (own.shape[0] - 16 - leaves * 4) // (leaves + cols)
     broad = cols + 2
@@ -431,6 +427,7 @@
     fields[split:] = own_blocks(dot(pair_pick, couple_pair[...], NT), cols)
     for copy in copies[5:]:
         copy.wait()
+    gathered[...] = local_part[...]
 
     def several(step, _):
         first = step * AT_ONCE
@@ -481,11 +478,8 @@
     )
     spread = spread.reshape(bands * leaves, RANK).astype(BF16)
     leaf_total = leaf_field + own_blocks(dot(spread, up_leaf[...], NT), leaves)[:, :RANK]
-    leaf_total = leaf_total.astype(BF16)
-    far_part = jnp.zeros((bands * leaves, leaf), F32)
-    which = row_of(far_part.shape, leaves)
-    for at in range(leaves):
-        far_part += jnp.where(which == at, dot(leaf_total, basis[at], NN), 0.0)
+    leaf_total = jnp.concatenate([leaf_total, leaf_total], axis=1)
+    far_part = dot(on_diagonal(leaf_total, leaves), basis[...], NN)
     out[...] = parts[0] + parts[1] * far_part.reshape(out.shape)
 
 
@@ -509,35 +503,31 @@
     tall = lax.axis_size("section")
     bands, rows, cols, leaf = radiosity.shape
     leaves = rows * cols
-    place = jnp.stack([lax.axis_index("section"), lax.axis_index("perim")]).astype(jnp.int32)
     mates = [(s, s ^ 1) for s in range(tall)]
     others = [(s, s + 1 if s % 2 else s - 1) for s in range(1, tall - 1)]
     sems = pltpu.SemaphoreType.DMA
-    basis_wide = basis.reshape(leaves * RANK, leaf)
-    basis = basis.reshape(leaves, RANK, leaf)
-    up_leaf_wide = up_leaf.reshape(leaves * RANK, RANK)
-    up_leaf = up_leaf.reshape(leaves, RANK, RANK)
-    up_pair_wide = upward_pair_transfer.reshape(cols * RANK, RANK)
-    up_pair = upward_pair_transfer[0]
+    basis = basis.reshape(leaves * RANK, leaf)
+    up_leaf = up_leaf.reshape(leaves * RANK, RANK)
+    up_pair = upward_pair_transfer.reshape(cols * RANK, RANK)
     sent, cells = pl.pallas_call(
         coefficients_kernel,
         out_shape=[
             pltpu.HBM((around, 16, WIDE), BF16),
             jax.ShapeDtypeStruct((leaves, bands, leaf), BF16),
         ],
-        in_specs=[SMEM] + [HBM] * 4,
+        in_specs=[HBM] * 4,
         out_specs=[HBM, VMEM],
         scratch_shapes=[
             pltpu.VMEM(radiosity.shape, F32),
-            pltpu.VMEM(basis_wide.shape, BF16),
+            pltpu.VMEM(basis.shape, BF16),
             pltpu.VMEM(up_leaf.shape, BF16),
             pltpu.VMEM(up_pair.shape, BF16),
             pltpu.VMEM((2, 16, WIDE), BF16),
             sems((around + 4,)),
         ],
-        compiler_params=limit(12),
+        compiler_params=limit(4),
         name="coefficients",
-    )(place, *map(far, [radiosity, basis_wide, up_leaf, up_pair]))
+    )(*map(far, [radiosity, basis, up_leaf, up_pair]))
     ring = lax.all_to_all(sent, "perim", 0, 0)
     blocks = near_block.reshape((leaves,) + near_block.shape[2:])
     couple_leaf = couple_leaf.reshape(leaves * RANK, -1)
@@ -553,39 +543,39 @@
         pltpu.HBM((names_leaf.size, 3 * around * leaves), BF16),
         pltpu.HBM((names_pair.size, 3 * around * cols), BF16),
         pltpu.HBM((bands * names_top.size, tall * around * bands), BF16),
-        pltpu.HBM((leaves, bands, leaf), F32),
         pltpu.HBM((1, LANES), jnp.int32),
+        jax.ShapeDtypeStruct((leaves, bands, leaf), F32),
     ]
-    choose_leaf, choose_pair, choose_top, local_part, todo = pl.pallas_call(
+    choose_leaf, choose_pair, choose_top, todo, local_part = pl.pallas_call(
         local_kernel,
         out_shape=choices,
-        in_specs=[SMEM, VMEM] + [HBM] * 5,
-        out_specs=[HBM] * 5,
+        in_specs=[VMEM] + [HBM] * 5,
+        out_specs=[HBM] * 4 + [VMEM],
         scratch_shapes=[
             pltpu.VMEM(window, F32),
             pltpu.SMEM(listed.shape, jnp.int32),
             pltpu.SMEM((1, LANES), jnp.int32),
         ]
-        + [pltpu.VMEM(x.shape, x.dtype) for x in names + [blocks] + choices[:4]]
+        + [pltpu.VMEM(x.shape, x.dtype) for x in names + [blocks] + choices[:3]]
         + [sems((leaves + 9,))],
-        compiler_params=limit(28),
+        compiler_params=limit(17),
         name="local",
-    )(place, cells, *map(far, [listed] + names + [blocks]))
+    )(cells, *map(far, [listed] + names + [blocks]))
     packed = pl.pallas_call(
         packing_kernel,
         out_shape=jax.ShapeDtypeStruct((around * (leaves + cols) + leaves * 4 + 16, 512), BF16),
-        in_specs=[SMEM, VMEM, VMEM, HBM],
+        in_specs=[VMEM, VMEM, ANY],
         out_specs=VMEM,
-        compiler_params=limit(8),
+        compiler_params=limit(4),
         name="packing",
-    )(place, ring, cells, far(local_part))
+    )(ring, cells, local_part)
     tops = pl.pallas_call(
         tops_kernel,
         out_shape=pltpu.HBM((tall, around, bands, LANES), BF16),
         in_specs=[VMEM],
         out_specs=HBM,
         scratch_shapes=[pltpu.VMEM((around, bands, LANES), BF16), sems((tall,))],
-        compiler_params=limit(8),
+        compiler_params=limit(3),
         name="tops",
     )(ring)
     from_mate = lax.ppermute(packed, "section", mates)
@@ -600,7 +590,7 @@
             jax.ShapeDtypeStruct((bands * (leaves + cols), LANES), F32),
             jax.ShapeDtypeStruct(choose_top.shape, BF16),
         ],
-        in_specs=[SMEM] + [VMEM] * 3 + [HBM] * 10,
+        in_specs=[VMEM] * 4 + [HBM] * 9,
         out_specs=[VMEM] * 3,
         scratch_shapes=[
             pltpu.VMEM((window[0] + 1,) + window[1:], F32),
@@ -608,21 +598,21 @@
         ]
         + [pltpu.VMEM(x.shape, x.dtype) for x in held]
         + [pltpu.VMEM((most, leaf, leaf), BF16), sems((9,)), sems((most,))],
-        compiler_params=limit(28),
+        compiler_params=limit(19),
         name="fields",
     )(
-        place,
         packed,
         from_mate,
         from_other,
-        *map(far, [todo] + held[:2] + [choose_top] + held[2:] + [blocks]),
+        local_part,
+        *map(far, [todo] + held[:2] + [choose_top] + held[3:] + [blocks]),
     )
     return pl.pallas_call(
         result_kernel,
         out_shape=jax.ShapeDtypeStruct(radiosity.shape, F32),
         in_specs=[VMEM] * 8,
         out_specs=VMEM,
-        compiler_params=limit(8),
+        compiler_params=limit(4),
         name="result",
     )(
         tops.reshape(tall * around * bands, LANES),
@@ -631,8 +621,8 @@
         choose_top,
         couple_top,
         basis,
-        up_leaf_wide,
-        up_pair_wide,
+        up_leaf,
+        up_pair,
     )
 
 

time: 44 us -> 42 us (0.955)
  Pallas kernels: 20.6 us -> 17.5 us
  waiting for transfers between devices: 4.34 us -> 5.53 us
    all_to_all x1, waiting for transfers between devices: 3.58 us -> 4.71 us  [body(): ring = lax.all_to_all(sent, 'perim', 0, 0)]
    pallas_call x1, Pallas kernels: 7.41 us -> 6.31 us  [body(): pl.pallas_call(local_kernel, out_shape=choices, in_specs=[VMEM] + [HBM] *...]
    pallas_call x1, Pallas kernels: 6.47 us -> 5.67 us  [body(): pl.pallas_call(field_kernel, out_shape=[jax.ShapeDtypeStruct((2,) + radio...]
    pallas_call x1, Pallas kernels: 3.56 us -> 2.99 us  [body(): pl.pallas_call(coefficients_kernel, out_shape=[pltpu.HBM((around, 16, WID...]
    pallas_call x1, Pallas kernels: 0.57 us -> 0.03 us  [body(): pl.pallas_call(packing_kernel, out_shape=jax.ShapeDtypeStruct((around * (...]
  transfers between devices with their start and end apart: 4 -> 4, of which waited for: 2 -> 3; matrix products, arithmetic and copies ran while one was open for 0% -> 0% of each run, Pallas kernels for 34% -> 31%
where the time goes in v4:
time: 42 us; the launch traced here: 41.6 us
  starting transfers between devices  18.4 us (44%)
  Pallas kernels  17.5 us (42%)
  waiting for transfers between devices  5.53 us (13%)
    all_to_all x1, starting transfers between devices, body(): ring = lax.all_to_all(sent, 'perim', 0, 0)  8.44 us
    pallas_call x1, Pallas kernels, body(): pl.pallas_call(local_kernel, out_shape=choices, in_specs=[VMEM] + [HBM] *...  6.31 us
    pallas_call x1, Pallas kernels, body(): pl.pallas_call(field_kernel, out_shape=[jax.ShapeDtypeStruct((2,) + radio...  5.67 us
    ppermute x1, starting transfers between devices, body(): from_other = lax.ppermute(packed, 'section', others)  5.21 us
    all_to_all x1, waiting for transfers between devices, body(): ring = lax.all_to_all(sent, 'perim', 0, 0)  4.71 us
    all_to_all x1, starting transfers between devices, body(): tops = lax.all_to_all(tops, 'section', 0, 0)  4.68 us
    pallas_call x1, Pallas kernels, body(): pl.pallas_call(coefficients_kernel, out_shape=[pltpu.HBM((around, 16, WID...  2.99 us
    pallas_call x1, Pallas kernels, body(): pl.pallas_call(result_kernel, out_shape=jax.ShapeDtypeStruct(radiosity.sh...  1.76 us
  transfers between devices with their start and end apart: 4, of which 3 were waited for; matrix products, arithmetic and copies ran while one was open for 0% of the time, Pallas kernels for 31%

profile of v4, /device:TPU:1, one launch (start us, length us, event | category | flops | bytes accessed | tf_op | source)
XLA Modules:
  0.0 41.6 jit_solution(5489633959967981580)
XLA Ops:
  0.0 3.0 %coefficients.1 = (bf16[16,16,1152]{2,1,0:T(8,128)(2,1)}, bf16[16,8,256]{2,1,0:T(8,128)(2,1)S(1)}) custom-call(f32[8,2,8,256]{3,2,1,0:T(8,128)} %far_radiosity.1, bf16[1024,256]{1,0:T(8,128)(2,1)} %bitcast.12, bf16[1024,64]{1,0:T(8,128)(2,1)} %bitcast.15, bf16[512,64]{1,0:T(8,128)(2,1)} %bitcast.17), custom_call_target="tpu_custom_call" | custom-call | tf_op jit(solution)/shard_map/coefficients/pallas_call | solution.py:512
  3.0 8.4 %all-to-all-start = ((bf16[16,16,1152]{2,1,0:T(8,128)(2,1)}), bf16[16,16,1152]{2,1,0:T(8,128)(2,1)S(1)}, u32[]{:S(2)}, u32[]{:S(2)}) async-start(bf16[16,16,1152]{2,1,0:T(8,128)(2,1)} %get-tuple-element.15), calls=%async_computation | async-start | bytes 1179648 | tf_op jit(solution)/shard_map/all_to_all | solution.py:531
  11.4 6.3 %local.1 = (bf16[256,768]{1,0:T(8,128)(2,1)}, bf16[128,384]{1,0:T(8,128)(2,1)}, bf16[64,1024]{1,0:T(8,128)(2,1)}, s32[1,128]{1,0:T(1,128)}, f32[16,8,256]{2,1,0:T(8,128)S(1)}) custom-call(bf16[16,8,256]{2,1,0:T(8,128)(2,1)S(1)} %get-tuple-element.16.cells, s32[6,2,8]{2,1,0:T(2,128)} %bitcast.25, s32[16,16]{1,0:T(8,128)} %bitcast.24, s32[8,16]{1,0:T(8,128)} %bitcast.26, ...), custom_call_target="tpu_custom_call" | custom-call | tf_op jit(solution)/shard_map/local/pallas_call | solution.py:549
  17.8 0.0 copy-start
  17.8 0.0 copy-start.1
  17.8 0.0 copy-start.2
  17.8 0.0 copy-start.3
  17.8 4.7 %all-to-all-done.ring = bf16[16,16,1152]{2,1,0:T(8,128)(2,1)S(1)} async-done(((bf16[16,16,1152]{2,1,0:T(8,128)(2,1)}), bf16[16,16,1152]{2,1,0:T(8,128)(2,1)S(1)}, u32[]{:S(2)}, u32[]{:S(2)}) %all-to-all-start) | async-done | bytes 589856 | tf_op jit(solution)/shard_map/all_to_all | solution.py:531
  22.6 5.2 %collective-permute-start.1 = (bf16[464,512]{1,0:T(8,128)(2,1)S(1)}, bf16[464,512]{1,0:T(8,128)(2,1)S(1)}, u32[]{:S(2)}, u32[]{:S(2)}) collective-permute-start(bf16[464,512]{1,0:T(8,128)(2,1)S(1)} %packing.1.own), channel_id=1, source_target_pairs={{16,32},{32,16},{48,64},{64,48},{80,96},{96,80},{17,33},{33,17},{4... | collective-permute-start | bytes 1425416 | tf_op jit(solution)/shard_map/ppermute | solution.py:582
  27.8 0.1 collective-permute-start
  27.9 0.8 %tops.1 = bf16[8,16,8,128]{3,2,1,0:T(8,128)(2,1)} custom-call(bf16[16,16,1152]{2,1,0:T(8,128)(2,1)S(1)} %all-to-all-done.ring), custom_call_target="tpu_custom_call" | custom-call | tf_op jit(solution)/shard_map/tops/pallas_call | solution.py:572
  28.7 4.7 %all-to-all-start.1 = ((bf16[8,16,8,128]{3,2,1,0:T(8,128)(2,1)}), bf16[8,16,8,128]{3,2,1,0:T(8,128)(2,1)S(1)}, u32[]{:S(2)}, u32[]{:S(2)}) async-start(bf16[8,16,8,128]{3,2,1,0:T(8,128)(2,1)} %tops.1), calls=%async_computation.1 | async-start | bytes 524288 | tf_op jit(solution)/shard_map/all_to_all | solution.py:583
  33.3 0.8 %collective-permute-done.1.from_other = bf16[464,512]{1,0:T(8,128)(2,1)S(1)} collective-permute-done((bf16[464,512]{1,0:T(8,128)(2,1)S(1)}, bf16[464,512]{1,0:T(8,128)(2,1)S(1)}, u32[]{:S(2)}, u32[]{:S(2)}) %collective-permute-start.1) | collective-permute-done | bytes 475168 | tf_op jit(solution)/shard_map/ppermute | solution.py:582
  34.1 0.0 collective-permute-done.from_mate
  34.1 5.7 %fields.1 = (f32[2,8,2,8,256]{4,3,2,1,0:T(8,128)S(1)}, f32[192,128]{1,0:T(8,128)S(1)}, bf16[64,1024]{1,0:T(8,128)(2,1)S(1)}) custom-call(bf16[464,512]{1,0:T(8,128)(2,1)S(1)} %packing.1.own, bf16[464,512]{1,0:T(8,128)(2,1)S(1)} %collective-permute-done.from_mate, bf16[464,512]{1,0:T(8,128)(2,1)S(1)} %collective-permute-done.1.from_other, ...), custom_call_target="tpu_custom_call" | custom-call | tf_op jit(solution)/shard_map/fields/pallas_call | solution.py:586
  39.8 0.1 all-to-all-done.1
  39.8 0.0 copy-done
  39.8 0.0 copy-done.1
  39.8 0.0 copy-done.2
  39.8 0.0 copy-done.3
  39.9 1.8 %result.1 = f32[8,2,8,256]{3,2,1,0:T(8,128)} custom-call(bf16[1024,128]{1,0:T(8,128)(2,1)S(1)} %bitcast.14, f32[2,8,2,8,256]{4,3,2,1,0:T(8,128)S(1)} %get-tuple-element.22.parts, f32[192,128]{1,0:T(8,128)S(1)} %get-tuple-element.23.fields, bf16[64,1024]{1,0:T(8,128)(2,1)S(1)} %get-tuple-element.24.choose_top, bf16[64,512]{1,0:T(8,128)(2,1)S(1)} %bitcast.19, ...), custom_call_target="tpu_custom_call" | custom-call | tf_op jit(solution)/shard_map/result/pallas_call | solution.py:610
  (1 shorter events, 0.0 us)
Async XLA Ops:
  3.0 19.5 %all-to-all-start = ((bf16[16,16,1152]{2,1,0:T(8,128)(2,1)}), bf16[16,16,1152]{2,1,0:T(8,128)(2,1)S(1)}, u32[]{:S(2)}, u32[]{:S(2)}) async-start(bf16[16,16,1152]{2,1,0:T(8,128)(2,1)} %get-tuple-element.15), calls=%async_computation | async-start | bytes 1179648 | tf_op jit(solution)/shard_map/all_to_all | solution.py:531
  17.8 22.1 %copy-start = (bf16[2,8,64,256]{3,2,1,0:T(8,128)(2,1)S(1)}, bf16[2,8,64,256]{3,2,1,0:T(8,128)(2,1)}, u32[]{:S(2)}) copy-start(bf16[2,8,64,256]{3,2,1,0:T(8,128)(2,1)} %param.17) | copy-start | bytes 1572868
  17.8 22.1 %copy-start.1 = (bf16[2,8,64,64]{3,2,1,0:T(8,128)(2,1)S(1)}, bf16[2,8,64,64]{3,2,1,0:T(8,128)(2,1)}, u32[]{:S(2)}) copy-start(bf16[2,8,64,64]{3,2,1,0:T(8,128)(2,1)} %param.18) | copy-start | bytes 393220
  17.8 22.1 %copy-start.2 = (bf16[1,8,64,64]{3,2,1,0:T(8,128)(2,1)S(1)}, bf16[1,8,64,64]{3,2,1,0:T(8,128)(2,1)}, u32[]{:S(2)}) copy-start(bf16[1,8,64,64]{3,2,1,0:T(8,128)(2,1)} %param.19) | copy-start | bytes 196612
  17.8 22.0 %copy-start.3 = (bf16[1,1,64,512]{3,2,1,0:T(8,128)(2,1)S(1)}, bf16[1,1,64,512]{3,2,1,0:T(8,128)(2,1)}, u32[]{:S(2)}) copy-start(bf16[1,1,64,512]{3,2,1,0:T(8,128)(2,1)} %param.23) | copy-start | bytes 196612
  22.6 11.5 %collective-permute-start.1 = (bf16[464,512]{1,0:T(8,128)(2,1)S(1)}, bf16[464,512]{1,0:T(8,128)(2,1)S(1)}, u32[]{:S(2)}, u32[]{:S(2)}) collective-permute-start(bf16[464,512]{1,0:T(8,128)(2,1)S(1)} %packing.1.own), channel_id=1, source_target_pairs={{16,32},{32,16},{48,64},{64,48},{80,96},{96,80},{17,33},{33,17},{4... | collective-permute-start | bytes 1425416 | tf_op jit(solution)/shard_map/ppermute | solution.py:582
  27.8 6.3 %collective-permute-start = (bf16[464,512]{1,0:T(8,128)(2,1)S(1)}, bf16[464,512]{1,0:T(8,128)(2,1)S(1)}, u32[]{:S(2)}, u32[]{:S(2)}) collective-permute-start(bf16[464,512]{1,0:T(8,128)(2,1)S(1)} %packing.1.own), channel_id=1, source_target_pairs={{0,16},{16,0},{32,48},{48,32},{64,80},{80,64},{96,112},{112,96},{1... | collective-permute-start | bytes 1425416 | tf_op jit(solution)/shard_map/ppermute | solution.py:581
  28.7 11.2 %all-to-all-start.1 = ((bf16[8,16,8,128]{3,2,1,0:T(8,128)(2,1)}), bf16[8,16,8,128]{3,2,1,0:T(8,128)(2,1)S(1)}, u32[]{:S(2)}, u32[]{:S(2)}) async-start(bf16[8,16,8,128]{3,2,1,0:T(8,128)(2,1)} %tops.1), calls=%async_computation.1 | async-start | bytes 524288 | tf_op jit(solution)/shard_map/all_to_all | solution.py:583

commit v5 on v4

--- a/solution.py
+++ b/solution.py
@@ -329,22 +329,15 @@
     far_todo,
     far_choose_leaf,
     far_choose_pair,
-    far_choose_top,
-    far_emission,
-    far_reflect,
     far_couple_leaf,
     far_couple_pair,
     far_blocks,
-    parts,
+    gathered,
     fields,
-    choose_top,
     window,
     todo,
     choose_leaf,
     choose_pair,
-    gathered,
-    emission,
-    reflect,
     couple_leaf,
     couple_pair,
     blocks,
@@ -358,15 +351,14 @@
             (far_choose_pair, choose_pair),
             (far_couple_leaf, couple_leaf),
             (far_couple_pair, couple_pair),
-            (far_choose_top, choose_top),
-            (far_emission, emission),
-            (far_reflect, reflect),
         ],
         sems,
     )
     leaves = gathered.shape[0]
     section = lax.axis_index("section")
-    bands, rows, cols, leaf = emission.shape
+    bands, leaf = gathered.shape[1:]
+    cols = fields.shape[0] // bands - leaves
+    rows = leaves // cols
     around = (own.shape[0] - 16 - leaves * 4) // (leaves + cols)
     broad = cols + 2
     width_all = around * cols
@@ -409,12 +401,18 @@
             far_blocks.at[at, n], blocks.at[slot], block_sems.at[slot]
         )
 
-    def fetch(slot, _):
-        pair = todo[0, slot]
-        block_copy((pair >> 4) & 255, pair & 15, slot).start()
+    def fetch(step, _):
+        for k in range(4):
+            slot = 4 * step + k
+
+            @pl.when(slot < found)
+            def _():
+                pair = todo[0, slot]
+                block_copy((pair >> 4) & 255, pair & 15, slot).start()
+
         return 0
 
-    lax.fori_loop(0, found, fetch, 0)
+    lax.fori_loop(0, (found + 3) // 4, fetch, 0)
     tables = (own, from_mate, from_other)
     copies[1].wait()
     leaf_pick = chosen(choose_leaf, tables, 0, leaves)
@@ -425,8 +423,6 @@
     fields[:split] = own_blocks(dot(leaf_pick, couple_leaf[...], NT), leaves)
     copies[4].wait()
     fields[split:] = own_blocks(dot(pair_pick, couple_pair[...], NT), cols)
-    for copy in copies[5:]:
-        copy.wait()
     gathered[...] = local_part[...]
 
     def several(step, _):
@@ -452,13 +448,11 @@
         return 0
 
     lax.fori_loop(0, (found + AT_ONCE - 1) // AT_ONCE, several, 0)
-    for g in range(rows):
-        near_part = jnp.swapaxes(gathered[g * cols : (g + 1) * cols], 0, 1)
-        parts[0, :, g] = emission[:, g] + reflect[:, g] * near_part
-        parts[1, :, g] = reflect[:, g]
-
-
-def result_kernel(tops, parts, fields, choose_top, couple_top, basis, up_leaf, up_pair, out):
+
+
+def result_kernel(
+    tops, gathered, fields, choose_top, couple_top, basis, up_leaf, up_pair, emission, reflect, out
+):
     bands, rows, cols, leaf = out.shape
     leaves = rows * cols
     picks = couple_top.shape[1] // RANK
@@ -480,7 +474,10 @@
     leaf_total = leaf_field + own_blocks(dot(spread, up_leaf[...], NT), leaves)[:, :RANK]
     leaf_total = jnp.concatenate([leaf_total, leaf_total], axis=1)
     far_part = dot(on_diagonal(leaf_total, leaves), basis[...], NN)
-    out[...] = parts[0] + parts[1] * far_part.reshape(out.shape)
+    far_part = far_part.reshape(out.shape)
+    for g in range(rows):
+        near_part = jnp.swapaxes(gathered[g * cols : (g + 1) * cols], 0, 1)
+        out[:, g] = emission[:, g] + reflect[:, g] * (near_part + far_part[:, g])
 
 
 def body(
@@ -582,22 +579,21 @@
     from_other = lax.ppermute(packed, "section", others)
     tops = lax.all_to_all(tops, "section", 0, 0)
     most = leaves * (listed.shape[0] - 1)
-    held = [choose_leaf, choose_pair, local_part, emission, reflect, couple_leaf, couple_pair]
-    parts, fields, choose_top = pl.pallas_call(
+    held = [choose_leaf, choose_pair, couple_leaf, couple_pair]
+    gathered, fields = pl.pallas_call(
         field_kernel,
         out_shape=[
-            jax.ShapeDtypeStruct((2,) + radiosity.shape, F32),
+            jax.ShapeDtypeStruct((leaves, bands, leaf), F32),
             jax.ShapeDtypeStruct((bands * (leaves + cols), LANES), F32),
-            jax.ShapeDtypeStruct(choose_top.shape, BF16),
-        ],
-        in_specs=[VMEM] * 4 + [HBM] * 9,
-        out_specs=[VMEM] * 3,
+        ],
+        in_specs=[VMEM] * 4 + [HBM] * 6,
+        out_specs=[VMEM] * 2,
         scratch_shapes=[
             pltpu.VMEM((window[0] + 1,) + window[1:], F32),
             pltpu.SMEM(todo.shape, jnp.int32),
         ]
         + [pltpu.VMEM(x.shape, x.dtype) for x in held]
-        + [pltpu.VMEM((most, leaf, leaf), BF16), sems((9,)), sems((most,))],
+        + [pltpu.VMEM((most, leaf, leaf), BF16), sems((5,)), sems((most,))],
         compiler_params=limit(19),
         name="fields",
     )(
@@ -605,24 +601,26 @@
         from_mate,
         from_other,
         local_part,
-        *map(far, [todo] + held[:2] + [choose_top] + held[3:] + [blocks]),
+        *map(far, [todo] + held + [blocks]),
     )
     return pl.pallas_call(
         result_kernel,
         out_shape=jax.ShapeDtypeStruct(radiosity.shape, F32),
-        in_specs=[VMEM] * 8,
+        in_specs=[VMEM] * 10,
         out_specs=VMEM,
         compiler_params=limit(4),
         name="result",
     )(
         tops.reshape(tall * around * bands, LANES),
-        parts,
+        gathered,
         fields,
         choose_top,
         couple_top,
         basis,
         up_leaf,
         up_pair,
+        emission,
+        reflect,
     )
 
 

time: 42 us -> 42 us (level)
  transfers between devices with their start and end apart: 4 -> 4, of which waited for: 3 -> 3; matrix products, arithmetic and copies ran while one was open for 0% -> 0% of each run, Pallas kernels for 31% -> 30%
where the time goes in v5:
time: 42 us; the launch traced here: 41.6 us
  starting transfers between devices  18.4 us (44%)
  Pallas kernels  17.4 us (41%)
  waiting for transfers between devices  5.6 us (13%)
    all_to_all x1, starting transfers between devices, body(): ring = lax.all_to_all(sent, 'perim', 0, 0)  8.44 us
    pallas_call x1, Pallas kernels, body(): pl.pallas_call(local_kernel, out_shape=choices, in_specs=[VMEM] + [HBM] *...  6.31 us
    pallas_call x1, Pallas kernels, body(): pl.pallas_call(field_kernel, out_shape=[jax.ShapeDtypeStruct((leaves, ban...  5.56 us
    ppermute x1, starting transfers between devices, body(): from_other = lax.ppermute(packed, 'section', others)  5.21 us
    all_to_all x1, starting transfers between devices, body(): tops = lax.all_to_all(tops, 'section', 0, 0)  4.68 us
    all_to_all x1, waiting for transfers between devices, body(): ring = lax.all_to_all(sent, 'perim', 0, 0)  4.67 us
    pallas_call x1, Pallas kernels, body(): pl.pallas_call(coefficients_kernel, out_shape=[pltpu.HBM((around, 16, WID...  2.98 us
    pallas_call x1, Pallas kernels, body(): pl.pallas_call(result_kernel, out_shape=jax.ShapeDtypeStruct(radiosity.sh...  1.77 us
  transfers between devices with their start and end apart: 4, of which 3 were waited for; matrix products, arithmetic and copies ran while one was open for 0% of the time, Pallas kernels for 30%

profile of v5, /device:TPU:1, one launch (start us, length us, event | category | flops | bytes accessed | tf_op | source)
XLA Modules:
  0.0 41.6 jit_solution(8135034828281084564)
XLA Ops:
  0.0 3.0 %coefficients.1 = (bf16[16,16,1152]{2,1,0:T(8,128)(2,1)}, bf16[16,8,256]{2,1,0:T(8,128)(2,1)S(1)}) custom-call(f32[8,2,8,256]{3,2,1,0:T(8,128)} %far_radiosity.1, bf16[1024,256]{1,0:T(8,128)(2,1)} %bitcast.12, bf16[1024,64]{1,0:T(8,128)(2,1)} %bitcast.15, bf16[512,64]{1,0:T(8,128)(2,1)} %bitcast.17), custom_call_target="tpu_custom_call" | custom-call | tf_op jit(solution)/shard_map/coefficients/pallas_call | solution.py:509
  3.0 8.4 %all-to-all-start = ((bf16[16,16,1152]{2,1,0:T(8,128)(2,1)}), bf16[16,16,1152]{2,1,0:T(8,128)(2,1)S(1)}, u32[]{:S(2)}, u32[]{:S(2)}) async-start(bf16[16,16,1152]{2,1,0:T(8,128)(2,1)} %get-tuple-element.14), calls=%async_computation | async-start | bytes 1179648 | tf_op jit(solution)/shard_map/all_to_all | solution.py:528
  11.4 6.3 %local.1 = (bf16[256,768]{1,0:T(8,128)(2,1)}, bf16[128,384]{1,0:T(8,128)(2,1)}, bf16[64,1024]{1,0:T(8,128)(2,1)}, s32[1,128]{1,0:T(1,128)}, f32[16,8,256]{2,1,0:T(8,128)S(1)}) custom-call(bf16[16,8,256]{2,1,0:T(8,128)(2,1)S(1)} %get-tuple-element.15.cells, s32[6,2,8]{2,1,0:T(2,128)} %bitcast.25, s32[16,16]{1,0:T(8,128)} %bitcast.24, s32[8,16]{1,0:T(8,128)} %bitcast.26, ...), custom_call_target="tpu_custom_call" | custom-call | tf_op jit(solution)/shard_map/local/pallas_call | solution.py:546
  17.8 0.0 copy-start
  17.8 0.0 copy-start.1
  17.8 0.0 copy-start.2
  17.8 0.0 copy-start.3
  17.8 0.0 copy-start.4
  17.8 0.0 copy-start.5
  17.8 0.0 copy-start.6
  17.8 4.7 %all-to-all-done.ring = bf16[16,16,1152]{2,1,0:T(8,128)(2,1)S(1)} async-done(((bf16[16,16,1152]{2,1,0:T(8,128)(2,1)}), bf16[16,16,1152]{2,1,0:T(8,128)(2,1)S(1)}, u32[]{:S(2)}, u32[]{:S(2)}) %all-to-all-start) | async-done | bytes 589856 | tf_op jit(solution)/shard_map/all_to_all | solution.py:528
  22.5 5.2 %collective-permute-start.1 = (bf16[464,512]{1,0:T(8,128)(2,1)S(1)}, bf16[464,512]{1,0:T(8,128)(2,1)S(1)}, u32[]{:S(2)}, u32[]{:S(2)}) collective-permute-start(bf16[464,512]{1,0:T(8,128)(2,1)S(1)} %packing.1.own), channel_id=1, source_target_pairs={{16,32},{32,16},{48,64},{64,48},{80,96},{96,80},{17,33},{33,17},{4... | collective-permute-start | bytes 1425416 | tf_op jit(solution)/shard_map/ppermute | solution.py:579
  27.8 0.1 collective-permute-start
  27.9 0.8 %tops.1 = bf16[8,16,8,128]{3,2,1,0:T(8,128)(2,1)} custom-call(bf16[16,16,1152]{2,1,0:T(8,128)(2,1)S(1)} %all-to-all-done.ring), custom_call_target="tpu_custom_call" | custom-call | tf_op jit(solution)/shard_map/tops/pallas_call | solution.py:569
  28.6 4.7 %all-to-all-start.1 = ((bf16[8,16,8,128]{3,2,1,0:T(8,128)(2,1)}), bf16[8,16,8,128]{3,2,1,0:T(8,128)(2,1)S(1)}, u32[]{:S(2)}, u32[]{:S(2)}) async-start(bf16[8,16,8,128]{3,2,1,0:T(8,128)(2,1)} %tops.1), calls=%async_computation.1 | async-start | bytes 524288 | tf_op jit(solution)/shard_map/all_to_all | solution.py:580
  33.3 0.8 %collective-permute-done.1.from_other = bf16[464,512]{1,0:T(8,128)(2,1)S(1)} collective-permute-done((bf16[464,512]{1,0:T(8,128)(2,1)S(1)}, bf16[464,512]{1,0:T(8,128)(2,1)S(1)}, u32[]{:S(2)}, u32[]{:S(2)}) %collective-permute-start.1) | collective-permute-done | bytes 475168 | tf_op jit(solution)/shard_map/ppermute | solution.py:579
  34.1 0.0 collective-permute-done.from_mate
  34.1 5.6 %fields.1 = (f32[16,8,256]{2,1,0:T(8,128)S(1)}, f32[192,128]{1,0:T(8,128)S(1)}) custom-call(bf16[464,512]{1,0:T(8,128)(2,1)S(1)} %packing.1.own, bf16[464,512]{1,0:T(8,128)(2,1)S(1)} %collective-permute-done.from_mate, bf16[464,512]{1,0:T(8,128)(2,1)S(1)} %collective-permute-done.1.from_other, f32[16,8,256]{2,1,0:T(8,128)S(1)} %get-tuple-element.16.local_part, ...), custom_call_target="tpu_custom_call" | custom-call | tf_op jit(solution)/shard_map/fields/pallas_call | solution.py:583
  39.7 0.2 all-to-all-done.1
  39.8 0.0 copy-done
  39.8 0.0 copy-done.1
  39.8 0.0 copy-done.2
  39.8 0.0 copy-done.3
  39.8 0.0 copy-done.4
  39.9 0.0 copy-done.5
  39.9 0.0 copy-done.6
  39.9 1.8 %result.1 = f32[8,2,8,256]{3,2,1,0:T(8,128)} custom-call(bf16[1024,128]{1,0:T(8,128)(2,1)S(1)} %bitcast.14, f32[16,8,256]{2,1,0:T(8,128)S(1)} %get-tuple-element.20.gathered, f32[192,128]{1,0:T(8,128)S(1)} %get-tuple-element.21.fields, bf16[64,1024]{1,0:T(8,128)(2,1)S(1)} %copy-done.5, bf16[64,512]{1,0:T(8,128)(2,1)S(1)} %bitcast.19, ...), custom_call_target="tpu_custom_call" | custom-call | tf_op jit(solution)/shard_map/result/pallas_call | solution.py:606
  (1 shorter events, 0.0 us)
Async XLA Ops:
  3.0 19.5 %all-to-all-start = ((bf16[16,16,1152]{2,1,0:T(8,128)(2,1)}), bf16[16,16,1152]{2,1,0:T(8,128)(2,1)S(1)}, u32[]{:S(2)}, u32[]{:S(2)}) async-start(bf16[16,16,1152]{2,1,0:T(8,128)(2,1)} %get-tuple-element.14), calls=%async_computation | async-start | bytes 1179648 | tf_op jit(solution)/shard_map/all_to_all | solution.py:528
  17.8 22.1 %copy-start = (bf16[2,8,64,256]{3,2,1,0:T(8,128)(2,1)S(1)}, bf16[2,8,64,256]{3,2,1,0:T(8,128)(2,1)}, u32[]{:S(2)}) copy-start(bf16[2,8,64,256]{3,2,1,0:T(8,128)(2,1)} %param.17) | copy-start | bytes 1572868
  17.8 22.1 %copy-start.1 = (bf16[2,8,64,64]{3,2,1,0:T(8,128)(2,1)S(1)}, bf16[2,8,64,64]{3,2,1,0:T(8,128)(2,1)}, u32[]{:S(2)}) copy-start(bf16[2,8,64,64]{3,2,1,0:T(8,128)(2,1)} %param.18) | copy-start | bytes 393220
  17.8 22.0 %copy-start.2 = (bf16[1,8,64,64]{3,2,1,0:T(8,128)(2,1)S(1)}, bf16[1,8,64,64]{3,2,1,0:T(8,128)(2,1)}, u32[]{:S(2)}) copy-start(bf16[1,8,64,64]{3,2,1,0:T(8,128)(2,1)} %param.19) | copy-start | bytes 196612
  17.8 22.0 %copy-start.3 = (f32[8,2,8,256]{3,2,1,0:T(8,128)S(1)}, f32[8,2,8,256]{3,2,1,0:T(8,128)}, u32[]{:S(2)}) copy-start(f32[8,2,8,256]{3,2,1,0:T(8,128)} %emission.1) | copy-start | bytes 393220
  17.8 22.0 %copy-start.4 = (f32[8,2,8,256]{3,2,1,0:T(8,128)S(1)}, f32[8,2,8,256]{3,2,1,0:T(8,128)}, u32[]{:S(2)}) copy-start(f32[8,2,8,256]{3,2,1,0:T(8,128)} %reflect.1) | copy-start | bytes 393220
  17.8 22.0 %copy-start.5 = (bf16[64,1024]{1,0:T(8,128)(2,1)S(1)}, bf16[64,1024]{1,0:T(8,128)(2,1)}, u32[]{:S(2)}) copy-start(bf16[64,1024]{1,0:T(8,128)(2,1)} %get-tuple-element.22.choose_top) | copy-start | bytes 393220
  17.8 22.0 %copy-start.6 = (bf16[1,1,64,512]{3,2,1,0:T(8,128)(2,1)S(1)}, bf16[1,1,64,512]{3,2,1,0:T(8,128)(2,1)}, u32[]{:S(2)}) copy-start(bf16[1,1,64,512]{3,2,1,0:T(8,128)(2,1)} %param.23) | copy-start | bytes 196612
  22.5 11.5 %collective-permute-start.1 = (bf16[464,512]{1,0:T(8,128)(2,1)S(1)}, bf16[464,512]{1,0:T(8,128)(2,1)S(1)}, u32[]{:S(2)}, u32[]{:S(2)}) collective-permute-start(bf16[464,512]{1,0:T(8,128)(2,1)S(1)} %packing.1.own), channel_id=1, source_target_pairs={{16,32},{32,16},{48,64},{64,48},{80,96},{96,80},{17,33},{33,17},{4... | collective-permute-start | bytes 1425416 | tf_op jit(solution)/shard_map/ppermute | solution.py:579
  27.8 6.3 %collective-permute-start = (bf16[464,512]{1,0:T(8,128)(2,1)S(1)}, bf16[464,512]{1,0:T(8,128)(2,1)S(1)}, u32[]{:S(2)}, u32[]{:S(2)}) collective-permute-start(bf16[464,512]{1,0:T(8,128)(2,1)S(1)} %packing.1.own), channel_id=1, source_target_pairs={{0,16},{16,0},{32,48},{48,32},{64,80},{80,64},{96,112},{112,96},{1... | collective-permute-start | bytes 1425416 | tf_op jit(solution)/shard_map/ppermute | solution.py:578
  28.6 11.2 %all-to-all-start.1 = ((bf16[8,16,8,128]{3,2,1,0:T(8,128)(2,1)}), bf16[8,16,8,128]{3,2,1,0:T(8,128)(2,1)S(1)}, u32[]{:S(2)}, u32[]{:S(2)}) async-start(bf16[8,16,8,128]{3,2,1,0:T(8,128)(2,1)} %tops.1), calls=%async_computation.1 | async-start | bytes 524288 | tf_op jit(solution)/shard_map/all_to_all | solution.py:580

commit v6 on v5

--- a/solution.py
+++ b/solution.py
@@ -158,7 +158,8 @@
 
 
 def tops_kernel(ring, tops, row_tops, sems):
-    row_tops[...] = ring[:, :8, 1024:]
+    rows = ring[:, :, 1024:].astype(F32)[:, :8]
+    row_tops[...] = rows.reshape(row_tops.shape).astype(BF16)
     for copy in started([(row_tops, tops.at[to]) for to in range(tops.shape[0])], sems):
         copy.wait()
 
@@ -568,10 +569,10 @@
     )(ring, cells, local_part)
     tops = pl.pallas_call(
         tops_kernel,
-        out_shape=pltpu.HBM((tall, around, bands, LANES), BF16),
+        out_shape=pltpu.HBM((tall, around * bands, LANES), BF16),
         in_specs=[VMEM],
         out_specs=HBM,
-        scratch_shapes=[pltpu.VMEM((around, bands, LANES), BF16), sems((tall,))],
+        scratch_shapes=[pltpu.VMEM((around * bands, LANES), BF16), sems((tall,))],
         compiler_params=limit(3),
         name="tops",
     )(ring)

time: 42 us -> 42 us (level)
  no operation moved by 1% of the time
where the time goes in v6:
time: 42 us; the launch traced here: 41.6 us
  starting transfers between devices  18.4 us (44%)
  Pallas kernels  17.4 us (41%)
  waiting for transfers between devices  5.6 us (13%)
    all_to_all x1, starting transfers between devices, body(): ring = lax.all_to_all(sent, 'perim', 0, 0)  8.44 us
    pallas_call x1, Pallas kernels, body(): pl.pallas_call(local_kernel, out_shape=choices, in_specs=[VMEM] + [HBM] *...  6.31 us
    pallas_call x1, Pallas kernels, body(): pl.pallas_call(field_kernel, out_shape=[jax.ShapeDtypeStruct((leaves, ban...  5.57 us
    ppermute x1, starting transfers between devices, body(): from_other = lax.ppermute(packed, 'section', others)  5.21 us
    all_to_all x1, starting transfers between devices, body(): tops = lax.all_to_all(tops, 'section', 0, 0)  4.68 us
    all_to_all x1, waiting for transfers between devices, body(): ring = lax.all_to_all(sent, 'perim', 0, 0)  4.67 us
    pallas_call x1, Pallas kernels, body(): pl.pallas_call(coefficients_kernel, out_shape=[pltpu.HBM((around, 16, WID...  2.98 us
    pallas_call x1, Pallas kernels, body(): pl.pallas_call(result_kernel, out_shape=jax.ShapeDtypeStruct(radiosity.sh...  1.77 us
  transfers between devices with their start and end apart: 4, of which 3 were waited for; matrix products, arithmetic and copies ran while one was open for 0% of the time, Pallas kernels for 30%

profile of v6, /device:TPU:1, one launch (start us, length us, event | category | flops | bytes accessed | tf_op | source)
XLA Modules:
  0.0 41.6 jit_solution(3796548033026031875)
XLA Ops:
  0.0 3.0 %coefficients.1 = (bf16[16,16,1152]{2,1,0:T(8,128)(2,1)}, bf16[16,8,256]{2,1,0:T(8,128)(2,1)S(1)}) custom-call(f32[8,2,8,256]{3,2,1,0:T(8,128)} %far_radiosity.1, bf16[1024,256]{1,0:T(8,128)(2,1)} %bitcast.12, bf16[1024,64]{1,0:T(8,128)(2,1)} %bitcast.15, bf16[512,64]{1,0:T(8,128)(2,1)} %bitcast.17), custom_call_target="tpu_custom_call" | custom-call | tf_op jit(solution)/shard_map/coefficients/pallas_call | solution.py:510
  3.0 8.4 %all-to-all-start = ((bf16[16,16,1152]{2,1,0:T(8,128)(2,1)}), bf16[16,16,1152]{2,1,0:T(8,128)(2,1)S(1)}, u32[]{:S(2)}, u32[]{:S(2)}) async-start(bf16[16,16,1152]{2,1,0:T(8,128)(2,1)} %get-tuple-element.14), calls=%async_computation | async-start | bytes 1179648 | tf_op jit(solution)/shard_map/all_to_all | solution.py:529
  11.4 6.3 %local.1 = (bf16[256,768]{1,0:T(8,128)(2,1)}, bf16[128,384]{1,0:T(8,128)(2,1)}, bf16[64,1024]{1,0:T(8,128)(2,1)}, s32[1,128]{1,0:T(1,128)}, f32[16,8,256]{2,1,0:T(8,128)S(1)}) custom-call(bf16[16,8,256]{2,1,0:T(8,128)(2,1)S(1)} %get-tuple-element.15.cells, s32[6,2,8]{2,1,0:T(2,128)} %bitcast.25, s32[16,16]{1,0:T(8,128)} %bitcast.24, s32[8,16]{1,0:T(8,128)} %bitcast.26, ...), custom_call_target="tpu_custom_call" | custom-call | tf_op jit(solution)/shard_map/local/pallas_call | solution.py:547
  17.8 0.0 copy-start
  17.8 0.0 copy-start.1
  17.8 0.0 copy-start.2
  17.8 0.0 copy-start.3
  17.8 0.0 copy-start.4
  17.8 0.0 copy-start.5
  17.8 0.0 copy-start.6
  17.8 4.7 %all-to-all-done.ring = bf16[16,16,1152]{2,1,0:T(8,128)(2,1)S(1)} async-done(((bf16[16,16,1152]{2,1,0:T(8,128)(2,1)}), bf16[16,16,1152]{2,1,0:T(8,128)(2,1)S(1)}, u32[]{:S(2)}, u32[]{:S(2)}) %all-to-all-start) | async-done | bytes 589856 | tf_op jit(solution)/shard_map/all_to_all | solution.py:529
  22.5 5.2 %collective-permute-start.1 = (bf16[464,512]{1,0:T(8,128)(2,1)S(1)}, bf16[464,512]{1,0:T(8,128)(2,1)S(1)}, u32[]{:S(2)}, u32[]{:S(2)}) collective-permute-start(bf16[464,512]{1,0:T(8,128)(2,1)S(1)} %packing.1.own), channel_id=1, source_target_pairs={{16,32},{32,16},{48,64},{64,48},{80,96},{96,80},{17,33},{33,17},{4... | collective-permute-start | bytes 1425416 | tf_op jit(solution)/shard_map/ppermute | solution.py:580
  27.8 0.1 collective-permute-start
  27.9 0.8 %tops.1 = bf16[8,128,128]{2,1,0:T(8,128)(2,1)} custom-call(bf16[16,16,1152]{2,1,0:T(8,128)(2,1)S(1)} %all-to-all-done.ring), custom_call_target="tpu_custom_call" | custom-call | tf_op jit(solution)/shard_map/tops/pallas_call | solution.py:570
  28.6 4.7 %all-to-all-start.1 = ((bf16[8,128,128]{2,1,0:T(8,128)(2,1)}), bf16[8,128,128]{2,1,0:T(8,128)(2,1)S(1)}, u32[]{:S(2)}, u32[]{:S(2)}) async-start(bf16[8,128,128]{2,1,0:T(8,128)(2,1)} %tops.1), calls=%async_computation.1 | async-start | bytes 524288 | tf_op jit(solution)/shard_map/all_to_all | solution.py:581
  33.3 0.8 %collective-permute-done.1.from_other = bf16[464,512]{1,0:T(8,128)(2,1)S(1)} collective-permute-done((bf16[464,512]{1,0:T(8,128)(2,1)S(1)}, bf16[464,512]{1,0:T(8,128)(2,1)S(1)}, u32[]{:S(2)}, u32[]{:S(2)}) %collective-permute-start.1) | collective-permute-done | bytes 475168 | tf_op jit(solution)/shard_map/ppermute | solution.py:580
  34.1 0.0 collective-permute-done.from_mate
  34.1 5.6 %fields.1 = (f32[16,8,256]{2,1,0:T(8,128)S(1)}, f32[192,128]{1,0:T(8,128)S(1)}) custom-call(bf16[464,512]{1,0:T(8,128)(2,1)S(1)} %packing.1.own, bf16[464,512]{1,0:T(8,128)(2,1)S(1)} %collective-permute-done.from_mate, bf16[464,512]{1,0:T(8,128)(2,1)S(1)} %collective-permute-done.1.from_other, f32[16,8,256]{2,1,0:T(8,128)S(1)} %get-tuple-element.16.local_part, ...), custom_call_target="tpu_custom_call" | custom-call | tf_op jit(solution)/shard_map/fields/pallas_call | solution.py:584
  39.7 0.2 all-to-all-done.1
  39.8 0.0 copy-done
  39.8 0.0 copy-done.1
  39.8 0.0 copy-done.2
  39.8 0.0 copy-done.3
  39.8 0.0 copy-done.4
  39.9 0.0 copy-done.5
  39.9 0.0 copy-done.6
  39.9 1.8 %result.1 = f32[8,2,8,256]{3,2,1,0:T(8,128)} custom-call(bf16[1024,128]{1,0:T(8,128)(2,1)S(1)} %bitcast.14, f32[16,8,256]{2,1,0:T(8,128)S(1)} %get-tuple-element.20.gathered, f32[192,128]{1,0:T(8,128)S(1)} %get-tuple-element.21.fields, bf16[64,1024]{1,0:T(8,128)(2,1)S(1)} %copy-done.5, bf16[64,512]{1,0:T(8,128)(2,1)S(1)} %bitcast.19, ...), custom_call_target="tpu_custom_call" | custom-call | tf_op jit(solution)/shard_map/result/pallas_call | solution.py:607
  (1 shorter events, 0.0 us)
Async XLA Ops:
  3.0 19.5 %all-to-all-start = ((bf16[16,16,1152]{2,1,0:T(8,128)(2,1)}), bf16[16,16,1152]{2,1,0:T(8,128)(2,1)S(1)}, u32[]{:S(2)}, u32[]{:S(2)}) async-start(bf16[16,16,1152]{2,1,0:T(8,128)(2,1)} %get-tuple-element.14), calls=%async_computation | async-start | bytes 1179648 | tf_op jit(solution)/shard_map/all_to_all | solution.py:529
  17.8 22.1 %copy-start = (bf16[2,8,64,256]{3,2,1,0:T(8,128)(2,1)S(1)}, bf16[2,8,64,256]{3,2,1,0:T(8,128)(2,1)}, u32[]{:S(2)}) copy-start(bf16[2,8,64,256]{3,2,1,0:T(8,128)(2,1)} %param.17) | copy-start | bytes 1572868
  17.8 22.1 %copy-start.1 = (bf16[2,8,64,64]{3,2,1,0:T(8,128)(2,1)S(1)}, bf16[2,8,64,64]{3,2,1,0:T(8,128)(2,1)}, u32[]{:S(2)}) copy-start(bf16[2,8,64,64]{3,2,1,0:T(8,128)(2,1)} %param.18) | copy-start | bytes 393220
  17.8 22.1 %copy-start.2 = (bf16[1,8,64,64]{3,2,1,0:T(8,128)(2,1)S(1)}, bf16[1,8,64,64]{3,2,1,0:T(8,128)(2,1)}, u32[]{:S(2)}) copy-start(bf16[1,8,64,64]{3,2,1,0:T(8,128)(2,1)} %param.19) | copy-start | bytes 196612
  17.8 22.0 %copy-start.3 = (f32[8,2,8,256]{3,2,1,0:T(8,128)S(1)}, f32[8,2,8,256]{3,2,1,0:T(8,128)}, u32[]{:S(2)}) copy-start(f32[8,2,8,256]{3,2,1,0:T(8,128)} %emission.1) | copy-start | bytes 393220
  17.8 22.0 %copy-start.4 = (f32[8,2,8,256]{3,2,1,0:T(8,128)S(1)}, f32[8,2,8,256]{3,2,1,0:T(8,128)}, u32[]{:S(2)}) copy-start(f32[8,2,8,256]{3,2,1,0:T(8,128)} %reflect.1) | copy-start | bytes 393220
  17.8 22.0 %copy-start.5 = (bf16[64,1024]{1,0:T(8,128)(2,1)S(1)}, bf16[64,1024]{1,0:T(8,128)(2,1)}, u32[]{:S(2)}) copy-start(bf16[64,1024]{1,0:T(8,128)(2,1)} %get-tuple-element.22.choose_top) | copy-start | bytes 393220
  17.8 22.0 %copy-start.6 = (bf16[1,1,64,512]{3,2,1,0:T(8,128)(2,1)S(1)}, bf16[1,1,64,512]{3,2,1,0:T(8,128)(2,1)}, u32[]{:S(2)}) copy-start(bf16[1,1,64,512]{3,2,1,0:T(8,128)(2,1)} %param.23) | copy-start | bytes 196612
  22.5 11.5 %collective-permute-start.1 = (bf16[464,512]{1,0:T(8,128)(2,1)S(1)}, bf16[464,512]{1,0:T(8,128)(2,1)S(1)}, u32[]{:S(2)}, u32[]{:S(2)}) collective-permute-start(bf16[464,512]{1,0:T(8,128)(2,1)S(1)} %packing.1.own), channel_id=1, source_target_pairs={{16,32},{32,16},{48,64},{64,48},{80,96},{96,80},{17,33},{33,17},{4... | collective-permute-start | bytes 1425416 | tf_op jit(solution)/shard_map/ppermute | solution.py:580
  27.8 6.3 %collective-permute-start = (bf16[464,512]{1,0:T(8,128)(2,1)S(1)}, bf16[464,512]{1,0:T(8,128)(2,1)S(1)}, u32[]{:S(2)}, u32[]{:S(2)}) collective-permute-start(bf16[464,512]{1,0:T(8,128)(2,1)S(1)} %packing.1.own), channel_id=1, source_target_pairs={{0,16},{16,0},{32,48},{48,32},{64,80},{80,64},{96,112},{112,96},{1... | collective-permute-start | bytes 1425416 | tf_op jit(solution)/shard_map/ppermute | solution.py:579
  28.6 11.2 %all-to-all-start.1 = ((bf16[8,128,128]{2,1,0:T(8,128)(2,1)}), bf16[8,128,128]{2,1,0:T(8,128)(2,1)S(1)}, u32[]{:S(2)}, u32[]{:S(2)}) async-start(bf16[8,128,128]{2,1,0:T(8,128)(2,1)} %tops.1), calls=%async_computation.1 | async-start | bytes 524288 | tf_op jit(solution)/shard_map/all_to_all | solution.py:581

commit v7 on v6

--- a/solution.py
+++ b/solution.py
@@ -159,6 +159,9 @@
 
 def tops_kernel(ring, tops, row_tops, sems):
     rows = ring[:, :, 1024:].astype(F32)[:, :8]
+    half = rows.shape[0] // 2
+    low = lax.broadcasted_iota(jnp.int32, rows[:half].shape, 2) < RANK
+    rows = jnp.where(low, rows[:half], rows[half:])
     row_tops[...] = rows.reshape(row_tops.shape).astype(BF16)
     for copy in started([(row_tops, tops.at[to]) for to in range(tops.shape[0])], sems):
         copy.wait()
@@ -259,6 +262,10 @@
     names = jnp.broadcast_to(names_top[...], square)
     diagonal = lax.broadcasted_iota(jnp.int32, square, 0) == lax.broadcasted_iota(jnp.int32, square, 1)
     names = jnp.sum(jnp.where(diagonal, names, 0), axis=1, keepdims=True)
+    around = width_all // cols
+    row, source = split_name(names, around)
+    upper, source = split_name(source, around // 2)
+    names = upper * (choose_top.shape[1] // bands // 2) + row * (around // 2) + source
     at = lax.broadcasted_iota(jnp.int32, (picks, choose_top.shape[1]), 1)
     choose_top[...] = jnp.concatenate(
         [(at == names * bands + b).astype(F32) for b in range(bands)], axis=0
@@ -459,7 +466,11 @@
     picks = couple_top.shape[1] // RANK
     leaf_field = fields[: bands * leaves, :RANK]
     pair_field = fields[bands * leaves :, :RANK]
-    top_pick = dot(choose_top[...], tops[...], NN)
+    size = tops.shape[0]
+    top_pick = dot(choose_top[:, :size], tops[...], NN)
+    upper = dot(choose_top[:, size:], tops[...], NN)
+    top_pick = jnp.where(lax.broadcasted_iota(jnp.int32, upper.shape, 1) < RANK, top_pick, upper)
+    top_pick = top_pick + pltpu.roll(top_pick, RANK, 1)
     top_pick = jnp.concatenate([top_pick] * (picks // 2), axis=1)
     kept = row_of(top_pick.shape, picks) == lax.broadcasted_iota(jnp.int32, top_pick.shape, 1) // RANK
     top_pick = jnp.where(kept, top_pick, 0.0).astype(BF16)
@@ -569,10 +580,10 @@
     )(ring, cells, local_part)
     tops = pl.pallas_call(
         tops_kernel,
-        out_shape=pltpu.HBM((tall, around * bands, LANES), BF16),
+        out_shape=pltpu.HBM((tall, around * bands // 2, LANES), BF16),
         in_specs=[VMEM],
         out_specs=HBM,
-        scratch_shapes=[pltpu.VMEM((around * bands, LANES), BF16), sems((tall,))],
+        scratch_shapes=[pltpu.VMEM((around * bands // 2, LANES), BF16), sems((tall,))],
         compiler_params=limit(3),
         name="tops",
     )(ring)
@@ -612,7 +623,7 @@
         compiler_params=limit(4),
         name="result",
     )(
-        tops.reshape(tall * around * bands, LANES),
+        tops.reshape(tall * around * bands // 2, LANES),
         gathered,
         fields,
         choose_top,

time: 42 us -> 41.9 us (level)
  transfers between devices with their start and end apart: 4 -> 4, of which waited for: 3 -> 2; matrix products, arithmetic and copies ran while one was open for 0% -> 0% of each run, Pallas kernels for 30% -> 30%
where the time goes in v7:
time: 41.9 us; the launch traced here: 41.6 us
  starting transfers between devices  18.4 us (44%)
  Pallas kernels  17.4 us (42%)
  waiting for transfers between devices  5.5 us (13%)
    all_to_all x1, starting transfers between devices, body(): ring = lax.all_to_all(sent, 'perim', 0, 0)  8.44 us
    pallas_call x1, Pallas kernels, body(): pl.pallas_call(local_kernel, out_shape=choices, in_specs=[VMEM] + [HBM] *...  6.31 us
    pallas_call x1, Pallas kernels, body(): pl.pallas_call(field_kernel, out_shape=[jax.ShapeDtypeStruct((leaves, ban...  5.56 us
    ppermute x1, starting transfers between devices, body(): from_other = lax.ppermute(packed, 'section', others)  5.21 us
    all_to_all x1, starting transfers between devices, body(): tops = lax.all_to_all(tops, 'section', 0, 0)  4.68 us
    all_to_all x1, waiting for transfers between devices, body(): ring = lax.all_to_all(sent, 'perim', 0, 0)  4.67 us
    pallas_call x1, Pallas kernels, body(): pl.pallas_call(coefficients_kernel, out_shape=[pltpu.HBM((around, 16, WID...  2.98 us
    pallas_call x1, Pallas kernels, body(): pl.pallas_call(result_kernel, out_shape=jax.ShapeDtypeStruct(radiosity.sh...  1.83 us
  transfers between devices with their start and end apart: 4, of which 2 were waited for; matrix products, arithmetic and copies ran while one was open for 0% of the time, Pallas kernels for 30%

profile of v7, /device:TPU:1, one launch (start us, length us, event | category | flops | bytes accessed | tf_op | source)
XLA Modules:
  0.0 41.6 jit_solution(11085980207631794603)
XLA Ops:
  0.0 3.0 %coefficients.1 = (bf16[16,16,1152]{2,1,0:T(8,128)(2,1)}, bf16[16,8,256]{2,1,0:T(8,128)(2,1)S(1)}) custom-call(f32[8,2,8,256]{3,2,1,0:T(8,128)} %far_radiosity.1, bf16[1024,256]{1,0:T(8,128)(2,1)} %bitcast.12, bf16[1024,64]{1,0:T(8,128)(2,1)} %bitcast.14, bf16[512,64]{1,0:T(8,128)(2,1)} %bitcast.17), custom_call_target="tpu_custom_call" | custom-call | tf_op jit(solution)/shard_map/coefficients/pallas_call | solution.py:521
  3.0 8.4 %all-to-all-start = ((bf16[16,16,1152]{2,1,0:T(8,128)(2,1)}), bf16[16,16,1152]{2,1,0:T(8,128)(2,1)S(1)}, u32[]{:S(2)}, u32[]{:S(2)}) async-start(bf16[16,16,1152]{2,1,0:T(8,128)(2,1)} %get-tuple-element.14), calls=%async_computation | async-start | bytes 1179648 | tf_op jit(solution)/shard_map/all_to_all | solution.py:540
  11.4 6.3 %local.1 = (bf16[256,768]{1,0:T(8,128)(2,1)}, bf16[128,384]{1,0:T(8,128)(2,1)}, bf16[64,1024]{1,0:T(8,128)(2,1)}, s32[1,128]{1,0:T(1,128)}, f32[16,8,256]{2,1,0:T(8,128)S(1)}) custom-call(bf16[16,8,256]{2,1,0:T(8,128)(2,1)S(1)} %get-tuple-element.15.cells, s32[6,2,8]{2,1,0:T(2,128)} %bitcast.25, s32[16,16]{1,0:T(8,128)} %bitcast.24, s32[8,16]{1,0:T(8,128)} %bitcast.26, ...), custom_call_target="tpu_custom_call" | custom-call | tf_op jit(solution)/shard_map/local/pallas_call | solution.py:558
  17.8 0.0 copy-start
  17.8 0.0 copy-start.1
  17.8 0.0 copy-start.2
  17.8 0.0 copy-start.3
  17.8 0.0 copy-start.4
  17.8 0.0 copy-start.5
  17.8 0.0 copy-start.6
  17.8 4.7 %all-to-all-done.ring = bf16[16,16,1152]{2,1,0:T(8,128)(2,1)S(1)} async-done(((bf16[16,16,1152]{2,1,0:T(8,128)(2,1)}), bf16[16,16,1152]{2,1,0:T(8,128)(2,1)S(1)}, u32[]{:S(2)}, u32[]{:S(2)}) %all-to-all-start) | async-done | bytes 589856 | tf_op jit(solution)/shard_map/all_to_all | solution.py:540
  22.5 5.2 %collective-permute-start.1 = (bf16[464,512]{1,0:T(8,128)(2,1)S(1)}, bf16[464,512]{1,0:T(8,128)(2,1)S(1)}, u32[]{:S(2)}, u32[]{:S(2)}) collective-permute-start(bf16[464,512]{1,0:T(8,128)(2,1)S(1)} %packing.1.own), channel_id=1, source_target_pairs={{16,32},{32,16},{48,64},{64,48},{80,96},{96,80},{17,33},{33,17},{4... | collective-permute-start | bytes 1425416 | tf_op jit(solution)/shard_map/ppermute | solution.py:591
  27.8 0.1 collective-permute-start
  27.9 0.7 %tops.1 = bf16[8,64,128]{2,1,0:T(8,128)(2,1)} custom-call(bf16[16,16,1152]{2,1,0:T(8,128)(2,1)S(1)} %all-to-all-done.ring), custom_call_target="tpu_custom_call" | custom-call | tf_op jit(solution)/shard_map/tops/pallas_call | solution.py:581
  28.6 4.7 %all-to-all-start.1 = ((bf16[8,64,128]{2,1,0:T(8,128)(2,1)}), bf16[8,64,128]{2,1,0:T(8,128)(2,1)S(1)}, u32[]{:S(2)}, u32[]{:S(2)}) async-start(bf16[8,64,128]{2,1,0:T(8,128)(2,1)} %tops.1), calls=%async_computation.1 | async-start | bytes 262144 | tf_op jit(solution)/shard_map/all_to_all | solution.py:592
  33.3 0.8 %collective-permute-done.1.from_other = bf16[464,512]{1,0:T(8,128)(2,1)S(1)} collective-permute-done((bf16[464,512]{1,0:T(8,128)(2,1)S(1)}, bf16[464,512]{1,0:T(8,128)(2,1)S(1)}, u32[]{:S(2)}, u32[]{:S(2)}) %collective-permute-start.1) | collective-permute-done | bytes 475168 | tf_op jit(solution)/shard_map/ppermute | solution.py:591
  34.1 0.0 collective-permute-done.from_mate
  34.1 5.6 %fields.1 = (f32[16,8,256]{2,1,0:T(8,128)S(1)}, f32[192,128]{1,0:T(8,128)S(1)}) custom-call(bf16[464,512]{1,0:T(8,128)(2,1)S(1)} %packing.1.own, bf16[464,512]{1,0:T(8,128)(2,1)S(1)} %collective-permute-done.from_mate, bf16[464,512]{1,0:T(8,128)(2,1)S(1)} %collective-permute-done.1.from_other, f32[16,8,256]{2,1,0:T(8,128)S(1)} %get-tuple-element.16.local_part, ...), custom_call_target="tpu_custom_call" | custom-call | tf_op jit(solution)/shard_map/fields/pallas_call | solution.py:595
  39.7 0.0 all-to-all-done.1
  39.7 0.0 copy-done
  39.7 0.0 copy-done.1
  39.7 0.0 copy-done.2
  39.7 0.0 copy-done.3
  39.7 0.0 copy-done.4
  39.7 0.0 copy-done.5
  39.7 0.0 copy-done.6
  39.7 1.8 %result.1 = f32[8,2,8,256]{3,2,1,0:T(8,128)} custom-call(bf16[512,128]{1,0:T(8,128)(2,1)S(1)} %bitcast.16, f32[16,8,256]{2,1,0:T(8,128)S(1)} %get-tuple-element.20.gathered, f32[192,128]{1,0:T(8,128)S(1)} %get-tuple-element.21.fields, bf16[64,1024]{1,0:T(8,128)(2,1)S(1)} %copy-done.5, bf16[64,512]{1,0:T(8,128)(2,1)S(1)} %bitcast.19, ...), custom_call_target="tpu_custom_call" | custom-call | tf_op jit(solution)/shard_map/result/pallas_call | solution.py:618
  (1 shorter events, 0.0 us)
Async XLA Ops:
  3.0 19.5 %all-to-all-start = ((bf16[16,16,1152]{2,1,0:T(8,128)(2,1)}), bf16[16,16,1152]{2,1,0:T(8,128)(2,1)S(1)}, u32[]{:S(2)}, u32[]{:S(2)}) async-start(bf16[16,16,1152]{2,1,0:T(8,128)(2,1)} %get-tuple-element.14), calls=%async_computation | async-start | bytes 1179648 | tf_op jit(solution)/shard_map/all_to_all | solution.py:540
  17.8 21.9 %copy-start = (bf16[2,8,64,256]{3,2,1,0:T(8,128)(2,1)S(1)}, bf16[2,8,64,256]{3,2,1,0:T(8,128)(2,1)}, u32[]{:S(2)}) copy-start(bf16[2,8,64,256]{3,2,1,0:T(8,128)(2,1)} %param.17) | copy-start | bytes 1572868
  17.8 21.9 %copy-start.1 = (bf16[2,8,64,64]{3,2,1,0:T(8,128)(2,1)S(1)}, bf16[2,8,64,64]{3,2,1,0:T(8,128)(2,1)}, u32[]{:S(2)}) copy-start(bf16[2,8,64,64]{3,2,1,0:T(8,128)(2,1)} %param.18) | copy-start | bytes 393220
  17.8 21.9 %copy-start.2 = (bf16[1,8,64,64]{3,2,1,0:T(8,128)(2,1)S(1)}, bf16[1,8,64,64]{3,2,1,0:T(8,128)(2,1)}, u32[]{:S(2)}) copy-start(bf16[1,8,64,64]{3,2,1,0:T(8,128)(2,1)} %param.19) | copy-start | bytes 196612
  17.8 21.9 %copy-start.3 = (f32[8,2,8,256]{3,2,1,0:T(8,128)S(1)}, f32[8,2,8,256]{3,2,1,0:T(8,128)}, u32[]{:S(2)}) copy-start(f32[8,2,8,256]{3,2,1,0:T(8,128)} %emission.1) | copy-start | bytes 393220
  17.8 21.9 %copy-start.4 = (f32[8,2,8,256]{3,2,1,0:T(8,128)S(1)}, f32[8,2,8,256]{3,2,1,0:T(8,128)}, u32[]{:S(2)}) copy-start(f32[8,2,8,256]{3,2,1,0:T(8,128)} %reflect.1) | copy-start | bytes 393220
  17.8 21.9 %copy-start.5 = (bf16[64,1024]{1,0:T(8,128)(2,1)S(1)}, bf16[64,1024]{1,0:T(8,128)(2,1)}, u32[]{:S(2)}) copy-start(bf16[64,1024]{1,0:T(8,128)(2,1)} %get-tuple-element.22.choose_top) | copy-start | bytes 393220
  17.8 21.9 %copy-start.6 = (bf16[1,1,64,512]{3,2,1,0:T(8,128)(2,1)S(1)}, bf16[1,1,64,512]{3,2,1,0:T(8,128)(2,1)}, u32[]{:S(2)}) copy-start(bf16[1,1,64,512]{3,2,1,0:T(8,128)(2,1)} %param.23) | copy-start | bytes 196612
  22.5 11.5 %collective-permute-start.1 = (bf16[464,512]{1,0:T(8,128)(2,1)S(1)}, bf16[464,512]{1,0:T(8,128)(2,1)S(1)}, u32[]{:S(2)}, u32[]{:S(2)}) collective-permute-start(bf16[464,512]{1,0:T(8,128)(2,1)S(1)} %packing.1.own), channel_id=1, source_target_pairs={{16,32},{32,16},{48,64},{64,48},{80,96},{96,80},{17,33},{33,17},{4... | collective-permute-start | bytes 1425416 | tf_op jit(solution)/shard_map/ppermute | solution.py:591
  27.8 6.3 %collective-permute-start = (bf16[464,512]{1,0:T(8,128)(2,1)S(1)}, bf16[464,512]{1,0:T(8,128)(2,1)S(1)}, u32[]{:S(2)}, u32[]{:S(2)}) collective-permute-start(bf16[464,512]{1,0:T(8,128)(2,1)S(1)} %packing.1.own), channel_id=1, source_target_pairs={{0,16},{16,0},{32,48},{48,32},{64,80},{80,64},{96,112},{112,96},{1... | collective-permute-start | bytes 1425416 | tf_op jit(solution)/shard_map/ppermute | solution.py:590
  28.6 11.1 %all-to-all-start.1 = ((bf16[8,64,128]{2,1,0:T(8,128)(2,1)}), bf16[8,64,128]{2,1,0:T(8,128)(2,1)S(1)}, u32[]{:S(2)}, u32[]{:S(2)}) async-start(bf16[8,64,128]{2,1,0:T(8,128)(2,1)} %tops.1), calls=%async_computation.1 | async-start | bytes 262144 | tf_op jit(solution)/shard_map/all_to_all | solution.py:592

commit v8 on v7

--- a/solution.py
+++ b/solution.py
@@ -15,7 +15,7 @@
 VMEM = pl.BlockSpec(memory_space=pltpu.VMEM)
 HBM = pl.BlockSpec(memory_space=pltpu.HBM)
 ANY = pl.BlockSpec(memory_space=pl.ANY)
-AT_ONCE = 16
+AT_ONCE = 20
 
 
 def dot(left, right, dims):

time: 41.9 us -> 41.5 us (level)
  no operation moved by 1% of the time
where the time goes in v8:
time: 41.5 us; the launch traced here: 41.2 us
  starting transfers between devices  18.4 us (44%)
  Pallas kernels  17.1 us (41%)
  waiting for transfers between devices  5.5 us (13%)
    all_to_all x1, starting transfers between devices, body(): ring = lax.all_to_all(sent, 'perim', 0, 0)  8.44 us
    pallas_call x1, Pallas kernels, body(): pl.pallas_call(local_kernel, out_shape=choices, in_specs=[VMEM] + [HBM] *...  6.31 us
    ppermute x1, starting transfers between devices, body(): from_other = lax.ppermute(packed, 'section', others)  5.21 us
    pallas_call x1, Pallas kernels, body(): pl.pallas_call(field_kernel, out_shape=[jax.ShapeDtypeStruct((leaves, ban...  5.18 us
    all_to_all x1, starting transfers between devices, body(): tops = lax.all_to_all(tops, 'section', 0, 0)  4.68 us
    all_to_all x1, waiting for transfers between devices, body(): ring = lax.all_to_all(sent, 'perim', 0, 0)  4.67 us
    pallas_call x1, Pallas kernels, body(): pl.pallas_call(coefficients_kernel, out_shape=[pltpu.HBM((around, 16, WID...  2.98 us
    pallas_call x1, Pallas kernels, body(): pl.pallas_call(result_kernel, out_shape=jax.ShapeDtypeStruct(radiosity.sh...  1.83 us
  transfers between devices with their start and end apart: 4, of which 2 were waited for; matrix products, arithmetic and copies ran while one was open for 0% of the time, Pallas kernels for 30%

profile of v8, /device:TPU:1, one launch (start us, length us, event | category | flops | bytes accessed | tf_op | source)
XLA Modules:
  0.0 41.2 jit_solution(9114838515064728425)
XLA Ops:
  0.0 3.0 %coefficients.1 = (bf16[16,16,1152]{2,1,0:T(8,128)(2,1)}, bf16[16,8,256]{2,1,0:T(8,128)(2,1)S(1)}) custom-call(f32[8,2,8,256]{3,2,1,0:T(8,128)} %far_radiosity.1, bf16[1024,256]{1,0:T(8,128)(2,1)} %bitcast.12, bf16[1024,64]{1,0:T(8,128)(2,1)} %bitcast.14, bf16[512,64]{1,0:T(8,128)(2,1)} %bitcast.17), custom_call_target="tpu_custom_call" | custom-call | tf_op jit(solution)/shard_map/coefficients/pallas_call | solution.py:521
  3.0 8.4 %all-to-all-start = ((bf16[16,16,1152]{2,1,0:T(8,128)(2,1)}), bf16[16,16,1152]{2,1,0:T(8,128)(2,1)S(1)}, u32[]{:S(2)}, u32[]{:S(2)}) async-start(bf16[16,16,1152]{2,1,0:T(8,128)(2,1)} %get-tuple-element.14), calls=%async_computation | async-start | bytes 1179648 | tf_op jit(solution)/shard_map/all_to_all | solution.py:540
  11.4 6.3 %local.1 = (bf16[256,768]{1,0:T(8,128)(2,1)}, bf16[128,384]{1,0:T(8,128)(2,1)}, bf16[64,1024]{1,0:T(8,128)(2,1)}, s32[1,128]{1,0:T(1,128)}, f32[16,8,256]{2,1,0:T(8,128)S(1)}) custom-call(bf16[16,8,256]{2,1,0:T(8,128)(2,1)S(1)} %get-tuple-element.15.cells, s32[6,2,8]{2,1,0:T(2,128)} %bitcast.25, s32[16,16]{1,0:T(8,128)} %bitcast.24, s32[8,16]{1,0:T(8,128)} %bitcast.26, ...), custom_call_target="tpu_custom_call" | custom-call | tf_op jit(solution)/shard_map/local/pallas_call | solution.py:558
  17.8 0.0 copy-start
  17.8 0.0 copy-start.1
  17.8 0.0 copy-start.2
  17.8 0.0 copy-start.3
  17.8 0.0 copy-start.4
  17.8 0.0 copy-start.5
  17.8 0.0 copy-start.6
  17.8 4.7 %all-to-all-done.ring = bf16[16,16,1152]{2,1,0:T(8,128)(2,1)S(1)} async-done(((bf16[16,16,1152]{2,1,0:T(8,128)(2,1)}), bf16[16,16,1152]{2,1,0:T(8,128)(2,1)S(1)}, u32[]{:S(2)}, u32[]{:S(2)}) %all-to-all-start) | async-done | bytes 589856 | tf_op jit(solution)/shard_map/all_to_all | solution.py:540
  22.5 5.2 %collective-permute-start.1 = (bf16[464,512]{1,0:T(8,128)(2,1)S(1)}, bf16[464,512]{1,0:T(8,128)(2,1)S(1)}, u32[]{:S(2)}, u32[]{:S(2)}) collective-permute-start(bf16[464,512]{1,0:T(8,128)(2,1)S(1)} %packing.1.own), channel_id=1, source_target_pairs={{16,32},{32,16},{48,64},{64,48},{80,96},{96,80},{17,33},{33,17},{4... | collective-permute-start | bytes 1425416 | tf_op jit(solution)/shard_map/ppermute | solution.py:591
  27.8 0.1 collective-permute-start
  27.9 0.7 %tops.1 = bf16[8,64,128]{2,1,0:T(8,128)(2,1)} custom-call(bf16[16,16,1152]{2,1,0:T(8,128)(2,1)S(1)} %all-to-all-done.ring), custom_call_target="tpu_custom_call" | custom-call | tf_op jit(solution)/shard_map/tops/pallas_call | solution.py:581
  28.6 4.7 %all-to-all-start.1 = ((bf16[8,64,128]{2,1,0:T(8,128)(2,1)}), bf16[8,64,128]{2,1,0:T(8,128)(2,1)S(1)}, u32[]{:S(2)}, u32[]{:S(2)}) async-start(bf16[8,64,128]{2,1,0:T(8,128)(2,1)} %tops.1), calls=%async_computation.1 | async-start | bytes 262144 | tf_op jit(solution)/shard_map/all_to_all | solution.py:592
  33.3 0.8 %collective-permute-done.1.from_other = bf16[464,512]{1,0:T(8,128)(2,1)S(1)} collective-permute-done((bf16[464,512]{1,0:T(8,128)(2,1)S(1)}, bf16[464,512]{1,0:T(8,128)(2,1)S(1)}, u32[]{:S(2)}, u32[]{:S(2)}) %collective-permute-start.1) | collective-permute-done | bytes 475168 | tf_op jit(solution)/shard_map/ppermute | solution.py:591
  34.1 0.0 collective-permute-done.from_mate
  34.1 5.2 %fields.1 = (f32[16,8,256]{2,1,0:T(8,128)S(1)}, f32[192,128]{1,0:T(8,128)S(1)}) custom-call(bf16[464,512]{1,0:T(8,128)(2,1)S(1)} %packing.1.own, bf16[464,512]{1,0:T(8,128)(2,1)S(1)} %collective-permute-done.from_mate, bf16[464,512]{1,0:T(8,128)(2,1)S(1)} %collective-permute-done.1.from_other, f32[16,8,256]{2,1,0:T(8,128)S(1)} %get-tuple-element.16.local_part, ...), custom_call_target="tpu_custom_call" | custom-call | tf_op jit(solution)/shard_map/fields/pallas_call | solution.py:595
  39.3 0.0 all-to-all-done.1
  39.3 0.0 copy-done
  39.3 0.0 copy-done.1
  39.3 0.0 copy-done.2
  39.3 0.0 copy-done.3
  39.3 0.0 copy-done.4
  39.3 0.0 copy-done.5
  39.3 0.0 copy-done.6
  39.4 1.8 %result.1 = f32[8,2,8,256]{3,2,1,0:T(8,128)} custom-call(bf16[512,128]{1,0:T(8,128)(2,1)S(1)} %bitcast.16, f32[16,8,256]{2,1,0:T(8,128)S(1)} %get-tuple-element.20.gathered, f32[192,128]{1,0:T(8,128)S(1)} %get-tuple-element.21.fields, bf16[64,1024]{1,0:T(8,128)(2,1)S(1)} %copy-done.5, bf16[64,512]{1,0:T(8,128)(2,1)S(1)} %bitcast.19, ...), custom_call_target="tpu_custom_call" | custom-call | tf_op jit(solution)/shard_map/result/pallas_call | solution.py:618
  (1 shorter events, 0.0 us)
Async XLA Ops:
  3.0 19.5 %all-to-all-start = ((bf16[16,16,1152]{2,1,0:T(8,128)(2,1)}), bf16[16,16,1152]{2,1,0:T(8,128)(2,1)S(1)}, u32[]{:S(2)}, u32[]{:S(2)}) async-start(bf16[16,16,1152]{2,1,0:T(8,128)(2,1)} %get-tuple-element.14), calls=%async_computation | async-start | bytes 1179648 | tf_op jit(solution)/shard_map/all_to_all | solution.py:540
  17.8 21.5 %copy-start = (bf16[2,8,64,256]{3,2,1,0:T(8,128)(2,1)S(1)}, bf16[2,8,64,256]{3,2,1,0:T(8,128)(2,1)}, u32[]{:S(2)}) copy-start(bf16[2,8,64,256]{3,2,1,0:T(8,128)(2,1)} %param.17) | copy-start | bytes 1572868
  17.8 21.5 %copy-start.1 = (bf16[2,8,64,64]{3,2,1,0:T(8,128)(2,1)S(1)}, bf16[2,8,64,64]{3,2,1,0:T(8,128)(2,1)}, u32[]{:S(2)}) copy-start(bf16[2,8,64,64]{3,2,1,0:T(8,128)(2,1)} %param.18) | copy-start | bytes 393220
  17.8 21.5 %copy-start.2 = (bf16[1,8,64,64]{3,2,1,0:T(8,128)(2,1)S(1)}, bf16[1,8,64,64]{3,2,1,0:T(8,128)(2,1)}, u32[]{:S(2)}) copy-start(bf16[1,8,64,64]{3,2,1,0:T(8,128)(2,1)} %param.19) | copy-start | bytes 196612
  17.8 21.5 %copy-start.3 = (f32[8,2,8,256]{3,2,1,0:T(8,128)S(1)}, f32[8,2,8,256]{3,2,1,0:T(8,128)}, u32[]{:S(2)}) copy-start(f32[8,2,8,256]{3,2,1,0:T(8,128)} %emission.1) | copy-start | bytes 393220
  17.8 21.5 %copy-start.4 = (f32[8,2,8,256]{3,2,1,0:T(8,128)S(1)}, f32[8,2,8,256]{3,2,1,0:T(8,128)}, u32[]{:S(2)}) copy-start(f32[8,2,8,256]{3,2,1,0:T(8,128)} %reflect.1) | copy-start | bytes 393220
  17.8 21.5 %copy-start.5 = (bf16[64,1024]{1,0:T(8,128)(2,1)S(1)}, bf16[64,1024]{1,0:T(8,128)(2,1)}, u32[]{:S(2)}) copy-start(bf16[64,1024]{1,0:T(8,128)(2,1)} %get-tuple-element.22.choose_top) | copy-start | bytes 393220
  17.8 21.5 %copy-start.6 = (bf16[1,1,64,512]{3,2,1,0:T(8,128)(2,1)S(1)}, bf16[1,1,64,512]{3,2,1,0:T(8,128)(2,1)}, u32[]{:S(2)}) copy-start(bf16[1,1,64,512]{3,2,1,0:T(8,128)(2,1)} %param.23) | copy-start | bytes 196612
  22.5 11.5 %collective-permute-start.1 = (bf16[464,512]{1,0:T(8,128)(2,1)S(1)}, bf16[464,512]{1,0:T(8,128)(2,1)S(1)}, u32[]{:S(2)}, u32[]{:S(2)}) collective-permute-start(bf16[464,512]{1,0:T(8,128)(2,1)S(1)} %packing.1.own), channel_id=1, source_target_pairs={{16,32},{32,16},{48,64},{64,48},{80,96},{96,80},{17,33},{33,17},{4... | collective-permute-start | bytes 1425416 | tf_op jit(solution)/shard_map/ppermute | solution.py:591
  27.8 6.3 %collective-permute-start = (bf16[464,512]{1,0:T(8,128)(2,1)S(1)}, bf16[464,512]{1,0:T(8,128)(2,1)S(1)}, u32[]{:S(2)}, u32[]{:S(2)}) collective-permute-start(bf16[464,512]{1,0:T(8,128)(2,1)S(1)} %packing.1.own), channel_id=1, source_target_pairs={{0,16},{16,0},{32,48},{48,32},{64,80},{80,64},{96,112},{112,96},{1... | collective-permute-start | bytes 1425416 | tf_op jit(solution)/shard_map/ppermute | solution.py:590
  28.6 10.7 %all-to-all-start.1 = ((bf16[8,64,128]{2,1,0:T(8,128)(2,1)}), bf16[8,64,128]{2,1,0:T(8,128)(2,1)S(1)}, u32[]{:S(2)}, u32[]{:S(2)}) async-start(bf16[8,64,128]{2,1,0:T(8,128)(2,1)} %tops.1), calls=%async_computation.1 | async-start | bytes 262144 | tf_op jit(solution)/shard_map/all_to_all | solution.py:592
